TPU v7x, 256 devices: a whole 4x4x8 slice. The times are simulated.
256 devices in a mesh: dp: 256 (over x, z, y, core).
Axes of the slice: x: 4, y: 4, z: 8, core: 2. Of those that a mesh axis runs over, the one named last changes fastest.
Arguments:
- image_emb: bfloat16 [131072, 1152], P('dp'), may hold values from -0.75 to 0.75
- text_emb: bfloat16 [131072, 1152], P('dp'), may hold values from -0.75 to 0.75
- log_scale: float32 [1], replicated, may hold values from 1 to 2.3
- logit_bias: float32 [1], replicated, may hold values from -4 to -1
Outputs:
- image_grad: float32 [131072, 1152], P('dp')
- text_grad: float32 [2, 512, 1152], P(None, 'dp')
- row_loss: float32 [131072], P('dp')
All inputs are finite; a program needn't handle non-finite values.
Results may differ from a plain program's by a relative error of at most 0.0019.
Values may be sent and summed in bfloat16 or wider, within the bound.
No kernel may reach another device: no remote copies, remote signals or barrier semaphores. Data moves between devices by JAX's collectives and lax.ppermute only.
A program may use at most 64 MiB of HBM per device.

v0:
```python
import jax
import jax.numpy as jnp
from jax import lax
from jax.sharding import PartitionSpec as P

STEPS = 2


def broadcast(shard, axis, root):
    mine = lax.axis_index(axis) == root
    return lax.psum(jnp.where(mine, shard, jnp.zeros_like(shard)), axis)


def local(image_emb, text_emb, log_scale, logit_bias):
    scale = jnp.exp(log_scale[0])
    bias = logit_bias[0]
    rows = image_emb.shape[0]
    devices = lax.axis_size("dp")
    mine = lax.axis_index("dp")
    eye = jnp.eye(rows, dtype=jnp.float32)
    image_grad = jnp.zeros(image_emb.shape, jnp.float32)
    row_loss = jnp.zeros((rows,), jnp.float32)
    pieces = []
    for step in range(STEPS):
        owner = step * (devices // STEPS)
        block = broadcast(text_emb, "dp", owner)
        logits = scale * jnp.dot(image_emb, block.T, preferred_element_type=jnp.float32) + bias
        positive = eye * (mine == owner).astype(jnp.float32)
        sign = 2.0 * positive - 1.0
        row_loss = row_loss + jnp.sum(jax.nn.softplus(-sign * logits), axis=1)
        weights = (jax.nn.sigmoid(logits) - positive).astype(jnp.bfloat16)
        image_grad = image_grad + scale * jnp.dot(
            weights, block, preferred_element_type=jnp.float32
        )
        text_term = scale * lax.dot_general(
            weights, image_emb, (((0,), (0,)), ((), ())), preferred_element_type=jnp.float32
        )
        pieces.append(lax.psum_scatter(text_term, "dp", scatter_dimension=0, tiled=True))
    text_grad = jnp.stack(pieces)
    return (image_grad, text_grad, row_loss)


def solution(mesh):
    in_specs = (P("dp", None), P("dp", None), P(), P())
    out_specs = (P("dp", None), P(None, "dp", None), P("dp"))
    return jax.shard_map(local, mesh=mesh, in_specs=in_specs, out_specs=out_specs, check_vma=False)
```

profile of v0, /device:TPU:32, one launch (start us, length us, event | category | flops | bytes accessed | tf_op | source)
XLA Modules:
  0.0 565.2 jit_solution(8551081654936366495)
XLA Ops:
  7.2 0.0 copy-start
  7.2 0.0 all-reduce.9.cloned.1.call-start
  7.2 3.0 broadcast_select_fusion
  10.2 0.0 all-reduce.9.cloned.1.call-update
  10.2 0.0 all-reduce.7.cloned.1.call-start
  11.6 265.1 %all-reduce.9.cloned.1.call-done = (bf16[512,1152]{1,0:T(8,128)(2,1)}, bf16[512,1152]{1,0:T(8,128)(2,1)}) async-done(((bf16[512,1152]{1,0:T(8,128)(2,1)}, bf16[512,1152]{1,0:T(8,128)(2,1)}), (bf16[512,1152]{1,0:T(8,128)(2,1)}, bf16[512,1152]{1,0:T(8,128)(2,1)})) %all-reduce.9.cloned.1.call-update) | async-done | bytes 2359312 | tf_op jit(solution)/shard_map/psum | solution.py:11
  276.7 0.0 copy-done
  276.7 2.7 fusion.14
  279.5 0.0 copy-start.2
  279.5 2.4 convolution_multiply_fusion
  281.9 0.0 copy-done.2
  281.9 1.5 fusion.13
  283.3 0.0 copy-start.3
  283.3 1.0 copy-done.3
  284.3 2.4 convolution_multiply_fusion.1
  286.8 0.0 all-reduce.7.cloned.1.call-update
  286.8 0.6 add.55
  287.4 0.0 copy-start.1
  287.4 2.2 fusion.18
  289.6 0.0 copy-done.1
  289.6 2.3 fusion
  292.0 265.0 %all-reduce.7.cloned.1.call-done = (f32[512,1152]{1,0:T(8,128)}, f32[512,1152]{1,0:T(8,128)}) async-done(((f32[512,1152]{1,0:T(8,128)}, f32[512,1152]{1,0:T(8,128)}), (f32[512,1152]{1,0:T(8,128)}, f32[512,1152]{1,0:T(8,128)})) %all-reduce.7.cloned.1.call-update) | async-done | bytes 4718608
  557.0 0.8 dynamic-slice_bitcast_fusion
  557.8 0.6 pad_maximum_fusion
Async XLA Ops:
  7.2 269.6 %copy-start = (bf16[512,1152]{1,0:T(8,128)(2,1)S(1)}, bf16[512,1152]{1,0:T(8,128)(2,1)}, u32[]{:S(2)}) copy-start(bf16[512,1152]{1,0:T(8,128)(2,1)} %param.4) | copy-start | bytes 3538948
  7.2 269.5 %all-reduce.9.cloned.1.call-start = ((), (), s32[]{:S(2)}) async-start(), calls=%async_computation.1 | async-start | bytes 4718592 | tf_op jit(solution)/shard_map/psum | solution.py:11
  10.2 546.7 %all-reduce.7.cloned.1.call-start = ((), (), s32[]{:S(2)}) async-start(), calls=%async_computation | async-start | bytes 9437184
  279.5 2.4 copy-start.2
  283.3 1.0 copy-start.3
  287.4 2.2 copy-start.1
Sparse Core Ops, SparseCore 0:
  14.2 262.4 all-reduce.8
  286.9 270.0 all-reduce.6
where the time goes:
time: 568 us; the launch traced here: 565 us
  waiting for transfers between devices  530 us (93%)
  between operations  15.4 us (3%)
  matrix products  13.6 us (2%)
    psum x1, waiting for transfers between devices, broadcast(): return lax.psum(jnp.where(mine, shard, jnp.zeros_like(shard)), axis)  265 us
    unnamed x3, waiting for transfers between devices  265 us
  transfers between devices with their start and end apart: 2, of which 2 were waited for; matrix products, arithmetic and copies ran while one was open for 1% of the time, Pallas kernels for 0%

commit v1 on v0

v1 whole, which is shorter than its diff:
```python
import jax
import jax.numpy as jnp
from jax import lax
from jax.sharding import Mesh, PartitionSpec as P

STEPS = 2
NX, NZ, NY, NC = 4, 8, 4, 2
AXES = ("x", "z", "y", "c")
PLANE = NX * NZ


def device(x, z, y, c):
    return ((x * NZ + z) * NY + y) * NC + c


def local(image, text, log_scale, logit_bias):
    f32, bf16 = jnp.float32, jnp.bfloat16
    scale = jnp.exp(log_scale[0])
    bias = logit_bias[0]
    rows, width = image.shape
    ix, iz, iy, ic = (lax.axis_index(a) for a in AXES)
    per = rows // (PLANE * NY * NC)
    line = PLANE * per

    images = lax.all_gather(image, ("y", "c"), tiled=True)

    k = jnp.arange(rows)
    c_, y_, p_, r_ = k // (rows // NC), k // line % NY, k // per % PLANE, k % per
    source = ((p_ * NY + y_) * NC + c_) * per + r_
    pick = (source[:, None] == k[None, :]).astype(bf16)
    ordered = jnp.dot(pick, text, preferred_element_type=f32).astype(bf16)
    ordered = ordered.reshape(NC, NY, line, width)

    half = jnp.where(ic == 0, ordered[0], lax.ppermute(ordered[1], "c", [(0, 1)]))
    parts = half[0]
    got = []
    for y in (2, 1, 3):
        pairs = [
            (device(x, 0, 0, c), device(x, 0, y, c))
            for x in range(0, NX, NX // STEPS)
            for c in range(NC)
        ]
        got.append(lax.ppermute(half[y], AXES, pairs))
    parts = jnp.where(iy == 0, parts, got[0] + got[1] + got[2])
    spread = lax.all_to_all(parts, ("x", "z"), 0, 0, tiled=True)
    spread = spread.reshape(PLANE, per, width)
    mine = jnp.stack([spread[s * (PLANE // STEPS)] for s in range(STEPS)])
    everywhere = jnp.broadcast_to(mine[None], (PLANE, STEPS, per, width))
    texts = lax.all_to_all(
        everywhere.reshape(PLANE * STEPS * per, width), ("x", "z"), 0, 0, tiled=True
    )
    count = texts.shape[0]

    t = jnp.arange(count)
    step = t // per % STEPS
    column = ((t // (STEPS * per) * NY + iy) * NC + ic) * per + t % per
    owner = (ix == step * (NX // STEPS)) & (iz == 0)
    b = jnp.arange(images.shape[0])
    positive = ((b[:, None] == column[None, :]) & owner[None, :]).astype(f32)
    logits = scale * jnp.dot(images, texts.T, preferred_element_type=f32) + bias
    weights = (jax.nn.sigmoid(logits) - positive).astype(bf16)
    term = lax.dot_general(
        weights, images, (((0,), (0,)), ((), ())), preferred_element_type=f32
    ).astype(bf16)
    terms = lax.all_to_all(term, ("x", "z"), 0, 0, tiled=True)
    terms = terms.reshape(PLANE, STEPS * per, width).astype(f32)
    text_grad = scale * jnp.sum(terms, axis=0).reshape(STEPS, per, width)

    slots = [texts]
    for n in range(1, NY):
        slots.append(lax.ppermute(texts, "y", [(i, (i + n) % NY) for i in range(NY)]))
    core = jnp.concatenate(slots)
    block = jnp.concatenate([core, lax.ppermute(core, "c", [(0, 1), (1, 0)])])
    t = jnp.arange(block.shape[0])
    c_ = (t // (NY * count) + ic) % NC
    y_ = (iy - t // count % NY) % NY
    step = t // per % STEPS
    column = ((t // (STEPS * per) % PLANE * NY + y_) * NC + c_) * per + t % per
    owner = (ix == step * (NX // STEPS)) & (iz == 0) & (iy == 0) & (ic == 0)
    b = jnp.arange(rows)
    positive = ((b[:, None] == column[None, :]) & owner[None, :]).astype(f32)
    logits = scale * jnp.dot(image, block.T, preferred_element_type=f32) + bias
    sign = 2.0 * positive - 1.0
    row_loss = jnp.sum(jax.nn.softplus(-sign * logits), axis=1)
    weights = (jax.nn.sigmoid(logits) - positive).astype(bf16)
    image_grad = scale * jnp.dot(weights, block, preferred_element_type=f32)
    return image_grad, text_grad, row_loss


def solution(mesh):
    mesh = Mesh(mesh.devices.reshape(NX, NZ, NY, NC), AXES)
    in_specs = (P(AXES, None), P(AXES, None), P(), P())
    out_specs = (P(AXES, None), P(None, AXES, None), P(AXES))
    return jax.shard_map(local, mesh=mesh, in_specs=in_specs, out_specs=out_specs, check_vma=False)
```

time: 568 us -> 130 us (0.23)
  waiting for transfers between devices: 530 us -> 30.7 us
  blocking collectives: 0 us -> 38.4 us
  starting transfers between devices: 0.08 us -> 17.5 us
  matrix products: 13.6 us -> 22.4 us
    psum x1 -> x0, waiting for transfers between devices: 265 us -> none  [broadcast(): return lax.psum(jnp.where(mine, shard, jnp.zeros_like(shard)), axis)]
    unnamed x3 -> x1, waiting for transfers between devices: 265 us -> 0.68 us
    all_to_all x0 -> x2, blocking collectives: none -> 38.4 us  [the longest x1 22.6 us: local(): spread = lax.all_to_all(parts, ('x', 'z'), 0, 0, tiled=True)]
    ppermute x0 -> x8, waiting for transfers between devices: none -> 22.4 us  [the longest x3 19.5 us: local(): lax.ppermute(texts, 'y', [(i, (i + n) % NY) for i in range(NY)])]
    ppermute x0 -> x8, starting transfers between devices: none -> 9.36 us  [the longest x3 5.48 us: local(): lax.ppermute(texts, 'y', [(i, (i + n) % NY) for i in range(NY)])]
    dot_general x6 -> x4, matrix products: 13.6 us -> 22.4 us  [the longest x1 11.1 us: local(): lax.dot_general(weights, images, (((0,), (0,)), ((), ())), preferred_elem...]
    all_to_all x0 -> x1, starting transfers between devices: none -> 8.11 us  [local(): terms = lax.all_to_all(term, ('x', 'z'), 0, 0, tiled=True)]
    all_to_all x0 -> x1, waiting for transfers between devices: none -> 7.7 us  [local(): terms = lax.all_to_all(term, ('x', 'z'), 0, 0, tiled=True)]
  transfers between devices with their start and end apart: 2 -> 10, of which waited for: 2 -> 6; matrix products, arithmetic and copies ran while one was open for 1% -> 9% of each run, Pallas kernels for 0% -> 0%
where the time goes in v1:
time: 130 us; the launch traced here: 129 us
  blocking collectives  38.4 us (30%)
  waiting for transfers between devices  30.7 us (24%)
  matrix products  22.4 us (17%)
  starting transfers between devices  17.5 us (13%)
  between operations  15.6 us (12%)
  local copies, waits for them, and re-layouts  3.99 us (3%)
    all_to_all x1, blocking collectives, local(): spread = lax.all_to_all(parts, ('x', 'z'), 0, 0, tiled=True)  22.6 us
    ppermute x3, waiting for transfers between devices, local(): lax.ppermute(texts, 'y', [(i, (i + n) % NY) for i in range(NY)])  19.5 us
    all_to_all x1, blocking collectives, local(): lax.all_to_all(everywhere.reshape(PLANE * STEPS * per, width), ('x', 'z')...  15.7 us
    dot_general x1, matrix products, local(): lax.dot_general(weights, images, (((0,), (0,)), ((), ())), preferred_elem...  11.1 us
    all_to_all x1, starting transfers between devices, local(): terms = lax.all_to_all(term, ('x', 'z'), 0, 0, tiled=True)  8.11 us
    all_to_all x1, waiting for transfers between devices, local(): terms = lax.all_to_all(term, ('x', 'z'), 0, 0, tiled=True)  7.7 us
    dot_general x1, matrix products, local(): image_grad = scale * jnp.dot(weights, block, preferred_element_type=f32)  5.54 us
    ppermute x3, starting transfers between devices, local(): lax.ppermute(texts, 'y', [(i, (i + n) % NY) for i in range(NY)])  5.48 us
  transfers between devices with their start and end apart: 10, of which 6 were waited for; matrix products, arithmetic and copies ran while one was open for 9% of the time, Pallas kernels for 0%

profile of v1, /device:TPU:32, one launch (start us, length us, event | category | flops | bytes accessed | tf_op | source)
XLA Modules:
  0.0 129.0 jit_solution(5357637139280032302)
XLA Ops:
  7.2 0.7 all-gather.2.cloned.1.call-update
  8.4 0.9 convolution_convert_fusion
  9.4 1.8 %collective-permute-start = (bf16[4,64,1152]{2,1,0:T(8,128)(2,1)S(1)}, bf16[4,64,1152]{2,1,0:T(8,128)(2,1)S(1)}, u32[]{:S(2)}, u32[]{:S(2)}) collective-permute-start(bf16[4,64,1152]{2,1,0:T(8,128)(2,1)S(1)} %bitcast.49), channel_id=1, source_target_pairs={{0,1},{2,3},{4,5},{6,7},{8,9},{10,11},{12,13},{14,15},{16,17},{18,... | collective-permute-start | bytes 1769480 | tf_op jit(solution)/shard_map/ppermute | solution.py:34
  11.2 1.6 %collective-permute-done = bf16[4,64,1152]{2,1,0:T(8,128)(2,1)S(1)} collective-permute-done((bf16[4,64,1152]{2,1,0:T(8,128)(2,1)S(1)}, bf16[4,64,1152]{2,1,0:T(8,128)(2,1)S(1)}, u32[]{:S(2)}, u32[]{:S(2)}) %collective-permute-start) | collective-permute-done | bytes 589856 | tf_op jit(solution)/shard_map/ppermute | solution.py:34
  12.9 0.7 collective-permute-start.2
  13.6 0.7 collective-permute-start.3
  14.3 0.7 collective-permute-start.1
  15.1 22.6 %all_to_all.27 = bf16[32,2,1152]{2,1,0:T(2,128)(2,1)S(1)} all-to-all(bf16[32,2,1152]{2,1,0:T(2,128)(2,1)S(1)} %all_to_all.18), channel_id=1, replica_groups=mesh['x'=4,'z'=8,'y'=4,'c'=2] {'x','z'}, dimensions={0} | all-to-all | bytes 294912 | tf_op jit(solution)/shard_map/all_to_all | solution.py:45
  37.9 15.7 %all_to_all.28 = bf16[32,4,1152]{2,1,0:T(4,128)(2,1)S(1)} all-to-all(bf16[32,4,1152]{2,1,0:T(4,128)(2,1)S(1)} %broadcast_in_dim.5), channel_id=1, replica_groups=mesh['x'=4,'z'=8,'y'=4,'c'=2] {'x','z'}, dimensions={0} | all-to-all | bytes 589824 | tf_op jit(solution)/shard_map/all_to_all | solution.py:49
  53.7 2.5 %collective-permute-start.6 = (bf16[128,1152]{1,0:T(8,128)(2,1)S(1)}, bf16[128,1152]{1,0:T(8,128)(2,1)S(1)}, u32[]{:S(2)}, u32[]{:S(2)}) collective-permute-start(bf16[128,1152]{1,0:T(8,128)(2,1)S(1)} %all_to_all.21), channel_id=1, source_target_pairs={{0,6},{2,0},{4,2},{6,4},{1,7},{3,1},{5,3},{7,5},{8,14},{10,8},{12,... | collective-permute-start | bytes 884744 | tf_op jit(solution)/shard_map/ppermute | solution.py:71
  56.2 1.7 %collective-permute-start.5 = (bf16[128,1152]{1,0:T(8,128)(2,1)S(1)}, bf16[128,1152]{1,0:T(8,128)(2,1)S(1)}, u32[]{:S(2)}, u32[]{:S(2)}) collective-permute-start(bf16[128,1152]{1,0:T(8,128)(2,1)S(1)} %all_to_all.21), channel_id=1, source_target_pairs={{0,4},{2,6},{4,0},{6,2},{1,5},{3,7},{5,1},{7,3},{8,12},{10,14},{12... | collective-permute-start | bytes 884744 | tf_op jit(solution)/shard_map/ppermute | solution.py:71
  57.9 1.3 %collective-permute-start.4 = (bf16[128,1152]{1,0:T(8,128)(2,1)S(1)}, bf16[128,1152]{1,0:T(8,128)(2,1)S(1)}, u32[]{:S(2)}, u32[]{:S(2)}) collective-permute-start(bf16[128,1152]{1,0:T(8,128)(2,1)S(1)} %all_to_all.21), channel_id=1, source_target_pairs={{0,2},{2,4},{4,6},{6,0},{1,3},{3,5},{5,7},{7,1},{8,10},{10,12},{12... | collective-permute-start | bytes 884744 | tf_op jit(solution)/shard_map/ppermute | solution.py:71
  59.2 10.7 %collective-permute-done.6 = bf16[128,1152]{1,0:T(8,128)(2,1)S(1)} collective-permute-done((bf16[128,1152]{1,0:T(8,128)(2,1)S(1)}, bf16[128,1152]{1,0:T(8,128)(2,1)S(1)}, u32[]{:S(2)}, u32[]{:S(2)}) %collective-permute-start.6) | collective-permute-done | bytes 294944 | tf_op jit(solution)/shard_map/ppermute | solution.py:71
  69.9 3.9 %collective-permute-done.5 = bf16[128,1152]{1,0:T(8,128)(2,1)S(1)} collective-permute-done((bf16[128,1152]{1,0:T(8,128)(2,1)S(1)}, bf16[128,1152]{1,0:T(8,128)(2,1)S(1)}, u32[]{:S(2)}, u32[]{:S(2)}) %collective-permute-start.5) | collective-permute-done | bytes 294944 | tf_op jit(solution)/shard_map/ppermute | solution.py:71
  73.8 4.8 %collective-permute-done.4 = bf16[128,1152]{1,0:T(8,128)(2,1)S(1)} collective-permute-done((bf16[128,1152]{1,0:T(8,128)(2,1)S(1)}, bf16[128,1152]{1,0:T(8,128)(2,1)S(1)}, u32[]{:S(2)}, u32[]{:S(2)}) %collective-permute-start.4) | collective-permute-done | bytes 294944 | tf_op jit(solution)/shard_map/ppermute | solution.py:71
  80.4 1.3 collective-permute-done.7
  81.9 1.4 %copy-done.2 = bf16[1024,1152]{1,0:T(8,128)(2,1)} copy-done((bf16[1024,1152]{1,0:T(8,128)(2,1)}, bf16[1024,1152]{1,0:T(8,128)(2,1)S(1)}, u32[]{:S(2)}) %copy-start.2) | copy-done | bytes 2359320
  83.3 4.9 %fusion.8 = (f32[512]{0:T(512)}, f32[1024,512]{1,0:T(8,128)}) fusion(s32[1024]{0:T(1024)S(1)} %fusion.34, f32[]{:T(128)} %bitcast.47, f32[]{:T(128)} %bitcast, pred[1024]{0:T(1024)(128)(4,1)S(1)} %and_and_fusion, bf16[1024,1152]{1,0:T(8,128)(2,1)S(1)} %constant_dynamic-update-slice_fusion, bf16[512,1152]{1,0:T(8,128)(2,1)S(1)} %copy-done.1), kind=kOutput, calls=%fused_computation.13 | convolution fusion | flops 1215823360 | bytes 5643272 | tf_op jit(solution)/shard_map/dot_general | solution.py:82
  88.2 11.1 %convolution_convert_fusion.1 = bf16[128,1152]{1,0:T(8,128)(2,1)S(1)} fusion(bf16[4096,1152]{1,0:T(8,128)(2,1)} %all-gather.2.cloned.1.call-done, bf16[128,1152]{1,0:T(8,128)(2,1)S(1)} %all_to_all.21, s32[128]{0:T(128)S(1)} %fusion.69, f32[]{:T(128)} %bitcast.46, f32[]{:T(128)} %bitcast, pred[128]{0:T(512)(128)(4,1)S(1)} %compare_and_fusion), kind=kOutput, calls=%fused_computation.12 | convolution fusion | flops 2421309440 | bytes 10027656 | tf_op jit(solution)/shard_map/dot_general | solution.py:62
  99.2 0.8 all_to_all.22
  100.0 8.1 %all-to-all-start.2 = ((bf16[32,4,1152]{2,1,0:T(4,128)(2,1)}), bf16[32,4,1152]{2,1,0:T(4,128)(2,1)S(1)}, u32[]{:S(2)}, u32[]{:S(2)}) async-start(bf16[32,4,1152]{2,1,0:T(4,128)(2,1)} %all_to_all.22), calls=%async_computation.2 | async-start | bytes 589824 | tf_op jit(solution)/shard_map/all_to_all | solution.py:65
  108.1 5.5 %convolution_multiply_fusion.1 = f32[512,1152]{1,0:T(8,128)} fusion(bf16[1024,1152]{1,0:T(8,128)(2,1)} %copy-done.2, f32[]{:T(128)} %bitcast, f32[1024,512]{1,0:T(8,128)} %get-tuple-element.11, s32[1024]{0:T(1024)S(1)} %fusion.34, f32[]{:T(128)} %bitcast.45, pred[1024]{0:T(1024)(128)(4,1)S(1)} %and_and_fusion), kind=kOutput, calls=%fused_computation.10 | convolution fusion | flops 1213792256 | bytes 6820872 | tf_op jit(solution)/shard_map/dot_general | solution.py:86
  113.7 7.7 %all-to-all-done.2 = bf16[32,4,1152]{2,1,0:T(4,128)(2,1)S(1)} async-done(((bf16[32,4,1152]{2,1,0:T(4,128)(2,1)}), bf16[32,4,1152]{2,1,0:T(4,128)(2,1)S(1)}, u32[]{:S(2)}, u32[]{:S(2)}) %all-to-all-start.2) | async-done | bytes 294944 | tf_op jit(solution)/shard_map/all_to_all | solution.py:65
  121.5 0.6 mul.140
  (34 shorter events, 1.8 us)
Async XLA Ops:
  7.2 1.3 copy-start
  7.2 81.0 %all-gather.2.cloned.1.call-start = ((), (), s32[]{:S(2)}) async-start(), calls=%async_computation.3 | async-start | bytes 10616832 | tf_op jit(solution)/shard_map/all_gather | solution.py:25
  9.4 3.4 %collective-permute-start = (bf16[4,64,1152]{2,1,0:T(8,128)(2,1)S(1)}, bf16[4,64,1152]{2,1,0:T(8,128)(2,1)S(1)}, u32[]{:S(2)}, u32[]{:S(2)}) collective-permute-start(bf16[4,64,1152]{2,1,0:T(8,128)(2,1)S(1)} %bitcast.49), channel_id=1, source_target_pairs={{0,1},{2,3},{4,5},{6,7},{8,9},{10,11},{12,13},{14,15},{16,17},{18,... | collective-permute-start | bytes 1769480 | tf_op jit(solution)/shard_map/ppermute | solution.py:34
  12.9 2.0 %collective-permute-start.2 = (bf16[64,1152]{1,0:T(8,128)(2,1)S(1)}, bf16[64,1152]{1,0:T(8,128)(2,1)S(1)}, u32[]{:S(2)}, u32[]{:S(2)}) collective-permute-start(bf16[64,1152]{1,0:T(8,128)(2,1)S(1)} %get-tuple-element.5), channel_id=1, source_target_pairs={{0,2},{1,3},{128,130},{129,131}} | collective-permute-start | bytes 442376 | tf_op jit(solution)/shard_map/ppermute | solution.py:43
  13.6 1.4 %collective-permute-start.3 = (bf16[64,1152]{1,0:T(8,128)(2,1)S(1)}, bf16[64,1152]{1,0:T(8,128)(2,1)S(1)}, u32[]{:S(2)}, u32[]{:S(2)}) collective-permute-start(bf16[64,1152]{1,0:T(8,128)(2,1)S(1)} %get-tuple-element.6), channel_id=1, source_target_pairs={{0,6},{1,7},{128,134},{129,135}} | collective-permute-start | bytes 442376 | tf_op jit(solution)/shard_map/ppermute | solution.py:43
  14.3 0.7 collective-permute-start.1
  53.7 16.2 %collective-permute-start.6 = (bf16[128,1152]{1,0:T(8,128)(2,1)S(1)}, bf16[128,1152]{1,0:T(8,128)(2,1)S(1)}, u32[]{:S(2)}, u32[]{:S(2)}) collective-permute-start(bf16[128,1152]{1,0:T(8,128)(2,1)S(1)} %all_to_all.21), channel_id=1, source_target_pairs={{0,6},{2,0},{4,2},{6,4},{1,7},{3,1},{5,3},{7,5},{8,14},{10,8},{12,... | collective-permute-start | bytes 884744 | tf_op jit(solution)/shard_map/ppermute | solution.py:71
  56.2 17.7 %collective-permute-start.5 = (bf16[128,1152]{1,0:T(8,128)(2,1)S(1)}, bf16[128,1152]{1,0:T(8,128)(2,1)S(1)}, u32[]{:S(2)}, u32[]{:S(2)}) collective-permute-start(bf16[128,1152]{1,0:T(8,128)(2,1)S(1)} %all_to_all.21), channel_id=1, source_target_pairs={{0,4},{2,6},{4,0},{6,2},{1,5},{3,7},{5,1},{7,3},{8,12},{10,14},{12... | collective-permute-start | bytes 884744 | tf_op jit(solution)/shard_map/ppermute | solution.py:71
  57.9 20.8 %collective-permute-start.4 = (bf16[128,1152]{1,0:T(8,128)(2,1)S(1)}, bf16[128,1152]{1,0:T(8,128)(2,1)S(1)}, u32[]{:S(2)}, u32[]{:S(2)}) collective-permute-start(bf16[128,1152]{1,0:T(8,128)(2,1)S(1)} %all_to_all.21), channel_id=1, source_target_pairs={{0,2},{2,4},{4,6},{6,0},{1,3},{3,5},{5,7},{7,1},{8,10},{10,12},{12... | collective-permute-start | bytes 884744 | tf_op jit(solution)/shard_map/ppermute | solution.py:71
  78.8 2.9 %collective-permute-start.7 = (bf16[512,1152]{1,0:T(8,128)(2,1)S(1)}, bf16[512,1152]{1,0:T(8,128)(2,1)S(1)}, u32[]{:S(2)}, u32[]{:S(2)}) collective-permute-start(bf16[512,1152]{1,0:T(8,128)(2,1)S(1)} %pad_maximum_fusion), channel_id=1, source_target_pairs={{0,1},{1,0},{2,3},{3,2},{4,5},{5,4},{6,7},{7,6},{8,9},{9,8},{10,11... | collective-permute-start | bytes 3538952 | tf_op jit(solution)/shard_map/ppermute | solution.py:73
  80.3 3.0 %copy-start.1 = (bf16[512,1152]{1,0:T(8,128)(2,1)S(1)}, bf16[512,1152]{1,0:T(8,128)(2,1)}, u32[]{:S(2)}) copy-start(bf16[512,1152]{1,0:T(8,128)(2,1)} %param.4) | copy-start | bytes 3538948
  81.9 1.4 %copy-start.2 = (bf16[1024,1152]{1,0:T(8,128)(2,1)}, bf16[1024,1152]{1,0:T(8,128)(2,1)S(1)}, u32[]{:S(2)}) copy-start(bf16[1024,1152]{1,0:T(8,128)(2,1)S(1)} %constant_dynamic-update-slice_fusion) | copy-start | bytes 7077892
  100.0 21.4 %all-to-all-start.2 = ((bf16[32,4,1152]{2,1,0:T(4,128)(2,1)}), bf16[32,4,1152]{2,1,0:T(4,128)(2,1)S(1)}, u32[]{:S(2)}, u32[]{:S(2)}) async-start(bf16[32,4,1152]{2,1,0:T(4,128)(2,1)} %all_to_all.22), calls=%async_computation.2 | async-start | bytes 589824 | tf_op jit(solution)/shard_map/all_to_all | solution.py:65
Sparse Core Ops, SparseCore 0:
  9.8 72.4 all-gather.1

commit v2 on v0

v2 whole, which is shorter than its diff:
```python
import functools

import jax
import jax.numpy as jnp
from jax import lax
from jax.experimental import pallas as pl
from jax.experimental.pallas import tpu as pltpu
from jax.sharding import Mesh, PartitionSpec as P

STEPS = 2
NX, NZ, NY, NC = 4, 8, 4, 2
AXES = ("x", "z", "y", "c")
PLANE = NX * NZ
f32, bf16, i32 = jnp.float32, jnp.bfloat16, jnp.int32
VMEM = pl.BlockSpec(memory_space=pltpu.VMEM)
SMEM = pl.BlockSpec(memory_space=pltpu.SMEM)


def device(x, z, y, c):
    return ((x * NZ + z) * NY + y) * NC + c


def around(a, way):
    pairs = [
        (y * NC + c, (y + way * (1 - 2 * c)) % NY * NC + c) for y in range(NY) for c in range(NC)
    ]
    return lax.ppermute(a, ("y", "c"), pairs)


def along_y(a, shift):
    return lax.ppermute(a, "y", [(i, (i + shift) % NY) for i in range(NY)])


def other_core(a):
    return lax.ppermute(a, "c", [(0, 1), (1, 0)])


def call(body, outs, args, flops=0, scalars=1, **options):
    moved = sum(a.size * a.dtype.itemsize for a in (*args, *outs))
    single = len(outs) == 1
    return pl.pallas_call(
        body,
        out_shape=outs[0] if single else outs,
        in_specs=options.pop("in_specs", [SMEM] * scalars + [VMEM] * (len(args) - scalars)),
        out_specs=VMEM if single else [VMEM] * len(outs),
        compiler_params=pltpu.CompilerParams(vmem_limit_bytes=48 * 2**20),
        cost_estimate=pl.CostEstimate(flops=flops, bytes_accessed=moved, transcendentals=0),
        **options,
    )(*args)


def shaped(*shape, dtype=bf16):
    return jax.ShapeDtypeStruct(shape, dtype)


def slices_kernel(place, text, *refs):
    *outs, sems = refs
    span = outs[0].shape[0]
    copies = []
    for n, out in enumerate(outs):
        at = pl.multiple_of((place[0] + n) % NX * span, span)
        copies.append(pltpu.make_async_copy(text.at[pl.ds(at, span), :], out, sems.at[n]))
        copies[-1].start()
    for copy in copies:
        copy.wait()


def join_kernel(place, *refs):
    *got, out = refs
    x, c = place[0], place[3]
    per = out.shape[1] // STEPS

    def fill(at, core):
        for s in range(STEPS):
            source = got[core * NX + (at - s * (NX // STEPS)) % NX]
            for p in range(out.shape[0]):
                first = (p * NC + core) * per
                out[p, s * per:(s + 1) * per, :] = source[first:first + per, :]

    for at in range(NX):
        for core in range(NC):
            pl.when((x == at) & (c == core))(functools.partial(fill, at, core))


def flat_kernel(chunks, out):
    n = chunks.shape[1]
    for p in range(chunks.shape[0]):
        out[p * n:(p + 1) * n, :] = chunks[p]


def text_row(t, y, c, per):
    return t // per % STEPS, ((t // (STEPS * per) * NY + y) * NC + c) * per + t % per


def term_kernel(turns, place, factors, own, other, *refs):
    images, rest = refs[:len(turns)], refs[len(turns):]
    x, z, y, c = (place[n] for n in range(4))
    scale, bias = factors[0], factors[1]
    count = own.shape[0]
    per = count // (PLANE * STEPS)
    block = jnp.concatenate([own[...], other[...]], axis=0)
    last = len(rest) > 1
    total = rest[0][...] if last else None
    for image, turn in zip(images, turns, strict=True):
        rows = image.shape[0]
        logits = scale * lax.dot_general(
            block, image[...], (((1,), (1,)), ((), ())), preferred_element_type=f32
        ) + bias
        t = lax.broadcasted_iota(i32, (NC * count, 1), 0)
        step, row = text_row(t % count, y, (c + t // count) % NC, per)
        held = (z == 0) & (c == 0) & ((y + turn) % NY == 0)
        row = jnp.where(held & (step * (NX // STEPS) == x), row, -1)
        b = lax.broadcasted_iota(i32, (NC * count, rows), 1)
        weights = (jax.nn.sigmoid(logits) - (b == row).astype(f32)).astype(bf16)
        term = jnp.dot(weights, image[...], preferred_element_type=f32)
        total = term if total is None else total + term
    if last:
        rest[1][...] = total[:count]
        rest[2][...] = total[count:].astype(bf16)
    else:
        rest[0][...] = total


def add_kernel(mine, received, out):
    n = out.shape[1]
    total = (mine[...] + received[...].astype(f32)).astype(bf16)
    for p in range(out.shape[0]):
        out[p] = total[p * n:(p + 1) * n, :]


def sum_kernel(factors, terms, out):
    total = terms[0].astype(f32)
    for p in range(1, terms.shape[0]):
        total = total + terms[p].astype(f32)
    total = factors[0] * total
    per = out.shape[1]
    for s in range(STEPS):
        out[s] = total[s * per:(s + 1) * per, :]


def image_kernel(place, factors, image, *refs):
    *texts, grad, loss = refs
    x, z, y, c = (place[n] for n in range(4))
    scale, bias = factors[0], factors[1]
    rows = image.shape[0]
    count = texts[0].shape[0]
    per = count // (PLANE * STEPS)
    held = (z == 0) & (y == 0) & (c == 0)
    total = losses = None
    for n in range(NY):
        block = jnp.concatenate([texts[n][...], texts[NY + n][...]], axis=0)
        logits = scale * lax.dot_general(
            image[...], block, (((1,), (1,)), ((), ())), preferred_element_type=f32
        ) + bias
        t = lax.broadcasted_iota(i32, (1, NC * count), 1)
        step, row = text_row(t % count, (y + NY - n) % NY, (c + t // count) % NC, per)
        row = jnp.where(held & (step * (NX // STEPS) == x), row, -1)
        b = lax.broadcasted_iota(i32, (rows, NC * count), 0)
        positive = b == row
        e = jnp.exp(-jnp.abs(logits))
        signed = jnp.where(positive, -logits, logits)
        part = jnp.sum(jnp.maximum(signed, 0.0) + jnp.log1p(e), axis=1)
        sigmoid = jnp.where(logits >= 0, 1.0, e) / (1.0 + e)
        weights = (sigmoid - positive.astype(f32)).astype(bf16)
        term = jnp.dot(weights, block, preferred_element_type=f32)
        total = term if total is None else total + term
        losses = part if losses is None else losses + part
    grad[...] = scale * total
    loss[...] = losses


def local(image, text, log_scale, logit_bias):
    rows, width = image.shape
    place = jnp.stack([lax.axis_index(a) for a in AXES]).astype(i32)
    factors = jnp.concatenate([jnp.exp(log_scale), logit_bias])
    per = rows // (PLANE * NY * NC)
    count = PLANE * STEPS * per
    side = NZ * NY * per

    pieces = call(
        slices_kernel,
        [shaped(side * NC, width)] * NX,
        (place, text),
        in_specs=[SMEM, pl.BlockSpec(memory_space=pl.ANY)],
        scratch_shapes=[pltpu.SemaphoreType.DMA((NX,))],
    )
    got = [pieces[0]] + [None] * (NX - 1)
    for n in (2, 1, 3):
        pairs = [
            (device(x, 0, 0, 0), device((x + n) % NX, 0, 0, 0)) for x in range(0, NX, NX // STEPS)
        ]
        got[n] = lax.ppermute(pieces[n], AXES, pairs)
    got += [lax.ppermute(a, "c", [(0, 1)]) for a in got]
    joined = call(join_kernel, [shaped(NZ * NY, STEPS * per, width)], (place, *got))

    images = [image, around(image, 1), around(image, -1)]
    images.append(around(images[1], 1))

    spread = lax.all_to_all(joined, ("z", "y"), 0, 0, tiled=True)
    everywhere = jnp.broadcast_to(spread[:1], (PLANE, STEPS * per, width))
    everywhere, images[1] = lax.optimization_barrier((everywhere, images[1]))
    chunks = lax.all_to_all(everywhere, ("x", "z"), 0, 0, tiled=True)
    texts = call(flat_kernel, [shaped(count, width)], (chunks,), scalars=0)

    other = other_core(texts)
    turns = (0, NY - 1, 1, 2)
    flops = 4 * rows * NC * count * width
    early = call(
        functools.partial(term_kernel, turns[:3]),
        [shaped(NC * count, width, dtype=f32)],
        (place, factors, texts, other, *images[:3]),
        flops=3 * flops,
        scalars=2,
    )
    mine, theirs = call(
        functools.partial(term_kernel, turns[3:]),
        [shaped(count, width, dtype=f32), shaped(count, width)],
        (place, factors, texts, other, *images[3:], early),
        flops=flops,
        scalars=2,
    )
    term = call(
        add_kernel, [shaped(PLANE, STEPS * per, width)], (mine, other_core(theirs)), scalars=0
    )
    terms = lax.all_to_all(term, ("x", "z"), 0, 0, tiled=True)
    text_grad = call(sum_kernel, [shaped(STEPS, per, width, dtype=f32)], (factors, terms))

    line = [texts] + [along_y(texts, n) for n in range(1, NY)]
    across = [other] + [other_core(a) for a in line[1:]]
    image_grad, row_loss = call(
        image_kernel,
        [shaped(rows, width, dtype=f32), shaped(rows, dtype=f32)],
        (place, factors, image, *line, *across),
        flops=NY * flops,
        scalars=2,
    )
    return image_grad, text_grad, row_loss


def solution(mesh):
    mesh = Mesh(mesh.devices.reshape(NX, NZ, NY, NC), AXES)
    in_specs = (P(AXES, None), P(AXES, None), P(), P())
    out_specs = (P(AXES, None), P(None, AXES, None), P(AXES))
    return jax.shard_map(local, mesh=mesh, in_specs=in_specs, out_specs=out_specs, check_vma=False)
```

time: 568 us -> 96.2 us (0.17)
  waiting for transfers between devices: 530 us -> 17.8 us
  starting transfers between devices: 0.08 us -> 37.7 us
  blocking collectives: 0 us -> 17.9 us
  Pallas kernels: 0 us -> 17.5 us
  matrix products: 13.6 us -> 0 us
  between operations: 15.4 us -> 2.16 us
    psum x1 -> x0, waiting for transfers between devices: 265 us -> none  [broadcast(): return lax.psum(jnp.where(mine, shard, jnp.zeros_like(shard)), axis)]
    unnamed x3 -> x0, waiting for transfers between devices: 265 us -> none
    all_to_all x0 -> x2, starting transfers between devices: none -> 19.3 us  [the longest x1 11.2 us: local(): spread = lax.all_to_all(joined, ('z', 'y'), 0, 0, tiled=True)]
    ppermute x0 -> x18, starting transfers between devices: none -> 18.4 us  [the longest x4 6.97 us: local(): got += [lax.ppermute(a, 'c', [(0, 1)]) for a in got]]
    all_to_all x0 -> x1, blocking collectives: none -> 17.9 us  [local(): chunks = lax.all_to_all(everywhere, ('x', 'z'), 0, 0, tiled=True)]
    pallas_call x0 -> x8, Pallas kernels: none -> 17.5 us  [call(): pl.pallas_call(body, out_shape=outs[0] if single else outs, in_specs=opti...]
    dot_general x6 -> x0, matrix products: 13.6 us -> none  [the longest x2 4.84 us: local(): lax.dot_general(weights, image_emb, (((0,), (0,)), ((), ())), preferred_e...]
    all_to_all x0 -> x2, waiting for transfers between devices: none -> 10.9 us  [the longest x1 10.9 us: local(): spread = lax.all_to_all(joined, ('z', 'y'), 0, 0, tiled=True)]
  transfers between devices with their start and end apart: 2 -> 20, of which waited for: 2 -> 8; matrix products, arithmetic and copies ran while one was open for 1% -> 0% of each run, Pallas kernels for 0% -> 15%
where the time goes in v2:
time: 96.2 us; the launch traced here: 94.6 us
  starting transfers between devices  37.7 us (39%)
  blocking collectives  17.9 us (19%)
  waiting for transfers between devices  17.8 us (19%)
  Pallas kernels  17.5 us (18%)
  between operations  2.16 us (2%)
  local copies, waits for them, and re-layouts  1.37 us (1%)
    all_to_all x1, blocking collectives, local(): chunks = lax.all_to_all(everywhere, ('x', 'z'), 0, 0, tiled=True)  17.9 us
    pallas_call x8, Pallas kernels, call(): pl.pallas_call(body, out_shape=outs[0] if single else outs, in_specs=opti...  17.5 us
    all_to_all x1, starting transfers between devices, local(): spread = lax.all_to_all(joined, ('z', 'y'), 0, 0, tiled=True)  11.2 us
    all_to_all x1, waiting for transfers between devices, local(): spread = lax.all_to_all(joined, ('z', 'y'), 0, 0, tiled=True)  10.9 us
    all_to_all x1, starting transfers between devices, local(): terms = lax.all_to_all(term, ('x', 'z'), 0, 0, tiled=True)  8.18 us
    ppermute x4, starting transfers between devices, local(): got += [lax.ppermute(a, 'c', [(0, 1)]) for a in got]  6.97 us
    ppermute x3, starting transfers between devices, around(): return lax.ppermute(a, ('y', 'c'), pairs)  4.43 us
    ppermute x3, starting transfers between devices, along_y(): return lax.ppermute(a, 'y', [(i, (i + shift) % NY) for i in range(NY)])  3.91 us
  transfers between devices with their start and end apart: 20, of which 8 were waited for; matrix products, arithmetic and copies ran while one was open for 0% of the time, Pallas kernels for 15%

profile of v2, /device:TPU:32, one launch (start us, length us, event | category | flops | bytes accessed | tf_op | source)
XLA Modules:
  0.0 94.6 jit_solution(17283985485462276739)
XLA Ops:
  0.6 1.7 %collective-permute-start.7 = (bf16[512,1152]{1,0:T(8,128)(2,1)}, bf16[512,1152]{1,0:T(8,128)(2,1)}, u32[]{:S(2)}, u32[]{:S(2)}) collective-permute-start(bf16[512,1152]{1,0:T(8,128)(2,1)} %refs_0_.1), channel_id=1, source_target_pairs={{0,2},{1,7},{2,4},{3,1},{4,6},{5,3},{6,0},{7,5},{8,10},{9,15},{10,... | collective-permute-start | bytes 3538952 | tf_op jit(solution)/shard_map/ppermute | solution.py:27
  2.4 1.3 %copy-done = bf16[512,1152]{1,0:T(8,128)(2,1)S(1)} copy-done((bf16[512,1152]{1,0:T(8,128)(2,1)S(1)}, bf16[512,1152]{1,0:T(8,128)(2,1)}, u32[]{:S(2)}) %copy-start) | copy-done | bytes 1179672
  3.6 0.9 shard_map.67
  5.2 0.7 collective-permute-start.1
  6.6 3.0 %collective-permute-start.3 = (bf16[128,1152]{1,0:T(8,128)(2,1)S(1)}, bf16[128,1152]{1,0:T(8,128)(2,1)S(1)}, u32[]{:S(2)}, u32[]{:S(2)}) collective-permute-start(bf16[128,1152]{1,0:T(8,128)(2,1)S(1)} %get-tuple-element.13.refs_0_), channel_id=1, source_target_pairs={{0,1},{2,3},{4,5},{6,7},{8,9},{10,11},{12,13},{14,15},{16,17},{18,... | collective-permute-start | bytes 884744 | tf_op jit(solution)/shard_map/ppermute | solution.py:193
  9.6 1.3 %collective-permute-start.4 = (bf16[128,1152]{1,0:T(8,128)(2,1)S(1)}, bf16[128,1152]{1,0:T(8,128)(2,1)S(1)}, u32[]{:S(2)}, u32[]{:S(2)}) collective-permute-start(bf16[128,1152]{1,0:T(8,128)(2,1)S(1)} %collective-permute-done.refs_1_), channel_id=1, source_target_pairs={{0,1},{2,3},{4,5},{6,7},{8,9},{10,11},{12,13},{14,15},{16,17},{18,... | collective-permute-start | bytes 884744 | tf_op jit(solution)/shard_map/ppermute | solution.py:193
  11.0 1.3 %collective-permute-start.5 = (bf16[128,1152]{1,0:T(8,128)(2,1)S(1)}, bf16[128,1152]{1,0:T(8,128)(2,1)S(1)}, u32[]{:S(2)}, u32[]{:S(2)}) collective-permute-start(bf16[128,1152]{1,0:T(8,128)(2,1)S(1)} %collective-permute-done.1.refs_2_), channel_id=1, source_target_pairs={{0,1},{2,3},{4,5},{6,7},{8,9},{10,11},{12,13},{14,15},{16,17},{18,... | collective-permute-start | bytes 884744 | tf_op jit(solution)/shard_map/ppermute | solution.py:193
  12.3 1.3 %collective-permute-start.6 = (bf16[128,1152]{1,0:T(8,128)(2,1)S(1)}, bf16[128,1152]{1,0:T(8,128)(2,1)S(1)}, u32[]{:S(2)}, u32[]{:S(2)}) collective-permute-start(bf16[128,1152]{1,0:T(8,128)(2,1)S(1)} %collective-permute-done.2.refs_3_), channel_id=1, source_target_pairs={{0,1},{2,3},{4,5},{6,7},{8,9},{10,11},{12,13},{14,15},{16,17},{18,... | collective-permute-start | bytes 884744 | tf_op jit(solution)/shard_map/ppermute | solution.py:193
  13.6 1.1 %collective-permute-done.6.refs_7_ = bf16[128,1152]{1,0:T(8,128)(2,1)S(1)} collective-permute-done((bf16[128,1152]{1,0:T(8,128)(2,1)S(1)}, bf16[128,1152]{1,0:T(8,128)(2,1)S(1)}, u32[]{:S(2)}, u32[]{:S(2)}) %collective-permute-start.6) | collective-permute-done | bytes 294944 | tf_op jit(solution)/shard_map/ppermute | solution.py:193
  14.8 1.5 %shard_map.68 = bf16[32,4,1152]{2,1,0:T(4,128)(2,1)} custom-call(s32[4]{0:T(128)S(1)} %pad_add_fusion.place, bf16[128,1152]{1,0:T(8,128)(2,1)S(1)} %get-tuple-element.13.refs_0_, bf16[128,1152]{1,0:T(8,128)(2,1)S(1)} %collective-permute-done.refs_1_, bf16[128,1152]{1,0:T(8,128)(2,1)S(1)} %collective-permute-done.1.refs_2_, ...), custom_call_target="tpu_custom_call" | custom-call | bytes 2654224 | tf_op jit(solution)/shard_map/pallas_call | solution.py:41
  16.3 11.2 %all-to-all-start = ((bf16[32,4,1152]{2,1,0:T(4,128)(2,1)}), bf16[32,4,1152]{2,1,0:T(4,128)(2,1)S(1)}, u32[]{:S(2)}, u32[]{:S(2)}) async-start(bf16[32,4,1152]{2,1,0:T(4,128)(2,1)} %shard_map.68), calls=%async_computation | async-start | bytes 589824 | tf_op jit(solution)/shard_map/all_to_all | solution.py:199
  27.4 2.8 %collective-permute-start.16 = (bf16[512,1152]{1,0:T(8,128)(2,1)S(1)}, bf16[512,1152]{1,0:T(8,128)(2,1)}, u32[]{:S(2)}, u32[]{:S(2)}) collective-permute-start(bf16[512,1152]{1,0:T(8,128)(2,1)S(1)} %copy-done.1), channel_id=1, source_target_pairs={{0,6},{1,3},{2,0},{3,5},{4,2},{5,7},{6,4},{7,1},{8,14},{9,11},{10,... | collective-permute-start | bytes 3538952 | tf_op jit(solution)/shard_map/ppermute | solution.py:27
  30.2 10.9 %all-to-all-done = bf16[32,4,1152]{2,1,0:T(4,128)(2,1)S(1)} async-done(((bf16[32,4,1152]{2,1,0:T(4,128)(2,1)}), bf16[32,4,1152]{2,1,0:T(4,128)(2,1)S(1)}, u32[]{:S(2)}, u32[]{:S(2)}) %all-to-all-start) | async-done | bytes 294944 | tf_op jit(solution)/shard_map/all_to_all | solution.py:199
  41.2 17.9 %all_to_all.15.chunks = bf16[32,4,1152]{2,1,0:T(4,128)(2,1)S(1)} all-to-all(bf16[32,4,1152]{2,1,0:T(4,128)(2,1)S(1)} %broadcast_in_dim.8), channel_id=1, replica_groups=mesh['x'=4,'z'=8,'y'=4,'c'=2] {'x','z'}, dimensions={0} | all-to-all | bytes 589824 | tf_op jit(solution)/shard_map/all_to_all | solution.py:202
  60.8 4.2 %shard_map.71.refs_1_ = f32[256,1152]{1,0:T(8,128)S(1)} custom-call(s32[4]{0:T(128)S(1)} %pad_add_fusion.place, f32[2]{0:T(128)S(1)} %pad_maximum_fusion.factors, bf16[128,1152]{1,0:T(8,128)(2,1)S(1)} %shard_map.69.refs_0_.own, bf16[128,1152]{1,0:T(8,128)(2,1)S(1)} %collective-permute-done.11.refs_4_.other, bf16[512,1152]{1,0:T(8,128)(2,1)S(1)} %copy-done.1, ...), custom_call_target="tpu_custom_call" | custom-call | flops 1811939328 | bytes 5308440 | tf_op jit(solution)/shard_map/pallas_call | solution.py:41
  65.1 1.7 %shard_map.72 = (f32[128,1152]{1,0:T(8,128)S(1)}, bf16[128,1152]{1,0:T(8,128)(2,1)S(1)}) custom-call(s32[4]{0:T(128)S(1)} %pad_add_fusion.place, f32[2]{0:T(128)S(1)} %pad_maximum_fusion.factors, bf16[128,1152]{1,0:T(8,128)(2,1)S(1)} %shard_map.69.refs_0_.own, bf16[128,1152]{1,0:T(8,128)(2,1)S(1)} %collective-permute-done.11.refs_4_.other, ...), custom_call_target="tpu_custom_call" | custom-call | flops 603979776 | bytes 3833880 | tf_op jit(solution)/shard_map/pallas_call | solution.py:41
  67.6 2.1 %collective-permute-start.9 = (bf16[128,1152]{1,0:T(8,128)(2,1)S(1)}, bf16[128,1152]{1,0:T(8,128)(2,1)S(1)}, u32[]{:S(2)}, u32[]{:S(2)}) collective-permute-start(bf16[128,1152]{1,0:T(8,128)(2,1)S(1)} %shard_map.69.refs_0_.own), channel_id=1, source_target_pairs={{0,4},{2,6},{4,0},{6,2},{1,5},{3,7},{5,1},{7,3},{8,12},{10,14},{12... | collective-permute-start | bytes 884744 | tf_op jit(solution)/shard_map/ppermute | solution.py:31
  69.7 1.4 %collective-permute-start.10 = (bf16[128,1152]{1,0:T(8,128)(2,1)S(1)}, bf16[128,1152]{1,0:T(8,128)(2,1)S(1)}, u32[]{:S(2)}, u32[]{:S(2)}) collective-permute-start(bf16[128,1152]{1,0:T(8,128)(2,1)S(1)} %shard_map.69.refs_0_.own), channel_id=1, source_target_pairs={{0,6},{2,0},{4,2},{6,4},{1,7},{3,1},{5,3},{7,5},{8,14},{10,8},{12,... | collective-permute-start | bytes 884744 | tf_op jit(solution)/shard_map/ppermute | solution.py:31
  71.1 0.8 shard_map.73
  71.9 8.2 %all-to-all-start.2 = ((bf16[32,4,1152]{2,1,0:T(4,128)(2,1)}), bf16[32,4,1152]{2,1,0:T(4,128)(2,1)S(1)}, u32[]{:S(2)}, u32[]{:S(2)}) async-start(bf16[32,4,1152]{2,1,0:T(4,128)(2,1)} %shard_map.73), calls=%async_computation.2 | async-start | bytes 589824 | tf_op jit(solution)/shard_map/all_to_all | solution.py:225
  80.1 3.7 %collective-permute-done.8.refs_1_ = bf16[128,1152]{1,0:T(8,128)(2,1)S(1)} collective-permute-done((bf16[128,1152]{1,0:T(8,128)(2,1)S(1)}, bf16[128,1152]{1,0:T(8,128)(2,1)S(1)}, u32[]{:S(2)}, u32[]{:S(2)}) %collective-permute-start.8) | collective-permute-done | bytes 294944 | tf_op jit(solution)/shard_map/ppermute | solution.py:31
  84.4 1.0 %collective-permute-done.12.refs_5_ = bf16[128,1152]{1,0:T(8,128)(2,1)S(1)} collective-permute-done((bf16[128,1152]{1,0:T(8,128)(2,1)S(1)}, bf16[128,1152]{1,0:T(8,128)(2,1)S(1)}, u32[]{:S(2)}, u32[]{:S(2)}) %collective-permute-start.12) | collective-permute-done | bytes 294944 | tf_op jit(solution)/shard_map/ppermute | solution.py:35
  86.2 7.2 %shard_map.70 = (f32[512,1152]{1,0:T(8,128)}, f32[512]{0:T(512)}) custom-call(s32[4]{0:T(128)S(1)} %pad_add_fusion.place, f32[2]{0:T(128)S(1)} %pad_maximum_fusion.factors, bf16[512,1152]{1,0:T(8,128)(2,1)S(1)} %copy-done.1, bf16[128,1152]{1,0:T(8,128)(2,1)S(1)} %shard_map.69.refs_0_.own, bf16[128,1152]{1,0:T(8,128)(2,1)S(1)} %collective-permute-done.8.refs_1_, ...), custom_call_target="tpu_custom_call" | custom-call | flops 2415919104 | bytes 5900312 | tf_op jit(solution)/shard_map/pallas_call | solution.py:41
  93.4 1.2 %shard_map.74 = f32[2,2,1152]{2,1,0:T(2,128)} custom-call(f32[2]{0:T(128)S(1)} %pad_maximum_fusion.factors, bf16[32,4,1152]{2,1,0:T(4,128)(2,1)S(1)} %all-to-all-done.2.terms), custom_call_target="tpu_custom_call" | custom-call | bytes 313352 | tf_op jit(solution)/shard_map/pallas_call | solution.py:41
  (33 shorter events, 4.3 us)
Async XLA Ops:
  0.6 29.6 %collective-permute-start.7 = (bf16[512,1152]{1,0:T(8,128)(2,1)}, bf16[512,1152]{1,0:T(8,128)(2,1)}, u32[]{:S(2)}, u32[]{:S(2)}) collective-permute-start(bf16[512,1152]{1,0:T(8,128)(2,1)} %refs_0_.1), channel_id=1, source_target_pairs={{0,2},{1,7},{2,4},{3,1},{4,6},{5,3},{6,0},{7,5},{8,10},{9,15},{10,... | collective-permute-start | bytes 3538952 | tf_op jit(solution)/shard_map/ppermute | solution.py:27
  2.4 1.3 %copy-start = (bf16[512,1152]{1,0:T(8,128)(2,1)S(1)}, bf16[512,1152]{1,0:T(8,128)(2,1)}, u32[]{:S(2)}) copy-start(bf16[512,1152]{1,0:T(8,128)(2,1)} %text.1) | copy-start | bytes 3538948
  4.5 5.1 %collective-permute-start = (bf16[128,1152]{1,0:T(8,128)(2,1)S(1)}, bf16[128,1152]{1,0:T(8,128)(2,1)S(1)}, u32[]{:S(2)}, u32[]{:S(2)}) collective-permute-start(bf16[128,1152]{1,0:T(8,128)(2,1)S(1)} %get-tuple-element.14), channel_id=1, source_target_pairs={{0,64},{128,192}} | collective-permute-start | bytes 884744 | tf_op jit(solution)/shard_map/ppermute | solution.py:192
  5.2 5.8 %collective-permute-start.1 = (bf16[128,1152]{1,0:T(8,128)(2,1)S(1)}, bf16[128,1152]{1,0:T(8,128)(2,1)S(1)}, u32[]{:S(2)}, u32[]{:S(2)}) collective-permute-start(bf16[128,1152]{1,0:T(8,128)(2,1)S(1)} %get-tuple-element.15), channel_id=1, source_target_pairs={{0,128},{128,0}} | collective-permute-start | bytes 884744 | tf_op jit(solution)/shard_map/ppermute | solution.py:192
  5.9 6.4 %collective-permute-start.2 = (bf16[128,1152]{1,0:T(8,128)(2,1)S(1)}, bf16[128,1152]{1,0:T(8,128)(2,1)S(1)}, u32[]{:S(2)}, u32[]{:S(2)}) collective-permute-start(bf16[128,1152]{1,0:T(8,128)(2,1)S(1)} %get-tuple-element.16), channel_id=1, source_target_pairs={{0,192},{128,64}} | collective-permute-start | bytes 884744 | tf_op jit(solution)/shard_map/ppermute | solution.py:192
  6.6 20.9 %copy-start.1 = (bf16[512,1152]{1,0:T(8,128)(2,1)S(1)}, bf16[512,1152]{1,0:T(8,128)(2,1)}, u32[]{:S(2)}) copy-start(bf16[512,1152]{1,0:T(8,128)(2,1)} %refs_0_.1) | copy-start | bytes 3538948
  6.6 7.0 %collective-permute-start.3 = (bf16[128,1152]{1,0:T(8,128)(2,1)S(1)}, bf16[128,1152]{1,0:T(8,128)(2,1)S(1)}, u32[]{:S(2)}, u32[]{:S(2)}) collective-permute-start(bf16[128,1152]{1,0:T(8,128)(2,1)S(1)} %get-tuple-element.13.refs_0_), channel_id=1, source_target_pairs={{0,1},{2,3},{4,5},{6,7},{8,9},{10,11},{12,13},{14,15},{16,17},{18,... | collective-permute-start | bytes 884744 | tf_op jit(solution)/shard_map/ppermute | solution.py:193
  9.6 4.0 %collective-permute-start.4 = (bf16[128,1152]{1,0:T(8,128)(2,1)S(1)}, bf16[128,1152]{1,0:T(8,128)(2,1)S(1)}, u32[]{:S(2)}, u32[]{:S(2)}) collective-permute-start(bf16[128,1152]{1,0:T(8,128)(2,1)S(1)} %collective-permute-done.refs_1_), channel_id=1, source_target_pairs={{0,1},{2,3},{4,5},{6,7},{8,9},{10,11},{12,13},{14,15},{16,17},{18,... | collective-permute-start | bytes 884744 | tf_op jit(solution)/shard_map/ppermute | solution.py:193
  11.0 2.7 %collective-permute-start.5 = (bf16[128,1152]{1,0:T(8,128)(2,1)S(1)}, bf16[128,1152]{1,0:T(8,128)(2,1)S(1)}, u32[]{:S(2)}, u32[]{:S(2)}) collective-permute-start(bf16[128,1152]{1,0:T(8,128)(2,1)S(1)} %collective-permute-done.1.refs_2_), channel_id=1, source_target_pairs={{0,1},{2,3},{4,5},{6,7},{8,9},{10,11},{12,13},{14,15},{16,17},{18,... | collective-permute-start | bytes 884744 | tf_op jit(solution)/shard_map/ppermute | solution.py:193
  12.3 2.5 %collective-permute-start.6 = (bf16[128,1152]{1,0:T(8,128)(2,1)S(1)}, bf16[128,1152]{1,0:T(8,128)(2,1)S(1)}, u32[]{:S(2)}, u32[]{:S(2)}) collective-permute-start(bf16[128,1152]{1,0:T(8,128)(2,1)S(1)} %collective-permute-done.2.refs_3_), channel_id=1, source_target_pairs={{0,1},{2,3},{4,5},{6,7},{8,9},{10,11},{12,13},{14,15},{16,17},{18,... | collective-permute-start | bytes 884744 | tf_op jit(solution)/shard_map/ppermute | solution.py:193
  16.3 24.8 %all-to-all-start = ((bf16[32,4,1152]{2,1,0:T(4,128)(2,1)}), bf16[32,4,1152]{2,1,0:T(4,128)(2,1)S(1)}, u32[]{:S(2)}, u32[]{:S(2)}) async-start(bf16[32,4,1152]{2,1,0:T(4,128)(2,1)} %shard_map.68), calls=%async_computation | async-start | bytes 589824 | tf_op jit(solution)/shard_map/all_to_all | solution.py:199
  27.4 33.2 %collective-permute-start.16 = (bf16[512,1152]{1,0:T(8,128)(2,1)S(1)}, bf16[512,1152]{1,0:T(8,128)(2,1)}, u32[]{:S(2)}, u32[]{:S(2)}) collective-permute-start(bf16[512,1152]{1,0:T(8,128)(2,1)S(1)} %copy-done.1), channel_id=1, source_target_pairs={{0,6},{1,3},{2,0},{3,5},{4,2},{5,7},{6,4},{7,1},{8,14},{9,11},{10,... | collective-permute-start | bytes 3538952 | tf_op jit(solution)/shard_map/ppermute | solution.py:27
  30.2 34.9 %collective-permute-start.15 = (bf16[512,1152]{1,0:T(8,128)(2,1)}, bf16[512,1152]{1,0:T(8,128)(2,1)S(1)}, u32[]{:S(2)}, u32[]{:S(2)}) collective-permute-start(bf16[512,1152]{1,0:T(8,128)(2,1)} %collective-permute-done.7.refs_1_), channel_id=1, source_target_pairs={{0,2},{1,7},{2,4},{3,1},{4,6},{5,3},{6,0},{7,5},{8,10},{9,15},{10,... | collective-permute-start | bytes 3538952 | tf_op jit(solution)/shard_map/ppermute | solution.py:27
  59.2 1.7 %collective-permute-start.11 = (bf16[128,1152]{1,0:T(8,128)(2,1)S(1)}, bf16[128,1152]{1,0:T(8,128)(2,1)S(1)}, u32[]{:S(2)}, u32[]{:S(2)}) collective-permute-start(bf16[128,1152]{1,0:T(8,128)(2,1)S(1)} %shard_map.69.refs_0_.own), channel_id=1, source_target_pairs={{0,1},{1,0},{2,3},{3,2},{4,5},{5,4},{6,7},{7,6},{8,9},{9,8},{10,11... | collective-permute-start | bytes 884744 | tf_op jit(solution)/shard_map/ppermute | solution.py:35
  66.8 4.3 %collective-permute-start.17 = (bf16[128,1152]{1,0:T(8,128)(2,1)S(1)}, bf16[128,1152]{1,0:T(8,128)(2,1)S(1)}, u32[]{:S(2)}, u32[]{:S(2)}) collective-permute-start(bf16[128,1152]{1,0:T(8,128)(2,1)S(1)} %get-tuple-element.21), channel_id=1, source_target_pairs={{0,1},{1,0},{2,3},{3,2},{4,5},{5,4},{6,7},{7,6},{8,9},{9,8},{10,11... | collective-permute-start | bytes 884744 | tf_op jit(solution)/shard_map/ppermute | solution.py:35
  67.2 16.6 %collective-permute-start.8 = (bf16[128,1152]{1,0:T(8,128)(2,1)S(1)}, bf16[128,1152]{1,0:T(8,128)(2,1)S(1)}, u32[]{:S(2)}, u32[]{:S(2)}) collective-permute-start(bf16[128,1152]{1,0:T(8,128)(2,1)S(1)} %shard_map.69.refs_0_.own), channel_id=1, source_target_pairs={{0,2},{2,4},{4,6},{6,0},{1,3},{3,5},{5,7},{7,1},{8,10},{10,12},{12... | collective-permute-start | bytes 884744 | tf_op jit(solution)/shard_map/ppermute | solution.py:31
  67.6 16.2 %collective-permute-start.9 = (bf16[128,1152]{1,0:T(8,128)(2,1)S(1)}, bf16[128,1152]{1,0:T(8,128)(2,1)S(1)}, u32[]{:S(2)}, u32[]{:S(2)}) collective-permute-start(bf16[128,1152]{1,0:T(8,128)(2,1)S(1)} %shard_map.69.refs_0_.own), channel_id=1, source_target_pairs={{0,4},{2,6},{4,0},{6,2},{1,5},{3,7},{5,1},{7,3},{8,12},{10,14},{12... | collective-permute-start | bytes 884744 | tf_op jit(solution)/shard_map/ppermute | solution.py:31
  69.7 14.7 %collective-permute-start.10 = (bf16[128,1152]{1,0:T(8,128)(2,1)S(1)}, bf16[128,1152]{1,0:T(8,128)(2,1)S(1)}, u32[]{:S(2)}, u32[]{:S(2)}) collective-permute-start(bf16[128,1152]{1,0:T(8,128)(2,1)S(1)} %shard_map.69.refs_0_.own), channel_id=1, source_target_pairs={{0,6},{2,0},{4,2},{6,4},{1,7},{3,1},{5,3},{7,5},{8,14},{10,8},{12,... | collective-permute-start | bytes 884744 | tf_op jit(solution)/shard_map/ppermute | solution.py:31
  71.9 21.5 %all-to-all-start.2 = ((bf16[32,4,1152]{2,1,0:T(4,128)(2,1)}), bf16[32,4,1152]{2,1,0:T(4,128)(2,1)S(1)}, u32[]{:S(2)}, u32[]{:S(2)}) async-start(bf16[32,4,1152]{2,1,0:T(4,128)(2,1)} %shard_map.73), calls=%async_computation.2 | async-start | bytes 589824 | tf_op jit(solution)/shard_map/all_to_all | solution.py:225
  83.8 1.6 %collective-permute-start.12 = (bf16[128,1152]{1,0:T(8,128)(2,1)S(1)}, bf16[128,1152]{1,0:T(8,128)(2,1)S(1)}, u32[]{:S(2)}, u32[]{:S(2)}) collective-permute-start(bf16[128,1152]{1,0:T(8,128)(2,1)S(1)} %collective-permute-done.8.refs_1_), channel_id=1, source_target_pairs={{0,1},{1,0},{2,3},{3,2},{4,5},{5,4},{6,7},{7,6},{8,9},{9,8},{10,11... | collective-permute-start | bytes 884744 | tf_op jit(solution)/shard_map/ppermute | solution.py:35
  83.8 2.0 %collective-permute-start.13 = (bf16[128,1152]{1,0:T(8,128)(2,1)S(1)}, bf16[128,1152]{1,0:T(8,128)(2,1)S(1)}, u32[]{:S(2)}, u32[]{:S(2)}) collective-permute-start(bf16[128,1152]{1,0:T(8,128)(2,1)S(1)} %collective-permute-done.9.refs_2_), channel_id=1, source_target_pairs={{0,1},{1,0},{2,3},{3,2},{4,5},{5,4},{6,7},{7,6},{8,9},{9,8},{10,11... | collective-permute-start | bytes 884744 | tf_op jit(solution)/shard_map/ppermute | solution.py:35
  84.4 1.8 %collective-permute-start.14 = (bf16[128,1152]{1,0:T(8,128)(2,1)S(1)}, bf16[128,1152]{1,0:T(8,128)(2,1)S(1)}, u32[]{:S(2)}, u32[]{:S(2)}) collective-permute-start(bf16[128,1152]{1,0:T(8,128)(2,1)S(1)} %collective-permute-done.10.refs_3_), channel_id=1, source_target_pairs={{0,1},{1,0},{2,3},{3,2},{4,5},{5,4},{6,7},{7,6},{8,9},{9,8},{10,11... | collective-permute-start | bytes 884744 | tf_op jit(solution)/shard_map/ppermute | solution.py:35

commit v3 on v2

--- a/solution.py
+++ b/solution.py
@@ -43,7 +43,7 @@
         out_shape=outs[0] if single else outs,
         in_specs=options.pop("in_specs", [SMEM] * scalars + [VMEM] * (len(args) - scalars)),
         out_specs=VMEM if single else [VMEM] * len(outs),
-        compiler_params=pltpu.CompilerParams(vmem_limit_bytes=48 * 2**20),
+        compiler_params=pltpu.CompilerParams(vmem_limit_bytes=16 * 2**20),
         cost_estimate=pl.CostEstimate(flops=flops, bytes_accessed=moved, transcendentals=0),
         **options,
     )(*args)
@@ -53,39 +53,67 @@
     return jax.ShapeDtypeStruct(shape, dtype)
 
 
-def slices_kernel(place, text, *refs):
-    *outs, sems = refs
-    span = outs[0].shape[0]
-    copies = []
-    for n, out in enumerate(outs):
-        at = pl.multiple_of((place[0] + n) % NX * span, span)
-        copies.append(pltpu.make_async_copy(text.at[pl.ds(at, span), :], out, sems.at[n]))
-        copies[-1].start()
-    for copy in copies:
-        copy.wait()
-
-
-def join_kernel(place, *refs):
-    *got, out = refs
-    x, c = place[0], place[3]
-    per = out.shape[1] // STEPS
-
-    def fill(at, core):
-        for s in range(STEPS):
-            source = got[core * NX + (at - s * (NX // STEPS)) % NX]
-            for p in range(out.shape[0]):
-                first = (p * NC + core) * per
-                out[p, s * per:(s + 1) * per, :] = source[first:first + per, :]
-
-    for at in range(NX):
-        for core in range(NC):
-            pl.when((x == at) & (c == core))(functools.partial(fill, at, core))
-
-
-def flat_kernel(chunks, out):
+def take_rows(source, c, outs):
+    n = outs[0].shape[1]
+    count = outs[0].shape[0] * n
+    span = NC * count
+    per = n * len(outs) // NX
+    i = lax.broadcasted_iota(i32, (count, span), 0)
+    j = lax.broadcasted_iota(i32, (count, span), 1)
+    wanted = (i // per % (n // per)) * (span * len(outs) // NX) + (i // n * NC + c) * per + i % per
+    pick = (j == wanted).astype(bf16)
+    for h, out in enumerate(outs):
+        half = jnp.dot(
+            pick, source[h * span:(h + 1) * span, :], preferred_element_type=f32
+        ).astype(bf16)
+        for p in range(out.shape[0]):
+            out[p] = half[p * n:(p + 1) * n, :]
+
+
+def own_rows_kernel(text, *outs):
+    take_rows(text, 0, outs)
+
+
+def core_rows_kernel(place, received, keep, send, *outs):
+    @pl.when(place[3] == 0)
+    def _():
+        outs[0][...] = keep[...]
+        outs[1][...] = send[...]
+
+    @pl.when(place[3] != 0)
+    def _():
+        take_rows(received, 1, outs)
+
+
+def flat_kernel(place, chunks, out):
     n = chunks.shape[1]
-    for p in range(chunks.shape[0]):
-        out[p * n:(p + 1) * n, :] = chunks[p]
+    per = n // 2
+
+    def fill(core):
+        for x in range(NX):
+            for z in range(NZ):
+                for s in range(STEPS):
+                    held = s * (NX // STEPS)
+                    if x >= NX // 2:
+                        held = (held + (-1 if core else 1)) % NX
+                    first = x % (NX // 2) * per
+                    at = ((x * NZ + z) * STEPS + s) * per
+                    out[at:at + per, :] = chunks[held * NZ + z, first:first + per, :]
+
+    for core in range(NC):
+        pl.when(place[3] == core)(functools.partial(fill, core))
+
+
+def choose_kernel(place, keep, moved, out):
+    owner = place[0] % (NX // STEPS) == 0
+
+    @pl.when(owner)
+    def _():
+        out[...] = keep[...]
+
+    @pl.when(jnp.logical_not(owner))
+    def _():
+        out[...] = moved[...]
 
 
 def text_row(t, y, c, per):
@@ -146,9 +174,10 @@
     count = texts[0].shape[0]
     per = count // (PLANE * STEPS)
     held = (z == 0) & (y == 0) & (c == 0)
-    total = losses = None
-    for n in range(NY):
-        block = jnp.concatenate([texts[n][...], texts[NY + n][...]], axis=0)
+    losses = None
+    kept = []
+    blocks = [jnp.concatenate([texts[n][...], texts[NY + n][...]], axis=0) for n in range(NY)]
+    for n, block in enumerate(blocks):
         logits = scale * lax.dot_general(
             image[...], block, (((1,), (1,)), ((), ())), preferred_element_type=f32
         ) + bias
@@ -159,14 +188,14 @@
         positive = b == row
         e = jnp.exp(-jnp.abs(logits))
         signed = jnp.where(positive, -logits, logits)
-        part = jnp.sum(jnp.maximum(signed, 0.0) + jnp.log1p(e), axis=1)
+        part = jnp.maximum(signed, 0.0) + jnp.log1p(e)
         sigmoid = jnp.where(logits >= 0, 1.0, e) / (1.0 + e)
-        weights = (sigmoid - positive.astype(f32)).astype(bf16)
-        term = jnp.dot(weights, block, preferred_element_type=f32)
-        total = term if total is None else total + term
+        kept.append((sigmoid - positive.astype(f32)).astype(bf16))
         losses = part if losses is None else losses + part
+    weights = jnp.concatenate(kept, axis=1)
+    total = jnp.dot(weights, jnp.concatenate(blocks, axis=0), preferred_element_type=f32)
     grad[...] = scale * total
-    loss[...] = losses
+    loss[...] = jnp.sum(losses, axis=1)
 
 
 def local(image, text, log_scale, logit_bias):
@@ -175,57 +204,56 @@
     factors = jnp.concatenate([jnp.exp(log_scale), logit_bias])
     per = rows // (PLANE * NY * NC)
     count = PLANE * STEPS * per
-    side = NZ * NY * per
-
-    pieces = call(
-        slices_kernel,
-        [shaped(side * NC, width)] * NX,
-        (place, text),
-        in_specs=[SMEM, pl.BlockSpec(memory_space=pl.ANY)],
-        scratch_shapes=[pltpu.SemaphoreType.DMA((NX,))],
-    )
-    got = [pieces[0]] + [None] * (NX - 1)
-    for n in (2, 1, 3):
-        pairs = [
-            (device(x, 0, 0, 0), device((x + n) % NX, 0, 0, 0)) for x in range(0, NX, NX // STEPS)
-        ]
-        got[n] = lax.ppermute(pieces[n], AXES, pairs)
-    got += [lax.ppermute(a, "c", [(0, 1)]) for a in got]
-    joined = call(join_kernel, [shaped(NZ * NY, STEPS * per, width)], (place, *got))
-
-    images = [image, around(image, 1), around(image, -1)]
-    images.append(around(images[1], 1))
+
+    chunk = shaped(NZ * NY, STEPS * per, width)
+    received = lax.ppermute(text, "c", [(0, 1)])
+    own = call(own_rows_kernel, [chunk] * 2, (text,), scalars=0)
+    keep, send = call(core_rows_kernel, [chunk] * 2, (place, received, *own))
+    owners = range(0, NX, NX // STEPS)
+    pairs = [
+        (device(x, 0, 0, c), device((x + 1 - 2 * c) % NX, 0, 0, c)) for x in owners for c in range(NC)
+    ]
+    moved = lax.ppermute(send, AXES, pairs)
+    joined = call(choose_kernel, [chunk], (place, keep, moved))
+
+    images = [image, around(image, 1)]
+    again, images[1] = lax.optimization_barrier((image, images[1]))
+    images += [around(again, -1), around(images[1], 1)]
 
     spread = lax.all_to_all(joined, ("z", "y"), 0, 0, tiled=True)
     everywhere = jnp.broadcast_to(spread[:1], (PLANE, STEPS * per, width))
     everywhere, images[1] = lax.optimization_barrier((everywhere, images[1]))
     chunks = lax.all_to_all(everywhere, ("x", "z"), 0, 0, tiled=True)
-    texts = call(flat_kernel, [shaped(count, width)], (chunks,), scalars=0)
+    texts = call(
+        flat_kernel,
+        [shaped(count, width)],
+        (place, chunks),
+    )
 
     other = other_core(texts)
     turns = (0, NY - 1, 1, 2)
     flops = 4 * rows * NC * count * width
     early = call(
-        functools.partial(term_kernel, turns[:3]),
+        functools.partial(term_kernel, turns[:2]),
         [shaped(NC * count, width, dtype=f32)],
-        (place, factors, texts, other, *images[:3]),
-        flops=3 * flops,
+        (place, factors, texts, other, *images[:2]),
+        flops=2 * flops,
         scalars=2,
     )
     mine, theirs = call(
-        functools.partial(term_kernel, turns[3:]),
+        functools.partial(term_kernel, turns[2:]),
         [shaped(count, width, dtype=f32), shaped(count, width)],
-        (place, factors, texts, other, *images[3:], early),
-        flops=flops,
+        (place, factors, texts, other, *images[2:], early),
+        flops=2 * flops,
         scalars=2,
     )
-    term = call(
-        add_kernel, [shaped(PLANE, STEPS * per, width)], (mine, other_core(theirs)), scalars=0
-    )
+    line = [texts] + [along_y(texts, n) for n in range(1, NY)]
+    passed = other_core(theirs)
+    passed, line[1], line[3] = lax.optimization_barrier((passed, line[1], line[3]))
+    term = call(add_kernel, [shaped(PLANE, STEPS * per, width)], (mine, passed), scalars=0)
     terms = lax.all_to_all(term, ("x", "z"), 0, 0, tiled=True)
     text_grad = call(sum_kernel, [shaped(STEPS, per, width, dtype=f32)], (factors, terms))
 
-    line = [texts] + [along_y(texts, n) for n in range(1, NY)]
     across = [other] + [other_core(a) for a in line[1:]]
     image_grad, row_loss = call(
         image_kernel,

time: 96.2 us -> 87.6 us (0.911)
  starting transfers between devices: 37.7 us -> 27.5 us
  blocking collectives: 17.9 us -> 19.9 us
    ppermute x7 -> x2, starting transfers between devices: 9.01 us -> 2.62 us  [the longest x1 1.81 us: local(): received = lax.ppermute(text, 'c', [(0, 1)])]
    all_to_all x1, starting transfers between devices: 8.18 us -> 4.62 us  [local(): terms = lax.all_to_all(term, ('x', 'z'), 0, 0, tiled=True)]
    all_to_all x1, blocking collectives: 17.9 us -> 19.9 us  [local(): chunks = lax.all_to_all(everywhere, ('x', 'z'), 0, 0, tiled=True)]
    ppermute x7 -> x2, waiting for transfers between devices: 1.16 us -> 0.01 us  [the longest x1 0.01 us: local(): received = lax.ppermute(text, 'c', [(0, 1)])]
    all_to_all x1, waiting for transfers between devices: 10.9 us -> 9.79 us  [local(): spread = lax.all_to_all(joined, ('z', 'y'), 0, 0, tiled=True)]
    pallas_call x8 -> x9, Pallas kernels: 17.5 us -> 17.7 us  [call(): pl.pallas_call(body, out_shape=outs[0] if single else outs, in_specs=opti...]
  transfers between devices with their start and end apart: 20 -> 15, of which waited for: 8 -> 9; matrix products, arithmetic and copies ran while one was open for 0% -> 0% of each run, Pallas kernels for 15% -> 19%
where the time goes in v3:
time: 87.6 us; the launch traced here: 86.9 us
  starting transfers between devices  27.5 us (31%)
  blocking collectives  19.9 us (23%)
  waiting for transfers between devices  18.3 us (21%)
  Pallas kernels  17.7 us (20%)
  between operations  2.1 us (2%)
  local copies, waits for them, and re-layouts  1.36 us (2%)
    all_to_all x1, blocking collectives, local(): chunks = lax.all_to_all(everywhere, ('x', 'z'), 0, 0, tiled=True)  19.9 us
    pallas_call x9, Pallas kernels, call(): pl.pallas_call(body, out_shape=outs[0] if single else outs, in_specs=opti...  17.7 us
    all_to_all x1, starting transfers between devices, local(): spread = lax.all_to_all(joined, ('z', 'y'), 0, 0, tiled=True)  11.1 us
    all_to_all x1, waiting for transfers between devices, local(): spread = lax.all_to_all(joined, ('z', 'y'), 0, 0, tiled=True)  9.79 us
    ppermute x3, starting transfers between devices, around(): return lax.ppermute(a, ('y', 'c'), pairs)  4.89 us
    all_to_all x1, starting transfers between devices, local(): terms = lax.all_to_all(term, ('x', 'z'), 0, 0, tiled=True)  4.62 us
    ppermute x3, waiting for transfers between devices, along_y(): return lax.ppermute(a, 'y', [(i, (i + shift) % NY) for i in range(NY)])  4.26 us
    ppermute x3, starting transfers between devices, along_y(): return lax.ppermute(a, 'y', [(i, (i + shift) % NY) for i in range(NY)])  3.57 us
  transfers between devices with their start and end apart: 15, of which 9 were waited for; matrix products, arithmetic and copies ran while one was open for 0% of the time, Pallas kernels for 19%

profile of v3, /device:TPU:32, one launch (start us, length us, event | category | flops | bytes accessed | tf_op | source)
XLA Modules:
  0.0 86.9 jit_solution(17854202727168189537)
XLA Ops:
  0.6 1.8 %collective-permute-start = (bf16[512,1152]{1,0:T(8,128)(2,1)}, bf16[512,1152]{1,0:T(8,128)(2,1)S(1)}, u32[]{:S(2)}, u32[]{:S(2)}) collective-permute-start(bf16[512,1152]{1,0:T(8,128)(2,1)} %text.1), channel_id=1, source_target_pairs={{0,1},{2,3},{4,5},{6,7},{8,9},{10,11},{12,13},{14,15},{16,17},{18,... | collective-permute-start | bytes 3538952 | tf_op jit(solution)/shard_map/ppermute | solution.py:209
  2.5 1.7 %collective-permute-start.2 = (bf16[512,1152]{1,0:T(8,128)(2,1)}, bf16[512,1152]{1,0:T(8,128)(2,1)}, u32[]{:S(2)}, u32[]{:S(2)}) collective-permute-start(bf16[512,1152]{1,0:T(8,128)(2,1)} %image.1), channel_id=1, source_target_pairs={{0,2},{1,7},{2,4},{3,1},{4,6},{5,3},{6,0},{7,5},{8,10},{9,15},{10,... | collective-permute-start | bytes 3538952 | tf_op jit(solution)/shard_map/ppermute | solution.py:27
  4.1 1.3 %copy-done = bf16[512,1152]{1,0:T(8,128)(2,1)S(1)} copy-done((bf16[512,1152]{1,0:T(8,128)(2,1)S(1)}, bf16[512,1152]{1,0:T(8,128)(2,1)}, u32[]{:S(2)}) %copy-start) | copy-done | bytes 1179672
  6.4 0.8 collective-permute-start.1
  7.3 1.3 %shard_map.69 = bf16[32,4,1152]{2,1,0:T(4,128)(2,1)} custom-call(s32[4]{0:T(128)S(1)} %pad_add_fusion.place, bf16[32,4,1152]{2,1,0:T(4,128)(2,1)S(1)} %get-tuple-element.20.keep, bf16[32,4,1152]{2,1,0:T(4,128)(2,1)S(1)} %collective-permute-done.1.moved), custom_call_target="tpu_custom_call" | custom-call | bytes 884752 | tf_op jit(solution)/shard_map/pallas_call | solution.py:41
  8.6 11.1 %all-to-all-start = ((bf16[32,4,1152]{2,1,0:T(4,128)(2,1)}), bf16[32,4,1152]{2,1,0:T(4,128)(2,1)S(1)}, u32[]{:S(2)}, u32[]{:S(2)}) async-start(bf16[32,4,1152]{2,1,0:T(4,128)(2,1)} %shard_map.69), calls=%async_computation | async-start | bytes 589824 | tf_op jit(solution)/shard_map/all_to_all | solution.py:223
  19.6 0.6 collective-permute-done.2.refs_1_
  20.3 0.9 %collective-permute-start.5 = (bf16[512,1152]{1,0:T(8,128)(2,1)}, bf16[512,1152]{1,0:T(8,128)(2,1)}, u32[]{:S(2)}, u32[]{:S(2)}) collective-permute-start(bf16[512,1152]{1,0:T(8,128)(2,1)} %collective-permute-done.2.refs_1_), channel_id=1, source_target_pairs={{0,2},{1,7},{2,4},{3,1},{4,6},{5,3},{6,0},{7,5},{8,10},{9,15},{10,... | collective-permute-start | bytes 3538952 | tf_op jit(solution)/shard_map/ppermute | solution.py:27
  21.2 2.3 %collective-permute-start.4 = (bf16[512,1152]{1,0:T(8,128)(2,1)S(1)}, bf16[512,1152]{1,0:T(8,128)(2,1)}, u32[]{:S(2)}, u32[]{:S(2)}) collective-permute-start(bf16[512,1152]{1,0:T(8,128)(2,1)S(1)} %copy-done.1), channel_id=1, source_target_pairs={{0,6},{1,3},{2,0},{3,5},{4,2},{5,7},{6,4},{7,1},{8,14},{9,11},{10,... | collective-permute-start | bytes 3538952 | tf_op jit(solution)/shard_map/ppermute | solution.py:27
  23.5 9.8 %all-to-all-done = bf16[32,4,1152]{2,1,0:T(4,128)(2,1)S(1)} async-done(((bf16[32,4,1152]{2,1,0:T(4,128)(2,1)}), bf16[32,4,1152]{2,1,0:T(4,128)(2,1)S(1)}, u32[]{:S(2)}, u32[]{:S(2)}) %all-to-all-start) | async-done | bytes 294944 | tf_op jit(solution)/shard_map/all_to_all | solution.py:223
  33.4 19.9 %all_to_all.15.chunks = bf16[32,4,1152]{2,1,0:T(4,128)(2,1)S(1)} all-to-all(bf16[32,4,1152]{2,1,0:T(4,128)(2,1)S(1)} %broadcast_in_dim.8), channel_id=1, replica_groups=mesh['x'=4,'z'=8,'y'=4,'c'=2] {'x','z'}, dimensions={0} | all-to-all | bytes 589824 | tf_op jit(solution)/shard_map/all_to_all | solution.py:226
  53.3 0.7 shard_map.70.own.refs_0_
  55.5 0.6 collective-permute-start.7
  56.1 2.6 %collective-permute-start.8 = (bf16[128,1152]{1,0:T(8,128)(2,1)S(1)}, bf16[128,1152]{1,0:T(8,128)(2,1)S(1)}, u32[]{:S(2)}, u32[]{:S(2)}) collective-permute-start(bf16[128,1152]{1,0:T(8,128)(2,1)S(1)} %shard_map.70.own.refs_0_), channel_id=1, source_target_pairs={{0,6},{2,0},{4,2},{6,4},{1,7},{3,1},{5,3},{7,5},{8,14},{10,8},{12,... | collective-permute-start | bytes 884744 | tf_op jit(solution)/shard_map/ppermute | solution.py:31
  58.7 3.1 %shard_map.71.refs_2_ = f32[256,1152]{1,0:T(8,128)S(1)} custom-call(s32[4]{0:T(128)S(1)} %pad_add_fusion.place, f32[2]{0:T(128)S(1)} %pad_maximum_fusion.factors, bf16[128,1152]{1,0:T(8,128)(2,1)S(1)} %shard_map.70.own.refs_0_, bf16[128,1152]{1,0:T(8,128)(2,1)S(1)} %collective-permute-done.3.other.refs_4_, bf16[512,1152]{1,0:T(8,128)(2,1)S(1)} %copy-done.1, ...), custom_call_target="tpu_custom_call" | custom-call | flops 1207959552 | bytes 4128792 | tf_op jit(solution)/shard_map/pallas_call | solution.py:41
  61.8 3.5 %shard_map.72 = (f32[128,1152]{1,0:T(8,128)S(1)}, bf16[128,1152]{1,0:T(8,128)(2,1)S(1)}) custom-call(s32[4]{0:T(128)S(1)} %pad_add_fusion.place, f32[2]{0:T(128)S(1)} %pad_maximum_fusion.factors, bf16[128,1152]{1,0:T(8,128)(2,1)S(1)} %shard_map.70.own.refs_0_, bf16[128,1152]{1,0:T(8,128)(2,1)S(1)} %collective-permute-done.3.other.refs_4_, ...), custom_call_target="tpu_custom_call" | custom-call | flops 1207959552 | bytes 5013528 | tf_op jit(solution)/shard_map/pallas_call | solution.py:41
  66.1 0.9 %collective-permute-done.6.received = bf16[128,1152]{1,0:T(8,128)(2,1)S(1)} collective-permute-done((bf16[128,1152]{1,0:T(8,128)(2,1)S(1)}, bf16[128,1152]{1,0:T(8,128)(2,1)S(1)}, u32[]{:S(2)}, u32[]{:S(2)}) %collective-permute-start.6) | collective-permute-done | bytes 294944 | tf_op jit(solution)/shard_map/ppermute | solution.py:35
  67.0 0.8 shard_map.74
  67.8 4.6 %all-to-all-start.2 = ((bf16[32,4,1152]{2,1,0:T(4,128)(2,1)}), bf16[32,4,1152]{2,1,0:T(4,128)(2,1)S(1)}, u32[]{:S(2)}, u32[]{:S(2)}) async-start(bf16[32,4,1152]{2,1,0:T(4,128)(2,1)} %shard_map.74), calls=%async_computation.2 | async-start | bytes 589824 | tf_op jit(solution)/shard_map/all_to_all | solution.py:254
  72.5 3.9 %collective-permute-done.9.refs_2_ = bf16[128,1152]{1,0:T(8,128)(2,1)S(1)} collective-permute-done((bf16[128,1152]{1,0:T(8,128)(2,1)S(1)}, bf16[128,1152]{1,0:T(8,128)(2,1)S(1)}, u32[]{:S(2)}, u32[]{:S(2)}) %collective-permute-start.9) | collective-permute-done | bytes 294944 | tf_op jit(solution)/shard_map/ppermute | solution.py:31
  76.9 1.1 %collective-permute-done.11.refs_6_ = bf16[128,1152]{1,0:T(8,128)(2,1)S(1)} collective-permute-done((bf16[128,1152]{1,0:T(8,128)(2,1)S(1)}, bf16[128,1152]{1,0:T(8,128)(2,1)S(1)}, u32[]{:S(2)}, u32[]{:S(2)}) %collective-permute-start.11) | collective-permute-done | bytes 294944 | tf_op jit(solution)/shard_map/ppermute | solution.py:35
  78.8 6.1 %shard_map.73 = (f32[512,1152]{1,0:T(8,128)}, f32[512]{0:T(512)}) custom-call(s32[4]{0:T(128)S(1)} %pad_add_fusion.place, f32[2]{0:T(128)S(1)} %pad_maximum_fusion.factors, bf16[512,1152]{1,0:T(8,128)(2,1)S(1)} %copy-done.1, bf16[128,1152]{1,0:T(8,128)(2,1)S(1)} %shard_map.70.own.refs_0_, bf16[128,1152]{1,0:T(8,128)(2,1)S(1)} %collective-permute-done.7.refs_1_, ...), custom_call_target="tpu_custom_call" | custom-call | flops 2415919104 | bytes 5900312 | tf_op jit(solution)/shard_map/pallas_call | solution.py:41
  85.0 0.7 all-to-all-done.2.terms
  85.7 1.2 %shard_map.75 = f32[2,2,1152]{2,1,0:T(2,128)} custom-call(f32[2]{0:T(128)S(1)} %pad_maximum_fusion.factors, bf16[32,4,1152]{2,1,0:T(4,128)(2,1)S(1)} %all-to-all-done.2.terms), custom_call_target="tpu_custom_call" | custom-call | bytes 313352 | tf_op jit(solution)/shard_map/pallas_call | solution.py:41
  (24 shorter events, 3.4 us)
Async XLA Ops:
  0.6 5.2 %collective-permute-start = (bf16[512,1152]{1,0:T(8,128)(2,1)}, bf16[512,1152]{1,0:T(8,128)(2,1)S(1)}, u32[]{:S(2)}, u32[]{:S(2)}) collective-permute-start(bf16[512,1152]{1,0:T(8,128)(2,1)} %text.1), channel_id=1, source_target_pairs={{0,1},{2,3},{4,5},{6,7},{8,9},{10,11},{12,13},{14,15},{16,17},{18,... | collective-permute-start | bytes 3538952 | tf_op jit(solution)/shard_map/ppermute | solution.py:209
  2.5 17.8 %collective-permute-start.2 = (bf16[512,1152]{1,0:T(8,128)(2,1)}, bf16[512,1152]{1,0:T(8,128)(2,1)}, u32[]{:S(2)}, u32[]{:S(2)}) collective-permute-start(bf16[512,1152]{1,0:T(8,128)(2,1)} %image.1), channel_id=1, source_target_pairs={{0,2},{1,7},{2,4},{3,1},{4,6},{5,3},{6,0},{7,5},{8,10},{9,15},{10,... | collective-permute-start | bytes 3538952 | tf_op jit(solution)/shard_map/ppermute | solution.py:27
  4.1 1.3 %copy-start = (bf16[512,1152]{1,0:T(8,128)(2,1)S(1)}, bf16[512,1152]{1,0:T(8,128)(2,1)}, u32[]{:S(2)}) copy-start(bf16[512,1152]{1,0:T(8,128)(2,1)} %text.1) | copy-start | bytes 3538948
  6.4 14.8 %copy-start.1 = (bf16[512,1152]{1,0:T(8,128)(2,1)S(1)}, bf16[512,1152]{1,0:T(8,128)(2,1)}, u32[]{:S(2)}) copy-start(bf16[512,1152]{1,0:T(8,128)(2,1)} %image.1) | copy-start | bytes 3538948
  6.4 0.8 collective-permute-start.1
  8.6 24.7 %all-to-all-start = ((bf16[32,4,1152]{2,1,0:T(4,128)(2,1)}), bf16[32,4,1152]{2,1,0:T(4,128)(2,1)S(1)}, u32[]{:S(2)}, u32[]{:S(2)}) async-start(bf16[32,4,1152]{2,1,0:T(4,128)(2,1)} %shard_map.69), calls=%async_computation | async-start | bytes 589824 | tf_op jit(solution)/shard_map/all_to_all | solution.py:223
  20.3 41.5 %collective-permute-start.5 = (bf16[512,1152]{1,0:T(8,128)(2,1)}, bf16[512,1152]{1,0:T(8,128)(2,1)}, u32[]{:S(2)}, u32[]{:S(2)}) collective-permute-start(bf16[512,1152]{1,0:T(8,128)(2,1)} %collective-permute-done.2.refs_1_), channel_id=1, source_target_pairs={{0,2},{1,7},{2,4},{3,1},{4,6},{5,3},{6,0},{7,5},{8,10},{9,15},{10,... | collective-permute-start | bytes 3538952 | tf_op jit(solution)/shard_map/ppermute | solution.py:27
  21.2 40.6 %collective-permute-start.4 = (bf16[512,1152]{1,0:T(8,128)(2,1)S(1)}, bf16[512,1152]{1,0:T(8,128)(2,1)}, u32[]{:S(2)}, u32[]{:S(2)}) collective-permute-start(bf16[512,1152]{1,0:T(8,128)(2,1)S(1)} %copy-done.1), channel_id=1, source_target_pairs={{0,6},{1,3},{2,0},{3,5},{4,2},{5,7},{6,4},{7,1},{8,14},{9,11},{10,... | collective-permute-start | bytes 3538952 | tf_op jit(solution)/shard_map/ppermute | solution.py:27
  54.0 4.8 %collective-permute-start.3 = (bf16[128,1152]{1,0:T(8,128)(2,1)S(1)}, bf16[128,1152]{1,0:T(8,128)(2,1)S(1)}, u32[]{:S(2)}, u32[]{:S(2)}) collective-permute-start(bf16[128,1152]{1,0:T(8,128)(2,1)S(1)} %shard_map.70.own.refs_0_), channel_id=1, source_target_pairs={{0,1},{1,0},{2,3},{3,2},{4,5},{5,4},{6,7},{7,6},{8,9},{9,8},{10,11... | collective-permute-start | bytes 884744 | tf_op jit(solution)/shard_map/ppermute | solution.py:35
  55.5 10.6 %collective-permute-start.7 = (bf16[128,1152]{1,0:T(8,128)(2,1)S(1)}, bf16[128,1152]{1,0:T(8,128)(2,1)S(1)}, u32[]{:S(2)}, u32[]{:S(2)}) collective-permute-start(bf16[128,1152]{1,0:T(8,128)(2,1)S(1)} %shard_map.70.own.refs_0_), channel_id=1, source_target_pairs={{0,2},{2,4},{4,6},{6,0},{1,3},{3,5},{5,7},{7,1},{8,10},{10,12},{12... | collective-permute-start | bytes 884744 | tf_op jit(solution)/shard_map/ppermute | solution.py:31
  56.1 10.0 %collective-permute-start.8 = (bf16[128,1152]{1,0:T(8,128)(2,1)S(1)}, bf16[128,1152]{1,0:T(8,128)(2,1)S(1)}, u32[]{:S(2)}, u32[]{:S(2)}) collective-permute-start(bf16[128,1152]{1,0:T(8,128)(2,1)S(1)} %shard_map.70.own.refs_0_), channel_id=1, source_target_pairs={{0,6},{2,0},{4,2},{6,4},{1,7},{3,1},{5,3},{7,5},{8,14},{10,8},{12,... | collective-permute-start | bytes 884744 | tf_op jit(solution)/shard_map/ppermute | solution.py:31
  65.4 1.7 %collective-permute-start.6 = (bf16[128,1152]{1,0:T(8,128)(2,1)S(1)}, bf16[128,1152]{1,0:T(8,128)(2,1)S(1)}, u32[]{:S(2)}, u32[]{:S(2)}) collective-permute-start(bf16[128,1152]{1,0:T(8,128)(2,1)S(1)} %get-tuple-element.26), channel_id=1, source_target_pairs={{0,1},{1,0},{2,3},{3,2},{4,5},{5,4},{6,7},{7,6},{8,9},{9,8},{10,11... | collective-permute-start | bytes 884744 | tf_op jit(solution)/shard_map/ppermute | solution.py:35
  65.5 10.9 %collective-permute-start.9 = (bf16[128,1152]{1,0:T(8,128)(2,1)S(1)}, bf16[128,1152]{1,0:T(8,128)(2,1)S(1)}, u32[]{:S(2)}, u32[]{:S(2)}) collective-permute-start(bf16[128,1152]{1,0:T(8,128)(2,1)S(1)} %shard_map.70.own.refs_0_), channel_id=1, source_target_pairs={{0,4},{2,6},{4,0},{6,2},{1,5},{3,7},{5,1},{7,3},{8,12},{10,14},{12... | collective-permute-start | bytes 884744 | tf_op jit(solution)/shard_map/ppermute | solution.py:31
  67.8 17.9 %all-to-all-start.2 = ((bf16[32,4,1152]{2,1,0:T(4,128)(2,1)}), bf16[32,4,1152]{2,1,0:T(4,128)(2,1)S(1)}, u32[]{:S(2)}, u32[]{:S(2)}) async-start(bf16[32,4,1152]{2,1,0:T(4,128)(2,1)} %shard_map.74), calls=%async_computation.2 | async-start | bytes 589824 | tf_op jit(solution)/shard_map/all_to_all | solution.py:254
  76.4 1.6 %collective-permute-start.11 = (bf16[128,1152]{1,0:T(8,128)(2,1)S(1)}, bf16[128,1152]{1,0:T(8,128)(2,1)S(1)}, u32[]{:S(2)}, u32[]{:S(2)}) collective-permute-start(bf16[128,1152]{1,0:T(8,128)(2,1)S(1)} %collective-permute-done.9.refs_2_), channel_id=1, source_target_pairs={{0,1},{1,0},{2,3},{3,2},{4,5},{5,4},{6,7},{7,6},{8,9},{9,8},{10,11... | collective-permute-start | bytes 884744 | tf_op jit(solution)/shard_map/ppermute | solution.py:35
  76.4 2.0 %collective-permute-start.10 = (bf16[128,1152]{1,0:T(8,128)(2,1)S(1)}, bf16[128,1152]{1,0:T(8,128)(2,1)S(1)}, u32[]{:S(2)}, u32[]{:S(2)}) collective-permute-start(bf16[128,1152]{1,0:T(8,128)(2,1)S(1)} %collective-permute-done.7.refs_1_), channel_id=1, source_target_pairs={{0,1},{1,0},{2,3},{3,2},{4,5},{5,4},{6,7},{7,6},{8,9},{9,8},{10,11... | collective-permute-start | bytes 884744 | tf_op jit(solution)/shard_map/ppermute | solution.py:35
  76.9 1.9 %collective-permute-start.12 = (bf16[128,1152]{1,0:T(8,128)(2,1)S(1)}, bf16[128,1152]{1,0:T(8,128)(2,1)S(1)}, u32[]{:S(2)}, u32[]{:S(2)}) collective-permute-start(bf16[128,1152]{1,0:T(8,128)(2,1)S(1)} %collective-permute-done.8.refs_3_), channel_id=1, source_target_pairs={{0,1},{1,0},{2,3},{3,2},{4,5},{5,4},{6,7},{7,6},{8,9},{9,8},{10,11... | collective-permute-start | bytes 884744 | tf_op jit(solution)/shard_map/ppermute | solution.py:35

commit v4 on v3

--- a/solution.py
+++ b/solution.py
@@ -22,13 +22,9 @@
 
 def around(a, way):
     pairs = [
-        (y * NC + c, (y + way * (1 - 2 * c)) % NY * NC + c) for y in range(NY) for c in range(NC)
+        (y * NC + c, (y + way * (2 * c - 1)) % NY * NC + c) for y in range(NY) for c in range(NC)
     ]
     return lax.ppermute(a, ("y", "c"), pairs)
-
-
-def along_y(a, shift):
-    return lax.ppermute(a, "y", [(i, (i + shift) % NY) for i in range(NY)])
 
 
 def other_core(a):
@@ -127,26 +123,23 @@
     count = own.shape[0]
     per = count // (PLANE * STEPS)
     block = jnp.concatenate([own[...], other[...]], axis=0)
-    last = len(rest) > 1
-    total = rest[0][...] if last else None
+    t = lax.broadcasted_iota(i32, (NC * count, 1), 0)
+    step, row = text_row(t % count, y, (c + t // count) % NC, per)
+    kept = []
     for image, turn in zip(images, turns, strict=True):
-        rows = image.shape[0]
         logits = scale * lax.dot_general(
             block, image[...], (((1,), (1,)), ((), ())), preferred_element_type=f32
         ) + bias
-        t = lax.broadcasted_iota(i32, (NC * count, 1), 0)
-        step, row = text_row(t % count, y, (c + t // count) % NC, per)
         held = (z == 0) & (c == 0) & ((y + turn) % NY == 0)
-        row = jnp.where(held & (step * (NX // STEPS) == x), row, -1)
-        b = lax.broadcasted_iota(i32, (NC * count, rows), 1)
-        weights = (jax.nn.sigmoid(logits) - (b == row).astype(f32)).astype(bf16)
+        mine = jnp.where(held & (step * (NX // STEPS) == x), row, -1)
+        b = lax.broadcasted_iota(i32, logits.shape, 1)
+        kept.append((jax.nn.sigmoid(logits) - (b == mine).astype(f32)).astype(bf16))
+    total = None
+    for weights, image in zip(kept, images, strict=True):
         term = jnp.dot(weights, image[...], preferred_element_type=f32)
         total = term if total is None else total + term
-    if last:
-        rest[1][...] = total[:count]
-        rest[2][...] = total[count:].astype(bf16)
-    else:
-        rest[0][...] = total
+    rest[0][...] = total[:count]
+    rest[1][...] = total[count:].astype(bf16)
 
 
 def add_kernel(mine, received, out):
@@ -166,36 +159,51 @@
         out[s] = total[s * per:(s + 1) * per, :]
 
 
-def image_kernel(place, factors, image, *refs):
-    *texts, grad, loss = refs
+def image_kernel(offsets, place, factors, image, *refs):
+    *texts, grad, loss, block = refs
     x, z, y, c = (place[n] for n in range(4))
     scale, bias = factors[0], factors[1]
     rows = image.shape[0]
     count = texts[0].shape[0]
     per = count // (PLANE * STEPS)
     held = (z == 0) & (y == 0) & (c == 0)
-    losses = None
-    kept = []
-    blocks = [jnp.concatenate([texts[n][...], texts[NY + n][...]], axis=0) for n in range(NY)]
-    for n, block in enumerate(blocks):
+    t = lax.broadcasted_iota(i32, (1, count), 1)
+    wanted = []
+    for n, (text, (turn, dc)) in enumerate(zip(texts, offsets, strict=True)):
+        dy = turn * (2 * c - 1)
+        block[n * count:(n + 1) * count, :] = text[...]
+        step, row = text_row(t, (y + dy + NY) % NY, (c + dc) % NC, per)
+        wanted.append(jnp.where(held & (step * (NX // STEPS) == x), row, -1))
+    row = jnp.concatenate(wanted, axis=1)
+
+    def fill(with_positives):
         logits = scale * lax.dot_general(
-            image[...], block, (((1,), (1,)), ((), ())), preferred_element_type=f32
+            image[...], block[...], (((1,), (1,)), ((), ())), preferred_element_type=f32
         ) + bias
-        t = lax.broadcasted_iota(i32, (1, NC * count), 1)
-        step, row = text_row(t % count, (y + NY - n) % NY, (c + t // count) % NC, per)
-        row = jnp.where(held & (step * (NX // STEPS) == x), row, -1)
-        b = lax.broadcasted_iota(i32, (rows, NC * count), 0)
-        positive = b == row
-        e = jnp.exp(-jnp.abs(logits))
-        signed = jnp.where(positive, -logits, logits)
-        part = jnp.maximum(signed, 0.0) + jnp.log1p(e)
-        sigmoid = jnp.where(logits >= 0, 1.0, e) / (1.0 + e)
-        kept.append((sigmoid - positive.astype(f32)).astype(bf16))
-        losses = part if losses is None else losses + part
-    weights = jnp.concatenate(kept, axis=1)
-    total = jnp.dot(weights, jnp.concatenate(blocks, axis=0), preferred_element_type=f32)
-    grad[...] = scale * total
-    loss[...] = jnp.sum(losses, axis=1)
+        e = jnp.exp(jnp.minimum(logits, -logits))
+        u = 1.0 + e
+        near = pl.reciprocal(u, approx=True)
+        r = near * (2.0 - u * near)
+        sigmoid = jnp.where(logits >= 0, r, e * r)
+        above = jnp.maximum(logits, 0.0)
+        if with_positives:
+            positive = lax.broadcasted_iota(i32, logits.shape, 0) == row
+            above = above - jnp.where(positive, logits, 0.0)
+            sigmoid = sigmoid - positive.astype(f32)
+        s = e
+        while s.shape[1] > 128:
+            half = s.shape[1] // 2
+            s = s[:, :half] + s[:, half:] + s[:, :half] * s[:, half:]
+            above = above[:, :half] + above[:, half:]
+        u = 1.0 + s
+        log1p = jnp.log(u) + (s - (u - 1.0)) / u
+        loss[...] = jnp.sum(above + log1p, axis=1)
+        grad[...] = scale * jnp.dot(
+            sigmoid.astype(bf16), block[...], preferred_element_type=f32
+        )
+
+    pl.when(held)(lambda: fill(True))
+    pl.when(jnp.logical_not(held))(lambda: fill(False))
 
 
 def local(image, text, log_scale, logit_bias):
@@ -231,36 +239,32 @@
     )
 
     other = other_core(texts)
-    turns = (0, NY - 1, 1, 2)
+    turns = (0, 1, NY - 1, 2)
     flops = 4 * rows * NC * count * width
-    early = call(
-        functools.partial(term_kernel, turns[:2]),
-        [shaped(NC * count, width, dtype=f32)],
-        (place, factors, texts, other, *images[:2]),
-        flops=2 * flops,
+    mine, theirs = call(
+        functools.partial(term_kernel, turns),
+        [shaped(count, width, dtype=f32), shaped(count, width)],
+        (place, factors, texts, other, *images),
+        flops=4 * flops,
         scalars=2,
     )
-    mine, theirs = call(
-        functools.partial(term_kernel, turns[2:]),
-        [shaped(count, width, dtype=f32), shaped(count, width)],
-        (place, factors, texts, other, *images[2:], early),
-        flops=2 * flops,
-        scalars=2,
-    )
-    line = [texts] + [along_y(texts, n) for n in range(1, NY)]
+    line = [texts, around(texts, 1), around(texts, -1)]
+    line.append(around(line[1], 1))
     passed = other_core(theirs)
-    passed, line[1], line[3] = lax.optimization_barrier((passed, line[1], line[3]))
+    passed, line[1], line[2] = lax.optimization_barrier((passed, line[1], line[2]))
     term = call(add_kernel, [shaped(PLANE, STEPS * per, width)], (mine, passed), scalars=0)
     terms = lax.all_to_all(term, ("x", "z"), 0, 0, tiled=True)
     text_grad = call(sum_kernel, [shaped(STEPS, per, width, dtype=f32)], (factors, terms))
 
     across = [other] + [other_core(a) for a in line[1:]]
+    offsets = [(0, 0), (-1, 0), (1, 0), (2, 0), (0, 1), (1, 1), (-1, 1), (2, 1)]
     image_grad, row_loss = call(
-        image_kernel,
+        functools.partial(image_kernel, offsets),
         [shaped(rows, width, dtype=f32), shaped(rows, dtype=f32)],
         (place, factors, image, *line, *across),
         flops=NY * flops,
         scalars=2,
+        scratch_shapes=[pltpu.VMEM((len(offsets) * count, width), bf16)],
     )
     return image_grad, text_grad, row_loss
 

time: 87.6 us -> 84.7 us (0.967)
  starting transfers between devices: 27.5 us -> 29.8 us
  blocking collectives: 19.9 us -> 17.8 us
  Pallas kernels: 17.7 us -> 15.7 us
  waiting for transfers between devices: 18.3 us -> 17.4 us
    ppermute x3 -> x6, starting transfers between devices: 4.89 us -> 9.15 us  [around(): return lax.ppermute(a, ('y', 'c'), pairs)]
    ppermute x3 -> x0, waiting for transfers between devices: 4.26 us -> none  [along_y(): return lax.ppermute(a, 'y', [(i, (i + shift) % NY) for i in range(NY)])]
    all_to_all x1, waiting for transfers between devices: 0.74 us -> 4.75 us  [local(): terms = lax.all_to_all(term, ('x', 'z'), 0, 0, tiled=True)]
    ppermute x3 -> x0, starting transfers between devices: 3.57 us -> none  [along_y(): return lax.ppermute(a, 'y', [(i, (i + shift) % NY) for i in range(NY)])]
    all_to_all x1, blocking collectives: 19.9 us -> 17.8 us  [local(): chunks = lax.all_to_all(everywhere, ('x', 'z'), 0, 0, tiled=True)]
    pallas_call x9 -> x8, Pallas kernels: 17.7 us -> 15.7 us  [call(): pl.pallas_call(body, out_shape=outs[0] if single else outs, in_specs=opti...]
    ppermute x5, starting transfers between devices: 0.7 us -> 2.2 us  [other_core(): return lax.ppermute(a, 'c', [(0, 1), (1, 0)])]
    ppermute x5, waiting for transfers between devices: 2.83 us -> 1.63 us  [other_core(): return lax.ppermute(a, 'c', [(0, 1), (1, 0)])]
  transfers between devices with their start and end apart: 15 -> 15, of which waited for: 9 -> 6; matrix products, arithmetic and copies ran while one was open for 0% -> 0% of each run, Pallas kernels for 19% -> 17%
where the time goes in v4:
time: 84.7 us; the launch traced here: 84.4 us
  starting transfers between devices  29.8 us (35%)
  blocking collectives  17.8 us (21%)
  waiting for transfers between devices  17.4 us (21%)
  Pallas kernels  15.7 us (19%)
  between operations  2.09 us (2%)
  local copies, waits for them, and re-layouts  1.36 us (2%)
    all_to_all x1, blocking collectives, local(): chunks = lax.all_to_all(everywhere, ('x', 'z'), 0, 0, tiled=True)  17.8 us
    pallas_call x8, Pallas kernels, call(): pl.pallas_call(body, out_shape=outs[0] if single else outs, in_specs=opti...  15.7 us
    all_to_all x1, starting transfers between devices, local(): spread = lax.all_to_all(joined, ('z', 'y'), 0, 0, tiled=True)  10.6 us
    all_to_all x1, waiting for transfers between devices, local(): spread = lax.all_to_all(joined, ('z', 'y'), 0, 0, tiled=True)  9.5 us
    ppermute x6, starting transfers between devices, around(): return lax.ppermute(a, ('y', 'c'), pairs)  9.15 us
    all_to_all x1, starting transfers between devices, local(): terms = lax.all_to_all(term, ('x', 'z'), 0, 0, tiled=True)  5.29 us
    all_to_all x1, waiting for transfers between devices, local(): terms = lax.all_to_all(term, ('x', 'z'), 0, 0, tiled=True)  4.75 us
    ppermute x5, starting transfers between devices, other_core(): return lax.ppermute(a, 'c', [(0, 1), (1, 0)])  2.2 us
  transfers between devices with their start and end apart: 15, of which 6 were waited for; matrix products, arithmetic and copies ran while one was open for 0% of the time, Pallas kernels for 17%

profile of v4, /device:TPU:32, one launch (start us, length us, event | category | flops | bytes accessed | tf_op | source)
XLA Modules:
  0.0 84.4 jit_solution(3713598794440827270)
XLA Ops:
  0.6 1.8 %collective-permute-start = (bf16[512,1152]{1,0:T(8,128)(2,1)}, bf16[512,1152]{1,0:T(8,128)(2,1)S(1)}, u32[]{:S(2)}, u32[]{:S(2)}) collective-permute-start(bf16[512,1152]{1,0:T(8,128)(2,1)} %text.1), channel_id=1, source_target_pairs={{0,1},{2,3},{4,5},{6,7},{8,9},{10,11},{12,13},{14,15},{16,17},{18,... | collective-permute-start | bytes 3538952 | tf_op jit(solution)/shard_map/ppermute | solution.py:217
  2.5 3.1 %collective-permute-start.2 = (bf16[512,1152]{1,0:T(8,128)(2,1)}, bf16[512,1152]{1,0:T(8,128)(2,1)}, u32[]{:S(2)}, u32[]{:S(2)}) collective-permute-start(bf16[512,1152]{1,0:T(8,128)(2,1)} %image.1), channel_id=1, source_target_pairs={{0,6},{1,3},{2,0},{3,5},{4,2},{5,7},{6,4},{7,1},{8,14},{9,11},{10,... | collective-permute-start | bytes 3538952 | tf_op jit(solution)/shard_map/ppermute | solution.py:27
  5.5 1.3 %copy-done = bf16[512,1152]{1,0:T(8,128)(2,1)S(1)} copy-done((bf16[512,1152]{1,0:T(8,128)(2,1)S(1)}, bf16[512,1152]{1,0:T(8,128)(2,1)}, u32[]{:S(2)}) %copy-start) | copy-done | bytes 1179672
  7.2 0.6 shard_map.68
  7.9 0.8 collective-permute-start.1
  8.7 1.3 %shard_map.69 = bf16[32,4,1152]{2,1,0:T(4,128)(2,1)} custom-call(s32[4]{0:T(128)S(1)} %pad_add_fusion.place, bf16[32,4,1152]{2,1,0:T(4,128)(2,1)S(1)} %get-tuple-element.20.keep, bf16[32,4,1152]{2,1,0:T(4,128)(2,1)S(1)} %collective-permute-done.1.moved), custom_call_target="tpu_custom_call" | custom-call | bytes 884752 | tf_op jit(solution)/shard_map/pallas_call | solution.py:37
  10.0 10.6 %all-to-all-start = ((bf16[32,4,1152]{2,1,0:T(4,128)(2,1)}), bf16[32,4,1152]{2,1,0:T(4,128)(2,1)S(1)}, u32[]{:S(2)}, u32[]{:S(2)}) async-start(bf16[32,4,1152]{2,1,0:T(4,128)(2,1)} %shard_map.69), calls=%async_computation | async-start | bytes 589824 | tf_op jit(solution)/shard_map/all_to_all | solution.py:231
  20.6 2.8 %collective-permute-start.5 = (bf16[512,1152]{1,0:T(8,128)(2,1)}, bf16[512,1152]{1,0:T(8,128)(2,1)}, u32[]{:S(2)}, u32[]{:S(2)}) collective-permute-start(bf16[512,1152]{1,0:T(8,128)(2,1)} %collective-permute-done.2.refs_1_), channel_id=1, source_target_pairs={{0,6},{1,3},{2,0},{3,5},{4,2},{5,7},{6,4},{7,1},{8,14},{9,11},{10,... | collective-permute-start | bytes 3538952 | tf_op jit(solution)/shard_map/ppermute | solution.py:27
  23.4 9.5 %all-to-all-done = bf16[32,4,1152]{2,1,0:T(4,128)(2,1)S(1)} async-done(((bf16[32,4,1152]{2,1,0:T(4,128)(2,1)}), bf16[32,4,1152]{2,1,0:T(4,128)(2,1)S(1)}, u32[]{:S(2)}, u32[]{:S(2)}) %all-to-all-start) | async-done | bytes 294944 | tf_op jit(solution)/shard_map/all_to_all | solution.py:231
  33.0 17.8 %all_to_all.15.chunks = bf16[32,4,1152]{2,1,0:T(4,128)(2,1)S(1)} all-to-all(bf16[32,4,1152]{2,1,0:T(4,128)(2,1)S(1)} %broadcast_in_dim.8), channel_id=1, replica_groups=mesh['x'=4,'z'=8,'y'=4,'c'=2] {'x','z'}, dimensions={0} | all-to-all | bytes 589824 | tf_op jit(solution)/shard_map/all_to_all | solution.py:234
  50.8 0.7 shard_map.70.own.refs_0_
  52.9 1.4 %collective-permute-start.7 = (bf16[128,1152]{1,0:T(8,128)(2,1)S(1)}, bf16[128,1152]{1,0:T(8,128)(2,1)S(1)}, u32[]{:S(2)}, u32[]{:S(2)}) collective-permute-start(bf16[128,1152]{1,0:T(8,128)(2,1)S(1)} %shard_map.70.own.refs_0_), channel_id=1, source_target_pairs={{0,6},{1,3},{2,0},{3,5},{4,2},{5,7},{6,4},{7,1},{8,14},{9,11},{10,... | collective-permute-start | bytes 884744 | tf_op jit(solution)/shard_map/ppermute | solution.py:27
  54.3 0.8 collective-permute-start.8
  55.1 5.0 %shard_map.71 = (f32[128,1152]{1,0:T(8,128)S(1)}, bf16[128,1152]{1,0:T(8,128)(2,1)S(1)}) custom-call(s32[4]{0:T(128)S(1)} %pad_add_fusion.place, f32[2]{0:T(128)S(1)} %pad_maximum_fusion.factors, bf16[128,1152]{1,0:T(8,128)(2,1)S(1)} %shard_map.70.own.refs_0_, bf16[128,1152]{1,0:T(8,128)(2,1)S(1)} %collective-permute-done.3.other.refs_4_, ...), custom_call_target="tpu_custom_call" | custom-call | flops 2415919104 | bytes 6193176 | tf_op jit(solution)/shard_map/pallas_call | solution.py:37
  60.1 1.2 %collective-permute-start.6 = (bf16[128,1152]{1,0:T(8,128)(2,1)S(1)}, bf16[128,1152]{1,0:T(8,128)(2,1)S(1)}, u32[]{:S(2)}, u32[]{:S(2)}) collective-permute-start(bf16[128,1152]{1,0:T(8,128)(2,1)S(1)} %get-tuple-element.26), channel_id=1, source_target_pairs={{0,1},{1,0},{2,3},{3,2},{4,5},{5,4},{6,7},{7,6},{8,9},{9,8},{10,11... | collective-permute-start | bytes 884744 | tf_op jit(solution)/shard_map/ppermute | solution.py:31
  61.3 1.5 %collective-permute-done.7.refs_1_ = bf16[128,1152]{1,0:T(8,128)(2,1)S(1)} collective-permute-done((bf16[128,1152]{1,0:T(8,128)(2,1)S(1)}, bf16[128,1152]{1,0:T(8,128)(2,1)S(1)}, u32[]{:S(2)}, u32[]{:S(2)}) %collective-permute-start.7) | collective-permute-done | bytes 294944 | tf_op jit(solution)/shard_map/ppermute | solution.py:27
  62.8 1.2 %collective-permute-start.9 = (bf16[128,1152]{1,0:T(8,128)(2,1)S(1)}, bf16[128,1152]{1,0:T(8,128)(2,1)S(1)}, u32[]{:S(2)}, u32[]{:S(2)}) collective-permute-start(bf16[128,1152]{1,0:T(8,128)(2,1)S(1)} %collective-permute-done.7.refs_1_), channel_id=1, source_target_pairs={{0,6},{1,3},{2,0},{3,5},{4,2},{5,7},{6,4},{7,1},{8,14},{9,11},{10,... | collective-permute-start | bytes 884744 | tf_op jit(solution)/shard_map/ppermute | solution.py:27
  64.0 0.8 shard_map.73
  64.8 5.3 %all-to-all-start.2 = ((bf16[32,4,1152]{2,1,0:T(4,128)(2,1)}), bf16[32,4,1152]{2,1,0:T(4,128)(2,1)S(1)}, u32[]{:S(2)}, u32[]{:S(2)}) async-start(bf16[32,4,1152]{2,1,0:T(4,128)(2,1)} %shard_map.73), calls=%async_computation.2 | async-start | bytes 589824 | tf_op jit(solution)/shard_map/all_to_all | solution.py:256
  70.2 0.5 collective-permute-start.11
  71.0 0.8 collective-permute-done.10.refs_5_
  72.6 5.8 %shard_map.72 = (f32[512,1152]{1,0:T(8,128)}, f32[512]{0:T(512)}) custom-call(s32[4]{0:T(128)S(1)} %pad_add_fusion.place, f32[2]{0:T(128)S(1)} %pad_maximum_fusion.factors, bf16[512,1152]{1,0:T(8,128)(2,1)S(1)} %copy-done.1, bf16[128,1152]{1,0:T(8,128)(2,1)S(1)} %shard_map.70.own.refs_0_, bf16[128,1152]{1,0:T(8,128)(2,1)S(1)} %collective-permute-done.7.refs_1_, ...), custom_call_target="tpu_custom_call" | custom-call | flops 2415919104 | bytes 5900312 | tf_op jit(solution)/shard_map/pallas_call | solution.py:37
  78.4 4.8 %all-to-all-done.2.terms = bf16[32,4,1152]{2,1,0:T(4,128)(2,1)S(1)} async-done(((bf16[32,4,1152]{2,1,0:T(4,128)(2,1)}), bf16[32,4,1152]{2,1,0:T(4,128)(2,1)S(1)}, u32[]{:S(2)}, u32[]{:S(2)}) %all-to-all-start.2) | async-done | bytes 294944 | tf_op jit(solution)/shard_map/all_to_all | solution.py:256
  83.1 1.2 %shard_map.74 = f32[2,2,1152]{2,1,0:T(2,128)} custom-call(f32[2]{0:T(128)S(1)} %pad_maximum_fusion.factors, bf16[32,4,1152]{2,1,0:T(4,128)(2,1)S(1)} %all-to-all-done.2.terms), custom_call_target="tpu_custom_call" | custom-call | bytes 313352 | tf_op jit(solution)/shard_map/pallas_call | solution.py:37
  (23 shorter events, 1.9 us)
Async XLA Ops:
  0.6 6.6 %collective-permute-start = (bf16[512,1152]{1,0:T(8,128)(2,1)}, bf16[512,1152]{1,0:T(8,128)(2,1)S(1)}, u32[]{:S(2)}, u32[]{:S(2)}) collective-permute-start(bf16[512,1152]{1,0:T(8,128)(2,1)} %text.1), channel_id=1, source_target_pairs={{0,1},{2,3},{4,5},{6,7},{8,9},{10,11},{12,13},{14,15},{16,17},{18,... | collective-permute-start | bytes 3538952 | tf_op jit(solution)/shard_map/ppermute | solution.py:217
  2.5 18.1 %collective-permute-start.2 = (bf16[512,1152]{1,0:T(8,128)(2,1)}, bf16[512,1152]{1,0:T(8,128)(2,1)}, u32[]{:S(2)}, u32[]{:S(2)}) collective-permute-start(bf16[512,1152]{1,0:T(8,128)(2,1)} %image.1), channel_id=1, source_target_pairs={{0,6},{1,3},{2,0},{3,5},{4,2},{5,7},{6,4},{7,1},{8,14},{9,11},{10,... | collective-permute-start | bytes 3538952 | tf_op jit(solution)/shard_map/ppermute | solution.py:27
  5.5 1.3 %copy-start = (bf16[512,1152]{1,0:T(8,128)(2,1)S(1)}, bf16[512,1152]{1,0:T(8,128)(2,1)}, u32[]{:S(2)}) copy-start(bf16[512,1152]{1,0:T(8,128)(2,1)} %text.1) | copy-start | bytes 3538948
  7.9 15.5 %copy-start.1 = (bf16[512,1152]{1,0:T(8,128)(2,1)S(1)}, bf16[512,1152]{1,0:T(8,128)(2,1)}, u32[]{:S(2)}) copy-start(bf16[512,1152]{1,0:T(8,128)(2,1)} %image.1) | copy-start | bytes 3538948
  7.9 0.8 collective-permute-start.1
  10.0 22.9 %all-to-all-start = ((bf16[32,4,1152]{2,1,0:T(4,128)(2,1)}), bf16[32,4,1152]{2,1,0:T(4,128)(2,1)S(1)}, u32[]{:S(2)}, u32[]{:S(2)}) async-start(bf16[32,4,1152]{2,1,0:T(4,128)(2,1)} %shard_map.69), calls=%async_computation | async-start | bytes 589824 | tf_op jit(solution)/shard_map/all_to_all | solution.py:231
  20.6 34.5 %collective-permute-start.5 = (bf16[512,1152]{1,0:T(8,128)(2,1)}, bf16[512,1152]{1,0:T(8,128)(2,1)}, u32[]{:S(2)}, u32[]{:S(2)}) collective-permute-start(bf16[512,1152]{1,0:T(8,128)(2,1)} %collective-permute-done.2.refs_1_), channel_id=1, source_target_pairs={{0,6},{1,3},{2,0},{3,5},{4,2},{5,7},{6,4},{7,1},{8,14},{9,11},{10,... | collective-permute-start | bytes 3538952 | tf_op jit(solution)/shard_map/ppermute | solution.py:27
  23.4 31.7 %collective-permute-start.4 = (bf16[512,1152]{1,0:T(8,128)(2,1)S(1)}, bf16[512,1152]{1,0:T(8,128)(2,1)}, u32[]{:S(2)}, u32[]{:S(2)}) collective-permute-start(bf16[512,1152]{1,0:T(8,128)(2,1)S(1)} %copy-done.1), channel_id=1, source_target_pairs={{0,2},{1,7},{2,4},{3,1},{4,6},{5,3},{6,0},{7,5},{8,10},{9,15},{10,... | collective-permute-start | bytes 3538952 | tf_op jit(solution)/shard_map/ppermute | solution.py:27
  51.5 3.6 %collective-permute-start.3 = (bf16[128,1152]{1,0:T(8,128)(2,1)S(1)}, bf16[128,1152]{1,0:T(8,128)(2,1)S(1)}, u32[]{:S(2)}, u32[]{:S(2)}) collective-permute-start(bf16[128,1152]{1,0:T(8,128)(2,1)S(1)} %shard_map.70.own.refs_0_), channel_id=1, source_target_pairs={{0,1},{1,0},{2,3},{3,2},{4,5},{5,4},{6,7},{7,6},{8,9},{9,8},{10,11... | collective-permute-start | bytes 884744 | tf_op jit(solution)/shard_map/ppermute | solution.py:31
  52.9 9.9 %collective-permute-start.7 = (bf16[128,1152]{1,0:T(8,128)(2,1)S(1)}, bf16[128,1152]{1,0:T(8,128)(2,1)S(1)}, u32[]{:S(2)}, u32[]{:S(2)}) collective-permute-start(bf16[128,1152]{1,0:T(8,128)(2,1)S(1)} %shard_map.70.own.refs_0_), channel_id=1, source_target_pairs={{0,6},{1,3},{2,0},{3,5},{4,2},{5,7},{6,4},{7,1},{8,14},{9,11},{10,... | collective-permute-start | bytes 884744 | tf_op jit(solution)/shard_map/ppermute | solution.py:27
  54.3 9.7 %collective-permute-start.8 = (bf16[128,1152]{1,0:T(8,128)(2,1)S(1)}, bf16[128,1152]{1,0:T(8,128)(2,1)S(1)}, u32[]{:S(2)}, u32[]{:S(2)}) collective-permute-start(bf16[128,1152]{1,0:T(8,128)(2,1)S(1)} %shard_map.70.own.refs_0_), channel_id=1, source_target_pairs={{0,2},{1,7},{2,4},{3,1},{4,6},{5,3},{6,0},{7,5},{8,10},{9,15},{10,... | collective-permute-start | bytes 884744 | tf_op jit(solution)/shard_map/ppermute | solution.py:27
  60.1 4.0 %collective-permute-start.6 = (bf16[128,1152]{1,0:T(8,128)(2,1)S(1)}, bf16[128,1152]{1,0:T(8,128)(2,1)S(1)}, u32[]{:S(2)}, u32[]{:S(2)}) collective-permute-start(bf16[128,1152]{1,0:T(8,128)(2,1)S(1)} %get-tuple-element.26), channel_id=1, source_target_pairs={{0,1},{1,0},{2,3},{3,2},{4,5},{5,4},{6,7},{7,6},{8,9},{9,8},{10,11... | collective-permute-start | bytes 884744 | tf_op jit(solution)/shard_map/ppermute | solution.py:31
  62.8 7.9 %collective-permute-start.9 = (bf16[128,1152]{1,0:T(8,128)(2,1)S(1)}, bf16[128,1152]{1,0:T(8,128)(2,1)S(1)}, u32[]{:S(2)}, u32[]{:S(2)}) collective-permute-start(bf16[128,1152]{1,0:T(8,128)(2,1)S(1)} %collective-permute-done.7.refs_1_), channel_id=1, source_target_pairs={{0,6},{1,3},{2,0},{3,5},{4,2},{5,7},{6,4},{7,1},{8,14},{9,11},{10,... | collective-permute-start | bytes 884744 | tf_op jit(solution)/shard_map/ppermute | solution.py:27
  64.8 18.3 %all-to-all-start.2 = ((bf16[32,4,1152]{2,1,0:T(4,128)(2,1)}), bf16[32,4,1152]{2,1,0:T(4,128)(2,1)S(1)}, u32[]{:S(2)}, u32[]{:S(2)}) async-start(bf16[32,4,1152]{2,1,0:T(4,128)(2,1)} %shard_map.73), calls=%async_computation.2 | async-start | bytes 589824 | tf_op jit(solution)/shard_map/all_to_all | solution.py:256
  70.1 1.7 %collective-permute-start.10 = (bf16[128,1152]{1,0:T(8,128)(2,1)S(1)}, bf16[128,1152]{1,0:T(8,128)(2,1)S(1)}, u32[]{:S(2)}, u32[]{:S(2)}) collective-permute-start(bf16[128,1152]{1,0:T(8,128)(2,1)S(1)} %collective-permute-done.7.refs_1_), channel_id=1, source_target_pairs={{0,1},{1,0},{2,3},{3,2},{4,5},{5,4},{6,7},{7,6},{8,9},{9,8},{10,11... | collective-permute-start | bytes 884744 | tf_op jit(solution)/shard_map/ppermute | solution.py:31
  70.2 2.0 %collective-permute-start.11 = (bf16[128,1152]{1,0:T(8,128)(2,1)S(1)}, bf16[128,1152]{1,0:T(8,128)(2,1)S(1)}, u32[]{:S(2)}, u32[]{:S(2)}) collective-permute-start(bf16[128,1152]{1,0:T(8,128)(2,1)S(1)} %collective-permute-done.8.refs_2_), channel_id=1, source_target_pairs={{0,1},{1,0},{2,3},{3,2},{4,5},{5,4},{6,7},{7,6},{8,9},{9,8},{10,11... | collective-permute-start | bytes 884744 | tf_op jit(solution)/shard_map/ppermute | solution.py:31
  70.7 1.9 %collective-permute-start.12 = (bf16[128,1152]{1,0:T(8,128)(2,1)S(1)}, bf16[128,1152]{1,0:T(8,128)(2,1)S(1)}, u32[]{:S(2)}, u32[]{:S(2)}) collective-permute-start(bf16[128,1152]{1,0:T(8,128)(2,1)S(1)} %collective-permute-done.9.refs_3_), channel_id=1, source_target_pairs={{0,1},{1,0},{2,3},{3,2},{4,5},{5,4},{6,7},{7,6},{8,9},{9,8},{10,11... | collective-permute-start | bytes 884744 | tf_op jit(solution)/shard_map/ppermute | solution.py:31

commit v5 on v4

--- a/solution.py
+++ b/solution.py
@@ -91,7 +91,7 @@
                 for s in range(STEPS):
                     held = s * (NX // STEPS)
                     if x >= NX // 2:
-                        held = (held + (-1 if core else 1)) % NX
+                        held = (held + (1 if core else -1)) % NX
                     first = x % (NX // 2) * per
                     at = ((x * NZ + z) * STEPS + s) * per
                     out[at:at + per, :] = chunks[held * NZ + z, first:first + per, :]
@@ -219,7 +219,7 @@
     keep, send = call(core_rows_kernel, [chunk] * 2, (place, received, *own))
     owners = range(0, NX, NX // STEPS)
     pairs = [
-        (device(x, 0, 0, c), device((x + 1 - 2 * c) % NX, 0, 0, c)) for x in owners for c in range(NC)
+        (device(x, 0, 0, c), device((x - 1 + 2 * c) % NX, 0, 0, c)) for x in owners for c in range(NC)
     ]
     moved = lax.ppermute(send, AXES, pairs)
     joined = call(choose_kernel, [chunk], (place, keep, moved))

time: 84.7 us -> 84 us (level)
  waiting for transfers between devices: 17.4 us -> 15.8 us
    all_to_all x1, starting transfers between devices: 10.6 us -> 11.9 us  [local(): spread = lax.all_to_all(joined, ('z', 'y'), 0, 0, tiled=True)]
    all_to_all x1, waiting for transfers between devices: 9.5 us -> 8.35 us  [local(): spread = lax.all_to_all(joined, ('z', 'y'), 0, 0, tiled=True)]
where the time goes in v5:
time: 84 us; the launch traced here: 83.6 us
  starting transfers between devices  30.6 us (36%)
  blocking collectives  18 us (21%)
  waiting for transfers between devices  15.8 us (19%)
  Pallas kernels  15.7 us (19%)
  between operations  2.09 us (2%)
  local copies, waits for them, and re-layouts  1.36 us (2%)
    all_to_all x1, blocking collectives, local(): chunks = lax.all_to_all(everywhere, ('x', 'z'), 0, 0, tiled=True)  18 us
    pallas_call x8, Pallas kernels, call(): pl.pallas_call(body, out_shape=outs[0] if single else outs, in_specs=opti...  15.7 us
    all_to_all x1, starting transfers between devices, local(): spread = lax.all_to_all(joined, ('z', 'y'), 0, 0, tiled=True)  11.9 us
    ppermute x6, starting transfers between devices, around(): return lax.ppermute(a, ('y', 'c'), pairs)  9.27 us
    all_to_all x1, waiting for transfers between devices, local(): spread = lax.all_to_all(joined, ('z', 'y'), 0, 0, tiled=True)  8.35 us
    all_to_all x1, starting transfers between devices, local(): terms = lax.all_to_all(term, ('x', 'z'), 0, 0, tiled=True)  4.6 us
    all_to_all x1, waiting for transfers between devices, local(): terms = lax.all_to_all(term, ('x', 'z'), 0, 0, tiled=True)  4.28 us
    ppermute x5, starting transfers between devices, other_core(): return lax.ppermute(a, 'c', [(0, 1), (1, 0)])  2.2 us
  transfers between devices with their start and end apart: 15, of which 6 were waited for; matrix products, arithmetic and copies ran while one was open for 0% of the time, Pallas kernels for 17%

profile of v5, /device:TPU:32, one launch (start us, length us, event | category | flops | bytes accessed | tf_op | source)
XLA Modules:
  0.0 83.6 jit_solution(13549570896090437581)
XLA Ops:
  0.6 1.8 %collective-permute-start = (bf16[512,1152]{1,0:T(8,128)(2,1)}, bf16[512,1152]{1,0:T(8,128)(2,1)S(1)}, u32[]{:S(2)}, u32[]{:S(2)}) collective-permute-start(bf16[512,1152]{1,0:T(8,128)(2,1)} %text.1), channel_id=1, source_target_pairs={{0,1},{2,3},{4,5},{6,7},{8,9},{10,11},{12,13},{14,15},{16,17},{18,... | collective-permute-start | bytes 3538952 | tf_op jit(solution)/shard_map/ppermute | solution.py:217
  2.5 3.1 %collective-permute-start.2 = (bf16[512,1152]{1,0:T(8,128)(2,1)}, bf16[512,1152]{1,0:T(8,128)(2,1)}, u32[]{:S(2)}, u32[]{:S(2)}) collective-permute-start(bf16[512,1152]{1,0:T(8,128)(2,1)} %image.1), channel_id=1, source_target_pairs={{0,6},{1,3},{2,0},{3,5},{4,2},{5,7},{6,4},{7,1},{8,14},{9,11},{10,... | collective-permute-start | bytes 3538952 | tf_op jit(solution)/shard_map/ppermute | solution.py:27
  5.5 1.3 %copy-done = bf16[512,1152]{1,0:T(8,128)(2,1)S(1)} copy-done((bf16[512,1152]{1,0:T(8,128)(2,1)S(1)}, bf16[512,1152]{1,0:T(8,128)(2,1)}, u32[]{:S(2)}) %copy-start) | copy-done | bytes 1179672
  7.2 0.6 shard_map.68
  7.9 0.8 collective-permute-start.1
  8.7 1.3 %shard_map.69 = bf16[32,4,1152]{2,1,0:T(4,128)(2,1)} custom-call(s32[4]{0:T(128)S(1)} %pad_add_fusion.place, bf16[32,4,1152]{2,1,0:T(4,128)(2,1)S(1)} %get-tuple-element.20.keep, bf16[32,4,1152]{2,1,0:T(4,128)(2,1)S(1)} %collective-permute-done.1.moved), custom_call_target="tpu_custom_call" | custom-call | bytes 884752 | tf_op jit(solution)/shard_map/pallas_call | solution.py:37
  10.0 11.9 %all-to-all-start = ((bf16[32,4,1152]{2,1,0:T(4,128)(2,1)}), bf16[32,4,1152]{2,1,0:T(4,128)(2,1)S(1)}, u32[]{:S(2)}, u32[]{:S(2)}) async-start(bf16[32,4,1152]{2,1,0:T(4,128)(2,1)} %shard_map.69), calls=%async_computation | async-start | bytes 589824 | tf_op jit(solution)/shard_map/all_to_all | solution.py:231
  21.9 2.8 %collective-permute-start.5 = (bf16[512,1152]{1,0:T(8,128)(2,1)}, bf16[512,1152]{1,0:T(8,128)(2,1)}, u32[]{:S(2)}, u32[]{:S(2)}) collective-permute-start(bf16[512,1152]{1,0:T(8,128)(2,1)} %collective-permute-done.2.refs_1_), channel_id=1, source_target_pairs={{0,6},{1,3},{2,0},{3,5},{4,2},{5,7},{6,4},{7,1},{8,14},{9,11},{10,... | collective-permute-start | bytes 3538952 | tf_op jit(solution)/shard_map/ppermute | solution.py:27
  24.6 8.4 %all-to-all-done = bf16[32,4,1152]{2,1,0:T(4,128)(2,1)S(1)} async-done(((bf16[32,4,1152]{2,1,0:T(4,128)(2,1)}), bf16[32,4,1152]{2,1,0:T(4,128)(2,1)S(1)}, u32[]{:S(2)}, u32[]{:S(2)}) %all-to-all-start) | async-done | bytes 294944 | tf_op jit(solution)/shard_map/all_to_all | solution.py:231
  33.1 18.0 %all_to_all.15.chunks = bf16[32,4,1152]{2,1,0:T(4,128)(2,1)S(1)} all-to-all(bf16[32,4,1152]{2,1,0:T(4,128)(2,1)S(1)} %broadcast_in_dim.8), channel_id=1, replica_groups=mesh['x'=4,'z'=8,'y'=4,'c'=2] {'x','z'}, dimensions={0} | all-to-all | bytes 589824 | tf_op jit(solution)/shard_map/all_to_all | solution.py:234
  51.1 0.7 shard_map.70.own.refs_0_
  53.2 1.4 %collective-permute-start.7 = (bf16[128,1152]{1,0:T(8,128)(2,1)S(1)}, bf16[128,1152]{1,0:T(8,128)(2,1)S(1)}, u32[]{:S(2)}, u32[]{:S(2)}) collective-permute-start(bf16[128,1152]{1,0:T(8,128)(2,1)S(1)} %shard_map.70.own.refs_0_), channel_id=1, source_target_pairs={{0,6},{1,3},{2,0},{3,5},{4,2},{5,7},{6,4},{7,1},{8,14},{9,11},{10,... | collective-permute-start | bytes 884744 | tf_op jit(solution)/shard_map/ppermute | solution.py:27
  54.7 0.7 collective-permute-start.8
  55.4 5.0 %shard_map.71 = (f32[128,1152]{1,0:T(8,128)S(1)}, bf16[128,1152]{1,0:T(8,128)(2,1)S(1)}) custom-call(s32[4]{0:T(128)S(1)} %pad_add_fusion.place, f32[2]{0:T(128)S(1)} %pad_maximum_fusion.factors, bf16[128,1152]{1,0:T(8,128)(2,1)S(1)} %shard_map.70.own.refs_0_, bf16[128,1152]{1,0:T(8,128)(2,1)S(1)} %collective-permute-done.3.other.refs_4_, ...), custom_call_target="tpu_custom_call" | custom-call | flops 2415919104 | bytes 6193176 | tf_op jit(solution)/shard_map/pallas_call | solution.py:37
  60.4 1.2 %collective-permute-start.6 = (bf16[128,1152]{1,0:T(8,128)(2,1)S(1)}, bf16[128,1152]{1,0:T(8,128)(2,1)S(1)}, u32[]{:S(2)}, u32[]{:S(2)}) collective-permute-start(bf16[128,1152]{1,0:T(8,128)(2,1)S(1)} %get-tuple-element.26), channel_id=1, source_target_pairs={{0,1},{1,0},{2,3},{3,2},{4,5},{5,4},{6,7},{7,6},{8,9},{9,8},{10,11... | collective-permute-start | bytes 884744 | tf_op jit(solution)/shard_map/ppermute | solution.py:31
  61.6 1.5 %collective-permute-done.7.refs_1_ = bf16[128,1152]{1,0:T(8,128)(2,1)S(1)} collective-permute-done((bf16[128,1152]{1,0:T(8,128)(2,1)S(1)}, bf16[128,1152]{1,0:T(8,128)(2,1)S(1)}, u32[]{:S(2)}, u32[]{:S(2)}) %collective-permute-start.7) | collective-permute-done | bytes 294944 | tf_op jit(solution)/shard_map/ppermute | solution.py:27
  63.1 1.3 %collective-permute-start.9 = (bf16[128,1152]{1,0:T(8,128)(2,1)S(1)}, bf16[128,1152]{1,0:T(8,128)(2,1)S(1)}, u32[]{:S(2)}, u32[]{:S(2)}) collective-permute-start(bf16[128,1152]{1,0:T(8,128)(2,1)S(1)} %collective-permute-done.7.refs_1_), channel_id=1, source_target_pairs={{0,6},{1,3},{2,0},{3,5},{4,2},{5,7},{6,4},{7,1},{8,14},{9,11},{10,... | collective-permute-start | bytes 884744 | tf_op jit(solution)/shard_map/ppermute | solution.py:27
  64.4 0.8 shard_map.73
  65.3 4.6 %all-to-all-start.2 = ((bf16[32,4,1152]{2,1,0:T(4,128)(2,1)}), bf16[32,4,1152]{2,1,0:T(4,128)(2,1)S(1)}, u32[]{:S(2)}, u32[]{:S(2)}) async-start(bf16[32,4,1152]{2,1,0:T(4,128)(2,1)} %shard_map.73), calls=%async_computation.2 | async-start | bytes 589824 | tf_op jit(solution)/shard_map/all_to_all | solution.py:256
  70.0 0.5 collective-permute-start.11
  70.7 0.8 collective-permute-done.10.refs_5_
  72.4 5.7 %shard_map.72 = (f32[512,1152]{1,0:T(8,128)}, f32[512]{0:T(512)}) custom-call(s32[4]{0:T(128)S(1)} %pad_add_fusion.place, f32[2]{0:T(128)S(1)} %pad_maximum_fusion.factors, bf16[512,1152]{1,0:T(8,128)(2,1)S(1)} %copy-done.1, bf16[128,1152]{1,0:T(8,128)(2,1)S(1)} %shard_map.70.own.refs_0_, bf16[128,1152]{1,0:T(8,128)(2,1)S(1)} %collective-permute-done.7.refs_1_, ...), custom_call_target="tpu_custom_call" | custom-call | flops 2415919104 | bytes 5900312 | tf_op jit(solution)/shard_map/pallas_call | solution.py:37
  78.1 4.3 %all-to-all-done.2.terms = bf16[32,4,1152]{2,1,0:T(4,128)(2,1)S(1)} async-done(((bf16[32,4,1152]{2,1,0:T(4,128)(2,1)}), bf16[32,4,1152]{2,1,0:T(4,128)(2,1)S(1)}, u32[]{:S(2)}, u32[]{:S(2)}) %all-to-all-start.2) | async-done | bytes 294944 | tf_op jit(solution)/shard_map/all_to_all | solution.py:256
  82.4 1.2 %shard_map.74 = f32[2,2,1152]{2,1,0:T(2,128)} custom-call(f32[2]{0:T(128)S(1)} %pad_maximum_fusion.factors, bf16[32,4,1152]{2,1,0:T(4,128)(2,1)S(1)} %all-to-all-done.2.terms), custom_call_target="tpu_custom_call" | custom-call | bytes 313352 | tf_op jit(solution)/shard_map/pallas_call | solution.py:37
  (23 shorter events, 1.9 us)
Async XLA Ops:
  0.6 6.6 %collective-permute-start = (bf16[512,1152]{1,0:T(8,128)(2,1)}, bf16[512,1152]{1,0:T(8,128)(2,1)S(1)}, u32[]{:S(2)}, u32[]{:S(2)}) collective-permute-start(bf16[512,1152]{1,0:T(8,128)(2,1)} %text.1), channel_id=1, source_target_pairs={{0,1},{2,3},{4,5},{6,7},{8,9},{10,11},{12,13},{14,15},{16,17},{18,... | collective-permute-start | bytes 3538952 | tf_op jit(solution)/shard_map/ppermute | solution.py:217
  2.5 19.4 %collective-permute-start.2 = (bf16[512,1152]{1,0:T(8,128)(2,1)}, bf16[512,1152]{1,0:T(8,128)(2,1)}, u32[]{:S(2)}, u32[]{:S(2)}) collective-permute-start(bf16[512,1152]{1,0:T(8,128)(2,1)} %image.1), channel_id=1, source_target_pairs={{0,6},{1,3},{2,0},{3,5},{4,2},{5,7},{6,4},{7,1},{8,14},{9,11},{10,... | collective-permute-start | bytes 3538952 | tf_op jit(solution)/shard_map/ppermute | solution.py:27
  5.5 1.3 %copy-start = (bf16[512,1152]{1,0:T(8,128)(2,1)S(1)}, bf16[512,1152]{1,0:T(8,128)(2,1)}, u32[]{:S(2)}) copy-start(bf16[512,1152]{1,0:T(8,128)(2,1)} %text.1) | copy-start | bytes 3538948
  7.9 16.8 %copy-start.1 = (bf16[512,1152]{1,0:T(8,128)(2,1)S(1)}, bf16[512,1152]{1,0:T(8,128)(2,1)}, u32[]{:S(2)}) copy-start(bf16[512,1152]{1,0:T(8,128)(2,1)} %image.1) | copy-start | bytes 3538948
  7.9 0.8 collective-permute-start.1
  10.0 23.0 %all-to-all-start = ((bf16[32,4,1152]{2,1,0:T(4,128)(2,1)}), bf16[32,4,1152]{2,1,0:T(4,128)(2,1)S(1)}, u32[]{:S(2)}, u32[]{:S(2)}) async-start(bf16[32,4,1152]{2,1,0:T(4,128)(2,1)} %shard_map.69), calls=%async_computation | async-start | bytes 589824 | tf_op jit(solution)/shard_map/all_to_all | solution.py:231
  21.9 33.5 %collective-permute-start.5 = (bf16[512,1152]{1,0:T(8,128)(2,1)}, bf16[512,1152]{1,0:T(8,128)(2,1)}, u32[]{:S(2)}, u32[]{:S(2)}) collective-permute-start(bf16[512,1152]{1,0:T(8,128)(2,1)} %collective-permute-done.2.refs_1_), channel_id=1, source_target_pairs={{0,6},{1,3},{2,0},{3,5},{4,2},{5,7},{6,4},{7,1},{8,14},{9,11},{10,... | collective-permute-start | bytes 3538952 | tf_op jit(solution)/shard_map/ppermute | solution.py:27
  24.6 30.8 %collective-permute-start.4 = (bf16[512,1152]{1,0:T(8,128)(2,1)S(1)}, bf16[512,1152]{1,0:T(8,128)(2,1)}, u32[]{:S(2)}, u32[]{:S(2)}) collective-permute-start(bf16[512,1152]{1,0:T(8,128)(2,1)S(1)} %copy-done.1), channel_id=1, source_target_pairs={{0,2},{1,7},{2,4},{3,1},{4,6},{5,3},{6,0},{7,5},{8,10},{9,15},{10,... | collective-permute-start | bytes 3538952 | tf_op jit(solution)/shard_map/ppermute | solution.py:27
  51.8 3.6 %collective-permute-start.3 = (bf16[128,1152]{1,0:T(8,128)(2,1)S(1)}, bf16[128,1152]{1,0:T(8,128)(2,1)S(1)}, u32[]{:S(2)}, u32[]{:S(2)}) collective-permute-start(bf16[128,1152]{1,0:T(8,128)(2,1)S(1)} %shard_map.70.own.refs_0_), channel_id=1, source_target_pairs={{0,1},{1,0},{2,3},{3,2},{4,5},{5,4},{6,7},{7,6},{8,9},{9,8},{10,11... | collective-permute-start | bytes 884744 | tf_op jit(solution)/shard_map/ppermute | solution.py:31
  53.2 9.9 %collective-permute-start.7 = (bf16[128,1152]{1,0:T(8,128)(2,1)S(1)}, bf16[128,1152]{1,0:T(8,128)(2,1)S(1)}, u32[]{:S(2)}, u32[]{:S(2)}) collective-permute-start(bf16[128,1152]{1,0:T(8,128)(2,1)S(1)} %shard_map.70.own.refs_0_), channel_id=1, source_target_pairs={{0,6},{1,3},{2,0},{3,5},{4,2},{5,7},{6,4},{7,1},{8,14},{9,11},{10,... | collective-permute-start | bytes 884744 | tf_op jit(solution)/shard_map/ppermute | solution.py:27
  54.7 9.8 %collective-permute-start.8 = (bf16[128,1152]{1,0:T(8,128)(2,1)S(1)}, bf16[128,1152]{1,0:T(8,128)(2,1)S(1)}, u32[]{:S(2)}, u32[]{:S(2)}) collective-permute-start(bf16[128,1152]{1,0:T(8,128)(2,1)S(1)} %shard_map.70.own.refs_0_), channel_id=1, source_target_pairs={{0,2},{1,7},{2,4},{3,1},{4,6},{5,3},{6,0},{7,5},{8,10},{9,15},{10,... | collective-permute-start | bytes 884744 | tf_op jit(solution)/shard_map/ppermute | solution.py:27
  60.4 4.1 %collective-permute-start.6 = (bf16[128,1152]{1,0:T(8,128)(2,1)S(1)}, bf16[128,1152]{1,0:T(8,128)(2,1)S(1)}, u32[]{:S(2)}, u32[]{:S(2)}) collective-permute-start(bf16[128,1152]{1,0:T(8,128)(2,1)S(1)} %get-tuple-element.26), channel_id=1, source_target_pairs={{0,1},{1,0},{2,3},{3,2},{4,5},{5,4},{6,7},{7,6},{8,9},{9,8},{10,11... | collective-permute-start | bytes 884744 | tf_op jit(solution)/shard_map/ppermute | solution.py:31
  63.1 7.3 %collective-permute-start.9 = (bf16[128,1152]{1,0:T(8,128)(2,1)S(1)}, bf16[128,1152]{1,0:T(8,128)(2,1)S(1)}, u32[]{:S(2)}, u32[]{:S(2)}) collective-permute-start(bf16[128,1152]{1,0:T(8,128)(2,1)S(1)} %collective-permute-done.7.refs_1_), channel_id=1, source_target_pairs={{0,6},{1,3},{2,0},{3,5},{4,2},{5,7},{6,4},{7,1},{8,14},{9,11},{10,... | collective-permute-start | bytes 884744 | tf_op jit(solution)/shard_map/ppermute | solution.py:27
  65.3 17.1 %all-to-all-start.2 = ((bf16[32,4,1152]{2,1,0:T(4,128)(2,1)}), bf16[32,4,1152]{2,1,0:T(4,128)(2,1)S(1)}, u32[]{:S(2)}, u32[]{:S(2)}) async-start(bf16[32,4,1152]{2,1,0:T(4,128)(2,1)} %shard_map.73), calls=%async_computation.2 | async-start | bytes 589824 | tf_op jit(solution)/shard_map/all_to_all | solution.py:256
  69.9 1.7 %collective-permute-start.10 = (bf16[128,1152]{1,0:T(8,128)(2,1)S(1)}, bf16[128,1152]{1,0:T(8,128)(2,1)S(1)}, u32[]{:S(2)}, u32[]{:S(2)}) collective-permute-start(bf16[128,1152]{1,0:T(8,128)(2,1)S(1)} %collective-permute-done.7.refs_1_), channel_id=1, source_target_pairs={{0,1},{1,0},{2,3},{3,2},{4,5},{5,4},{6,7},{7,6},{8,9},{9,8},{10,11... | collective-permute-start | bytes 884744 | tf_op jit(solution)/shard_map/ppermute | solution.py:31
  70.0 2.0 %collective-permute-start.11 = (bf16[128,1152]{1,0:T(8,128)(2,1)S(1)}, bf16[128,1152]{1,0:T(8,128)(2,1)S(1)}, u32[]{:S(2)}, u32[]{:S(2)}) collective-permute-start(bf16[128,1152]{1,0:T(8,128)(2,1)S(1)} %collective-permute-done.8.refs_2_), channel_id=1, source_target_pairs={{0,1},{1,0},{2,3},{3,2},{4,5},{5,4},{6,7},{7,6},{8,9},{9,8},{10,11... | collective-permute-start | bytes 884744 | tf_op jit(solution)/shard_map/ppermute | solution.py:31
  70.5 1.9 %collective-permute-start.12 = (bf16[128,1152]{1,0:T(8,128)(2,1)S(1)}, bf16[128,1152]{1,0:T(8,128)(2,1)S(1)}, u32[]{:S(2)}, u32[]{:S(2)}) collective-permute-start(bf16[128,1152]{1,0:T(8,128)(2,1)S(1)} %collective-permute-done.9.refs_3_), channel_id=1, source_target_pairs={{0,1},{1,0},{2,3},{3,2},{4,5},{5,4},{6,7},{7,6},{8,9},{9,8},{10,11... | collective-permute-start | bytes 884744 | tf_op jit(solution)/shard_map/ppermute | solution.py:31

commit v6 on v5

--- a/solution.py
+++ b/solution.py
@@ -133,7 +133,11 @@
         held = (z == 0) & (c == 0) & ((y + turn) % NY == 0)
         mine = jnp.where(held & (step * (NX // STEPS) == x), row, -1)
         b = lax.broadcasted_iota(i32, logits.shape, 1)
-        kept.append((jax.nn.sigmoid(logits) - (b == mine).astype(f32)).astype(bf16))
+        e = jnp.exp(jnp.minimum(logits, -logits))
+        near = pl.reciprocal(1.0 + e, approx=True)
+        r = near * (2.0 - (1.0 + e) * near)
+        sigmoid = jnp.where(logits >= 0, r, e * r)
+        kept.append((sigmoid - (b == mine).astype(f32)).astype(bf16))
     total = None
     for weights, image in zip(kept, images, strict=True):
         term = jnp.dot(weights, image[...], preferred_element_type=f32)
@@ -214,10 +218,12 @@
     count = PLANE * STEPS * per
 
     chunk = shaped(NZ * NY, STEPS * per, width)
-    received = lax.ppermute(text, "c", [(0, 1)])
+    owners = range(0, NX, NX // STEPS)
+    received = lax.ppermute(
+        text, AXES, [(device(x, 0, 0, 0), device(x, 0, 0, 1)) for x in owners]
+    )
     own = call(own_rows_kernel, [chunk] * 2, (text,), scalars=0)
     keep, send = call(core_rows_kernel, [chunk] * 2, (place, received, *own))
-    owners = range(0, NX, NX // STEPS)
     pairs = [
         (device(x, 0, 0, c), device((x - 1 + 2 * c) % NX, 0, 0, c)) for x in owners for c in range(NC)
     ]

time: 84 us -> 83.1 us (0.989)
    ppermute x1, starting transfers between devices: 1.81 us -> 0.74 us  [local(): lax.ppermute(text, AXES, [(device(x, 0, 0, 0), device(x, 0, 0, 1)) for x...]
  transfers between devices with their start and end apart: 15 -> 15, of which waited for: 6 -> 6; matrix products, arithmetic and copies ran while one was open for 0% -> 0% of each run, Pallas kernels for 17% -> 18%
where the time goes in v6:
time: 83.1 us; the launch traced here: 82.7 us
  starting transfers between devices  29.9 us (36%)
  blocking collectives  18.1 us (22%)
  Pallas kernels  15.9 us (19%)
  waiting for transfers between devices  15.2 us (18%)
  between operations  2.1 us (3%)
  local copies, waits for them, and re-layouts  1.36 us (2%)
    all_to_all x1, blocking collectives, local(): chunks = lax.all_to_all(everywhere, ('x', 'z'), 0, 0, tiled=True)  18.1 us
    pallas_call x8, Pallas kernels, call(): pl.pallas_call(body, out_shape=outs[0] if single else outs, in_specs=opti...  15.9 us
    all_to_all x1, starting transfers between devices, local(): spread = lax.all_to_all(joined, ('z', 'y'), 0, 0, tiled=True)  11.8 us
    ppermute x6, starting transfers between devices, around(): return lax.ppermute(a, ('y', 'c'), pairs)  8.93 us
    all_to_all x1, waiting for transfers between devices, local(): spread = lax.all_to_all(joined, ('z', 'y'), 0, 0, tiled=True)  8.39 us
    all_to_all x1, starting transfers between devices, local(): terms = lax.all_to_all(term, ('x', 'z'), 0, 0, tiled=True)  5.37 us
    all_to_all x1, waiting for transfers between devices, local(): terms = lax.all_to_all(term, ('x', 'z'), 0, 0, tiled=True)  4.03 us
    ppermute x5, starting transfers between devices, other_core(): return lax.ppermute(a, 'c', [(0, 1), (1, 0)])  2.2 us
  transfers between devices with their start and end apart: 15, of which 6 were waited for; matrix products, arithmetic and copies ran while one was open for 0% of the time, Pallas kernels for 18%

profile of v6, /device:TPU:32, one launch (start us, length us, event | category | flops | bytes accessed | tf_op | source)
XLA Modules:
  0.0 82.7 jit_solution(1890230888054306183)
XLA Ops:
  0.6 0.7 collective-permute-start
  1.4 3.1 %collective-permute-start.2 = (bf16[512,1152]{1,0:T(8,128)(2,1)}, bf16[512,1152]{1,0:T(8,128)(2,1)}, u32[]{:S(2)}, u32[]{:S(2)}) collective-permute-start(bf16[512,1152]{1,0:T(8,128)(2,1)} %image.1), channel_id=1, source_target_pairs={{0,6},{1,3},{2,0},{3,5},{4,2},{5,7},{6,4},{7,1},{8,14},{9,11},{10,... | collective-permute-start | bytes 3538952 | tf_op jit(solution)/shard_map/ppermute | solution.py:27
  4.5 1.3 %copy-done = bf16[512,1152]{1,0:T(8,128)(2,1)S(1)} copy-done((bf16[512,1152]{1,0:T(8,128)(2,1)S(1)}, bf16[512,1152]{1,0:T(8,128)(2,1)}, u32[]{:S(2)}) %copy-start) | copy-done | bytes 1179672
  6.2 0.6 shard_map.68
  6.8 0.8 collective-permute-start.1
  7.6 1.3 %shard_map.69 = bf16[32,4,1152]{2,1,0:T(4,128)(2,1)} custom-call(s32[4]{0:T(128)S(1)} %pad_add_fusion.place, bf16[32,4,1152]{2,1,0:T(4,128)(2,1)S(1)} %get-tuple-element.20.keep, bf16[32,4,1152]{2,1,0:T(4,128)(2,1)S(1)} %collective-permute-done.1.moved), custom_call_target="tpu_custom_call" | custom-call | bytes 884752 | tf_op jit(solution)/shard_map/pallas_call | solution.py:37
  8.9 11.8 %all-to-all-start = ((bf16[32,4,1152]{2,1,0:T(4,128)(2,1)}), bf16[32,4,1152]{2,1,0:T(4,128)(2,1)S(1)}, u32[]{:S(2)}, u32[]{:S(2)}) async-start(bf16[32,4,1152]{2,1,0:T(4,128)(2,1)} %shard_map.69), calls=%async_computation | async-start | bytes 589824 | tf_op jit(solution)/shard_map/all_to_all | solution.py:237
  20.8 2.8 %collective-permute-start.5 = (bf16[512,1152]{1,0:T(8,128)(2,1)}, bf16[512,1152]{1,0:T(8,128)(2,1)}, u32[]{:S(2)}, u32[]{:S(2)}) collective-permute-start(bf16[512,1152]{1,0:T(8,128)(2,1)} %collective-permute-done.2.refs_1_), channel_id=1, source_target_pairs={{0,6},{1,3},{2,0},{3,5},{4,2},{5,7},{6,4},{7,1},{8,14},{9,11},{10,... | collective-permute-start | bytes 3538952 | tf_op jit(solution)/shard_map/ppermute | solution.py:27
  23.6 8.4 %all-to-all-done = bf16[32,4,1152]{2,1,0:T(4,128)(2,1)S(1)} async-done(((bf16[32,4,1152]{2,1,0:T(4,128)(2,1)}), bf16[32,4,1152]{2,1,0:T(4,128)(2,1)S(1)}, u32[]{:S(2)}, u32[]{:S(2)}) %all-to-all-start) | async-done | bytes 294944 | tf_op jit(solution)/shard_map/all_to_all | solution.py:237
  32.1 18.1 %all_to_all.15.chunks = bf16[32,4,1152]{2,1,0:T(4,128)(2,1)S(1)} all-to-all(bf16[32,4,1152]{2,1,0:T(4,128)(2,1)S(1)} %broadcast_in_dim.8), channel_id=1, replica_groups=mesh['x'=4,'z'=8,'y'=4,'c'=2] {'x','z'}, dimensions={0} | all-to-all | bytes 589824 | tf_op jit(solution)/shard_map/all_to_all | solution.py:240
  50.1 0.7 shard_map.70.own.refs_0_
  52.2 1.2 %collective-permute-start.7 = (bf16[128,1152]{1,0:T(8,128)(2,1)S(1)}, bf16[128,1152]{1,0:T(8,128)(2,1)S(1)}, u32[]{:S(2)}, u32[]{:S(2)}) collective-permute-start(bf16[128,1152]{1,0:T(8,128)(2,1)S(1)} %shard_map.70.own.refs_0_), channel_id=1, source_target_pairs={{0,6},{1,3},{2,0},{3,5},{4,2},{5,7},{6,4},{7,1},{8,14},{9,11},{10,... | collective-permute-start | bytes 884744 | tf_op jit(solution)/shard_map/ppermute | solution.py:27
  53.5 0.9 %collective-permute-start.8 = (bf16[128,1152]{1,0:T(8,128)(2,1)S(1)}, bf16[128,1152]{1,0:T(8,128)(2,1)S(1)}, u32[]{:S(2)}, u32[]{:S(2)}) collective-permute-start(bf16[128,1152]{1,0:T(8,128)(2,1)S(1)} %shard_map.70.own.refs_0_), channel_id=1, source_target_pairs={{0,2},{1,7},{2,4},{3,1},{4,6},{5,3},{6,0},{7,5},{8,10},{9,15},{10,... | collective-permute-start | bytes 884744 | tf_op jit(solution)/shard_map/ppermute | solution.py:27
  54.4 5.2 %shard_map.71 = (f32[128,1152]{1,0:T(8,128)S(1)}, bf16[128,1152]{1,0:T(8,128)(2,1)S(1)}) custom-call(s32[4]{0:T(128)S(1)} %pad_add_fusion.place, f32[2]{0:T(128)S(1)} %pad_maximum_fusion.factors, bf16[128,1152]{1,0:T(8,128)(2,1)S(1)} %shard_map.70.own.refs_0_, bf16[128,1152]{1,0:T(8,128)(2,1)S(1)} %collective-permute-done.3.other.refs_4_, ...), custom_call_target="tpu_custom_call" | custom-call | flops 2415919104 | bytes 6193176 | tf_op jit(solution)/shard_map/pallas_call | solution.py:37
  59.7 1.2 %collective-permute-start.6 = (bf16[128,1152]{1,0:T(8,128)(2,1)S(1)}, bf16[128,1152]{1,0:T(8,128)(2,1)S(1)}, u32[]{:S(2)}, u32[]{:S(2)}) collective-permute-start(bf16[128,1152]{1,0:T(8,128)(2,1)S(1)} %get-tuple-element.26), channel_id=1, source_target_pairs={{0,1},{1,0},{2,3},{3,2},{4,5},{5,4},{6,7},{7,6},{8,9},{9,8},{10,11... | collective-permute-start | bytes 884744 | tf_op jit(solution)/shard_map/ppermute | solution.py:31
  60.9 1.1 %collective-permute-done.7.refs_1_ = bf16[128,1152]{1,0:T(8,128)(2,1)S(1)} collective-permute-done((bf16[128,1152]{1,0:T(8,128)(2,1)S(1)}, bf16[128,1152]{1,0:T(8,128)(2,1)S(1)}, u32[]{:S(2)}, u32[]{:S(2)}) %collective-permute-start.7) | collective-permute-done | bytes 294944 | tf_op jit(solution)/shard_map/ppermute | solution.py:27
  62.0 1.0 %collective-permute-start.9 = (bf16[128,1152]{1,0:T(8,128)(2,1)S(1)}, bf16[128,1152]{1,0:T(8,128)(2,1)S(1)}, u32[]{:S(2)}, u32[]{:S(2)}) collective-permute-start(bf16[128,1152]{1,0:T(8,128)(2,1)S(1)} %collective-permute-done.7.refs_1_), channel_id=1, source_target_pairs={{0,6},{1,3},{2,0},{3,5},{4,2},{5,7},{6,4},{7,1},{8,14},{9,11},{10,... | collective-permute-start | bytes 884744 | tf_op jit(solution)/shard_map/ppermute | solution.py:27
  63.0 0.8 shard_map.73
  63.8 5.4 %all-to-all-start.2 = ((bf16[32,4,1152]{2,1,0:T(4,128)(2,1)}), bf16[32,4,1152]{2,1,0:T(4,128)(2,1)S(1)}, u32[]{:S(2)}, u32[]{:S(2)}) async-start(bf16[32,4,1152]{2,1,0:T(4,128)(2,1)} %shard_map.73), calls=%async_computation.2 | async-start | bytes 589824 | tf_op jit(solution)/shard_map/all_to_all | solution.py:262
  69.3 0.5 collective-permute-start.11
  70.1 0.8 collective-permute-done.10.refs_5_
  71.7 5.7 %shard_map.72 = (f32[512,1152]{1,0:T(8,128)}, f32[512]{0:T(512)}) custom-call(s32[4]{0:T(128)S(1)} %pad_add_fusion.place, f32[2]{0:T(128)S(1)} %pad_maximum_fusion.factors, bf16[512,1152]{1,0:T(8,128)(2,1)S(1)} %copy-done.1, bf16[128,1152]{1,0:T(8,128)(2,1)S(1)} %shard_map.70.own.refs_0_, bf16[128,1152]{1,0:T(8,128)(2,1)S(1)} %collective-permute-done.7.refs_1_, ...), custom_call_target="tpu_custom_call" | custom-call | flops 2415919104 | bytes 5900312 | tf_op jit(solution)/shard_map/pallas_call | solution.py:37
  77.5 4.0 %all-to-all-done.2.terms = bf16[32,4,1152]{2,1,0:T(4,128)(2,1)S(1)} async-done(((bf16[32,4,1152]{2,1,0:T(4,128)(2,1)}), bf16[32,4,1152]{2,1,0:T(4,128)(2,1)S(1)}, u32[]{:S(2)}, u32[]{:S(2)}) %all-to-all-start.2) | async-done | bytes 294944 | tf_op jit(solution)/shard_map/all_to_all | solution.py:262
  81.5 1.2 %shard_map.74 = f32[2,2,1152]{2,1,0:T(2,128)} custom-call(f32[2]{0:T(128)S(1)} %pad_maximum_fusion.factors, bf16[32,4,1152]{2,1,0:T(4,128)(2,1)S(1)} %all-to-all-done.2.terms), custom_call_target="tpu_custom_call" | custom-call | bytes 313352 | tf_op jit(solution)/shard_map/pallas_call | solution.py:37
  (23 shorter events, 1.9 us)
Async XLA Ops:
  0.6 5.6 %collective-permute-start = (bf16[512,1152]{1,0:T(8,128)(2,1)}, bf16[512,1152]{1,0:T(8,128)(2,1)S(1)}, u32[]{:S(2)}, u32[]{:S(2)}) collective-permute-start(bf16[512,1152]{1,0:T(8,128)(2,1)} %text.1), channel_id=1, source_target_pairs={{0,1},{128,129}} | collective-permute-start | bytes 3538952 | tf_op jit(solution)/shard_map/ppermute | solution.py:222
  1.4 19.4 %collective-permute-start.2 = (bf16[512,1152]{1,0:T(8,128)(2,1)}, bf16[512,1152]{1,0:T(8,128)(2,1)}, u32[]{:S(2)}, u32[]{:S(2)}) collective-permute-start(bf16[512,1152]{1,0:T(8,128)(2,1)} %image.1), channel_id=1, source_target_pairs={{0,6},{1,3},{2,0},{3,5},{4,2},{5,7},{6,4},{7,1},{8,14},{9,11},{10,... | collective-permute-start | bytes 3538952 | tf_op jit(solution)/shard_map/ppermute | solution.py:27
  4.5 1.3 %copy-start = (bf16[512,1152]{1,0:T(8,128)(2,1)S(1)}, bf16[512,1152]{1,0:T(8,128)(2,1)}, u32[]{:S(2)}) copy-start(bf16[512,1152]{1,0:T(8,128)(2,1)} %text.1) | copy-start | bytes 3538948
  6.8 16.8 %copy-start.1 = (bf16[512,1152]{1,0:T(8,128)(2,1)S(1)}, bf16[512,1152]{1,0:T(8,128)(2,1)}, u32[]{:S(2)}) copy-start(bf16[512,1152]{1,0:T(8,128)(2,1)} %image.1) | copy-start | bytes 3538948
  6.8 0.8 collective-permute-start.1
  8.9 23.0 %all-to-all-start = ((bf16[32,4,1152]{2,1,0:T(4,128)(2,1)}), bf16[32,4,1152]{2,1,0:T(4,128)(2,1)S(1)}, u32[]{:S(2)}, u32[]{:S(2)}) async-start(bf16[32,4,1152]{2,1,0:T(4,128)(2,1)} %shard_map.69), calls=%async_computation | async-start | bytes 589824 | tf_op jit(solution)/shard_map/all_to_all | solution.py:237
  20.8 33.6 %collective-permute-start.5 = (bf16[512,1152]{1,0:T(8,128)(2,1)}, bf16[512,1152]{1,0:T(8,128)(2,1)}, u32[]{:S(2)}, u32[]{:S(2)}) collective-permute-start(bf16[512,1152]{1,0:T(8,128)(2,1)} %collective-permute-done.2.refs_1_), channel_id=1, source_target_pairs={{0,6},{1,3},{2,0},{3,5},{4,2},{5,7},{6,4},{7,1},{8,14},{9,11},{10,... | collective-permute-start | bytes 3538952 | tf_op jit(solution)/shard_map/ppermute | solution.py:27
  23.6 30.9 %collective-permute-start.4 = (bf16[512,1152]{1,0:T(8,128)(2,1)S(1)}, bf16[512,1152]{1,0:T(8,128)(2,1)}, u32[]{:S(2)}, u32[]{:S(2)}) collective-permute-start(bf16[512,1152]{1,0:T(8,128)(2,1)S(1)} %copy-done.1), channel_id=1, source_target_pairs={{0,2},{1,7},{2,4},{3,1},{4,6},{5,3},{6,0},{7,5},{8,10},{9,15},{10,... | collective-permute-start | bytes 3538952 | tf_op jit(solution)/shard_map/ppermute | solution.py:27
  50.8 3.6 %collective-permute-start.3 = (bf16[128,1152]{1,0:T(8,128)(2,1)S(1)}, bf16[128,1152]{1,0:T(8,128)(2,1)S(1)}, u32[]{:S(2)}, u32[]{:S(2)}) collective-permute-start(bf16[128,1152]{1,0:T(8,128)(2,1)S(1)} %shard_map.70.own.refs_0_), channel_id=1, source_target_pairs={{0,1},{1,0},{2,3},{3,2},{4,5},{5,4},{6,7},{7,6},{8,9},{9,8},{10,11... | collective-permute-start | bytes 884744 | tf_op jit(solution)/shard_map/ppermute | solution.py:31
  52.2 9.8 %collective-permute-start.7 = (bf16[128,1152]{1,0:T(8,128)(2,1)S(1)}, bf16[128,1152]{1,0:T(8,128)(2,1)S(1)}, u32[]{:S(2)}, u32[]{:S(2)}) collective-permute-start(bf16[128,1152]{1,0:T(8,128)(2,1)S(1)} %shard_map.70.own.refs_0_), channel_id=1, source_target_pairs={{0,6},{1,3},{2,0},{3,5},{4,2},{5,7},{6,4},{7,1},{8,14},{9,11},{10,... | collective-permute-start | bytes 884744 | tf_op jit(solution)/shard_map/ppermute | solution.py:27
  53.5 9.5 %collective-permute-start.8 = (bf16[128,1152]{1,0:T(8,128)(2,1)S(1)}, bf16[128,1152]{1,0:T(8,128)(2,1)S(1)}, u32[]{:S(2)}, u32[]{:S(2)}) collective-permute-start(bf16[128,1152]{1,0:T(8,128)(2,1)S(1)} %shard_map.70.own.refs_0_), channel_id=1, source_target_pairs={{0,2},{1,7},{2,4},{3,1},{4,6},{5,3},{6,0},{7,5},{8,10},{9,15},{10,... | collective-permute-start | bytes 884744 | tf_op jit(solution)/shard_map/ppermute | solution.py:27
  59.7 3.3 %collective-permute-start.6 = (bf16[128,1152]{1,0:T(8,128)(2,1)S(1)}, bf16[128,1152]{1,0:T(8,128)(2,1)S(1)}, u32[]{:S(2)}, u32[]{:S(2)}) collective-permute-start(bf16[128,1152]{1,0:T(8,128)(2,1)S(1)} %get-tuple-element.26), channel_id=1, source_target_pairs={{0,1},{1,0},{2,3},{3,2},{4,5},{5,4},{6,7},{7,6},{8,9},{9,8},{10,11... | collective-permute-start | bytes 884744 | tf_op jit(solution)/shard_map/ppermute | solution.py:31
  62.0 7.8 %collective-permute-start.9 = (bf16[128,1152]{1,0:T(8,128)(2,1)S(1)}, bf16[128,1152]{1,0:T(8,128)(2,1)S(1)}, u32[]{:S(2)}, u32[]{:S(2)}) collective-permute-start(bf16[128,1152]{1,0:T(8,128)(2,1)S(1)} %collective-permute-done.7.refs_1_), channel_id=1, source_target_pairs={{0,6},{1,3},{2,0},{3,5},{4,2},{5,7},{6,4},{7,1},{8,14},{9,11},{10,... | collective-permute-start | bytes 884744 | tf_op jit(solution)/shard_map/ppermute | solution.py:27
  63.8 17.7 %all-to-all-start.2 = ((bf16[32,4,1152]{2,1,0:T(4,128)(2,1)}), bf16[32,4,1152]{2,1,0:T(4,128)(2,1)S(1)}, u32[]{:S(2)}, u32[]{:S(2)}) async-start(bf16[32,4,1152]{2,1,0:T(4,128)(2,1)} %shard_map.73), calls=%async_computation.2 | async-start | bytes 589824 | tf_op jit(solution)/shard_map/all_to_all | solution.py:262
  69.2 1.7 %collective-permute-start.10 = (bf16[128,1152]{1,0:T(8,128)(2,1)S(1)}, bf16[128,1152]{1,0:T(8,128)(2,1)S(1)}, u32[]{:S(2)}, u32[]{:S(2)}) collective-permute-start(bf16[128,1152]{1,0:T(8,128)(2,1)S(1)} %collective-permute-done.7.refs_1_), channel_id=1, source_target_pairs={{0,1},{1,0},{2,3},{3,2},{4,5},{5,4},{6,7},{7,6},{8,9},{9,8},{10,11... | collective-permute-start | bytes 884744 | tf_op jit(solution)/shard_map/ppermute | solution.py:31
  69.3 2.0 %collective-permute-start.11 = (bf16[128,1152]{1,0:T(8,128)(2,1)S(1)}, bf16[128,1152]{1,0:T(8,128)(2,1)S(1)}, u32[]{:S(2)}, u32[]{:S(2)}) collective-permute-start(bf16[128,1152]{1,0:T(8,128)(2,1)S(1)} %collective-permute-done.8.refs_2_), channel_id=1, source_target_pairs={{0,1},{1,0},{2,3},{3,2},{4,5},{5,4},{6,7},{7,6},{8,9},{9,8},{10,11... | collective-permute-start | bytes 884744 | tf_op jit(solution)/shard_map/ppermute | solution.py:31
  69.8 1.9 %collective-permute-start.12 = (bf16[128,1152]{1,0:T(8,128)(2,1)S(1)}, bf16[128,1152]{1,0:T(8,128)(2,1)S(1)}, u32[]{:S(2)}, u32[]{:S(2)}) collective-permute-start(bf16[128,1152]{1,0:T(8,128)(2,1)S(1)} %collective-permute-done.9.refs_3_), channel_id=1, source_target_pairs={{0,1},{1,0},{2,3},{3,2},{4,5},{5,4},{6,7},{7,6},{8,9},{9,8},{10,11... | collective-permute-start | bytes 884744 | tf_op jit(solution)/shard_map/ppermute | solution.py:31

commit v7 on v6

--- a/solution.py
+++ b/solution.py
@@ -254,8 +254,8 @@
         flops=4 * flops,
         scalars=2,
     )
-    line = [texts, around(texts, 1), around(texts, -1)]
-    line.append(around(line[1], 1))
+    line = [texts, around(texts, -1), around(texts, 1)]
+    line.append(around(line[1], -1))
     passed = other_core(theirs)
     passed, line[1], line[2] = lax.optimization_barrier((passed, line[1], line[2]))
     term = call(add_kernel, [shaped(PLANE, STEPS * per, width)], (mine, passed), scalars=0)
@@ -263,7 +263,7 @@
     text_grad = call(sum_kernel, [shaped(STEPS, per, width, dtype=f32)], (factors, terms))
 
     across = [other] + [other_core(a) for a in line[1:]]
-    offsets = [(0, 0), (-1, 0), (1, 0), (2, 0), (0, 1), (1, 1), (-1, 1), (2, 1)]
+    offsets = [(0, 0), (1, 0), (-1, 0), (2, 0), (0, 1), (-1, 1), (1, 1), (2, 1)]
     image_grad, row_loss = call(
         functools.partial(image_kernel, offsets),
         [shaped(rows, width, dtype=f32), shaped(rows, dtype=f32)],

time: 83.1 us -> 84.2 us (1.013)
  waiting for transfers between devices: 15.2 us -> 18 us
  starting transfers between devices: 29.9 us -> 28.3 us
    ppermute x6, waiting for transfers between devices: 1.15 us -> 3.69 us  [around(): return lax.ppermute(a, ('y', 'c'), pairs)]
    ppermute x5, starting transfers between devices: 2.2 us -> 0.94 us  [other_core(): return lax.ppermute(a, 'c', [(0, 1), (1, 0)])]
  transfers between devices with their start and end apart: 15 -> 15, of which waited for: 6 -> 5; matrix products, arithmetic and copies ran while one was open for 0% -> 0% of each run, Pallas kernels for 18% -> 18%
where the time goes in v7:
time: 84.2 us; the launch traced here: 83.8 us
  starting transfers between devices  28.3 us (34%)
  blocking collectives  18.1 us (21%)
  waiting for transfers between devices  18 us (21%)
  Pallas kernels  15.9 us (19%)
  between operations  2.1 us (2%)
  local copies, waits for them, and re-layouts  1.36 us (2%)
    all_to_all x1, blocking collectives, local(): chunks = lax.all_to_all(everywhere, ('x', 'z'), 0, 0, tiled=True)  18.1 us
    pallas_call x8, Pallas kernels, call(): pl.pallas_call(body, out_shape=outs[0] if single else outs, in_specs=opti...  15.9 us
    all_to_all x1, starting transfers between devices, local(): spread = lax.all_to_all(joined, ('z', 'y'), 0, 0, tiled=True)  11.8 us
    ppermute x6, starting transfers between devices, around(): return lax.ppermute(a, ('y', 'c'), pairs)  9.19 us
    all_to_all x1, waiting for transfers between devices, local(): spread = lax.all_to_all(joined, ('z', 'y'), 0, 0, tiled=True)  8.39 us
    all_to_all x1, starting transfers between devices, local(): terms = lax.all_to_all(term, ('x', 'z'), 0, 0, tiled=True)  4.77 us
    all_to_all x1, waiting for transfers between devices, local(): terms = lax.all_to_all(term, ('x', 'z'), 0, 0, tiled=True)  4.3 us
    ppermute x6, waiting for transfers between devices, around(): return lax.ppermute(a, ('y', 'c'), pairs)  3.69 us
  transfers between devices with their start and end apart: 15, of which 5 were waited for; matrix products, arithmetic and copies ran while one was open for 0% of the time, Pallas kernels for 18%

profile of v7, /device:TPU:32, one launch (start us, length us, event | category | flops | bytes accessed | tf_op | source)
XLA Modules:
  0.0 83.8 jit_solution(502265044477978055)
XLA Ops:
  0.6 0.7 collective-permute-start
  1.4 3.1 %collective-permute-start.2 = (bf16[512,1152]{1,0:T(8,128)(2,1)}, bf16[512,1152]{1,0:T(8,128)(2,1)}, u32[]{:S(2)}, u32[]{:S(2)}) collective-permute-start(bf16[512,1152]{1,0:T(8,128)(2,1)} %image.1), channel_id=1, source_target_pairs={{0,6},{1,3},{2,0},{3,5},{4,2},{5,7},{6,4},{7,1},{8,14},{9,11},{10,... | collective-permute-start | bytes 3538952 | tf_op jit(solution)/shard_map/ppermute | solution.py:27
  4.5 1.3 %copy-done = bf16[512,1152]{1,0:T(8,128)(2,1)S(1)} copy-done((bf16[512,1152]{1,0:T(8,128)(2,1)S(1)}, bf16[512,1152]{1,0:T(8,128)(2,1)}, u32[]{:S(2)}) %copy-start) | copy-done | bytes 1179672
  5.7 0.4 shard_map.67
  6.2 0.6 shard_map.68
  6.8 0.8 collective-permute-start.1
  7.6 1.3 %shard_map.69 = bf16[32,4,1152]{2,1,0:T(4,128)(2,1)} custom-call(s32[4]{0:T(128)S(1)} %pad_add_fusion.place, bf16[32,4,1152]{2,1,0:T(4,128)(2,1)S(1)} %get-tuple-element.20.keep, bf16[32,4,1152]{2,1,0:T(4,128)(2,1)S(1)} %collective-permute-done.1.moved), custom_call_target="tpu_custom_call" | custom-call | bytes 884752 | tf_op jit(solution)/shard_map/pallas_call | solution.py:37
  8.9 11.8 %all-to-all-start = ((bf16[32,4,1152]{2,1,0:T(4,128)(2,1)}), bf16[32,4,1152]{2,1,0:T(4,128)(2,1)S(1)}, u32[]{:S(2)}, u32[]{:S(2)}) async-start(bf16[32,4,1152]{2,1,0:T(4,128)(2,1)} %shard_map.69), calls=%async_computation | async-start | bytes 589824 | tf_op jit(solution)/shard_map/all_to_all | solution.py:237
  20.8 2.8 %collective-permute-start.5 = (bf16[512,1152]{1,0:T(8,128)(2,1)}, bf16[512,1152]{1,0:T(8,128)(2,1)}, u32[]{:S(2)}, u32[]{:S(2)}) collective-permute-start(bf16[512,1152]{1,0:T(8,128)(2,1)} %collective-permute-done.2.refs_1_), channel_id=1, source_target_pairs={{0,6},{1,3},{2,0},{3,5},{4,2},{5,7},{6,4},{7,1},{8,14},{9,11},{10,... | collective-permute-start | bytes 3538952 | tf_op jit(solution)/shard_map/ppermute | solution.py:27
  23.6 8.4 %all-to-all-done = bf16[32,4,1152]{2,1,0:T(4,128)(2,1)S(1)} async-done(((bf16[32,4,1152]{2,1,0:T(4,128)(2,1)}), bf16[32,4,1152]{2,1,0:T(4,128)(2,1)S(1)}, u32[]{:S(2)}, u32[]{:S(2)}) %all-to-all-start) | async-done | bytes 294944 | tf_op jit(solution)/shard_map/all_to_all | solution.py:237
  32.1 18.1 %all_to_all.15.chunks = bf16[32,4,1152]{2,1,0:T(4,128)(2,1)S(1)} all-to-all(bf16[32,4,1152]{2,1,0:T(4,128)(2,1)S(1)} %broadcast_in_dim.8), channel_id=1, replica_groups=mesh['x'=4,'z'=8,'y'=4,'c'=2] {'x','z'}, dimensions={0} | all-to-all | bytes 589824 | tf_op jit(solution)/shard_map/all_to_all | solution.py:240
  50.1 0.7 shard_map.70.own.refs_0_
  52.2 0.6 collective-permute-start.7
  52.9 2.7 %collective-permute-start.8 = (bf16[128,1152]{1,0:T(8,128)(2,1)S(1)}, bf16[128,1152]{1,0:T(8,128)(2,1)S(1)}, u32[]{:S(2)}, u32[]{:S(2)}) collective-permute-start(bf16[128,1152]{1,0:T(8,128)(2,1)S(1)} %shard_map.70.own.refs_0_), channel_id=1, source_target_pairs={{0,6},{1,3},{2,0},{3,5},{4,2},{5,7},{6,4},{7,1},{8,14},{9,11},{10,... | collective-permute-start | bytes 884744 | tf_op jit(solution)/shard_map/ppermute | solution.py:27
  55.7 5.2 %shard_map.71 = (f32[128,1152]{1,0:T(8,128)S(1)}, bf16[128,1152]{1,0:T(8,128)(2,1)S(1)}) custom-call(s32[4]{0:T(128)S(1)} %pad_add_fusion.place, f32[2]{0:T(128)S(1)} %pad_maximum_fusion.factors, bf16[128,1152]{1,0:T(8,128)(2,1)S(1)} %shard_map.70.own.refs_0_, bf16[128,1152]{1,0:T(8,128)(2,1)S(1)} %collective-permute-done.3.other.refs_4_, ...), custom_call_target="tpu_custom_call" | custom-call | flops 2415919104 | bytes 6193176 | tf_op jit(solution)/shard_map/pallas_call | solution.py:37
  61.0 2.1 %collective-permute-done.7.refs_1_ = bf16[128,1152]{1,0:T(8,128)(2,1)S(1)} collective-permute-done((bf16[128,1152]{1,0:T(8,128)(2,1)S(1)}, bf16[128,1152]{1,0:T(8,128)(2,1)S(1)}, u32[]{:S(2)}, u32[]{:S(2)}) %collective-permute-start.7) | collective-permute-done | bytes 294944 | tf_op jit(solution)/shard_map/ppermute | solution.py:27
  63.1 0.8 shard_map.73
  63.9 4.8 %all-to-all-start.2 = ((bf16[32,4,1152]{2,1,0:T(4,128)(2,1)}), bf16[32,4,1152]{2,1,0:T(4,128)(2,1)S(1)}, u32[]{:S(2)}, u32[]{:S(2)}) async-start(bf16[32,4,1152]{2,1,0:T(4,128)(2,1)} %shard_map.73), calls=%async_computation.2 | async-start | bytes 589824 | tf_op jit(solution)/shard_map/all_to_all | solution.py:262
  68.7 0.5 collective-permute-start.10
  69.4 1.6 %collective-permute-done.9.refs_3_ = bf16[128,1152]{1,0:T(8,128)(2,1)S(1)} collective-permute-done((bf16[128,1152]{1,0:T(8,128)(2,1)S(1)}, bf16[128,1152]{1,0:T(8,128)(2,1)S(1)}, u32[]{:S(2)}, u32[]{:S(2)}) %collective-permute-start.9) | collective-permute-done | bytes 294944 | tf_op jit(solution)/shard_map/ppermute | solution.py:27
  71.0 1.6 %collective-permute-done.12.refs_7_ = bf16[128,1152]{1,0:T(8,128)(2,1)S(1)} collective-permute-done((bf16[128,1152]{1,0:T(8,128)(2,1)S(1)}, bf16[128,1152]{1,0:T(8,128)(2,1)S(1)}, u32[]{:S(2)}, u32[]{:S(2)}) %collective-permute-start.12) | collective-permute-done | bytes 294944 | tf_op jit(solution)/shard_map/ppermute | solution.py:31
  72.6 5.8 %shard_map.72 = (f32[512,1152]{1,0:T(8,128)}, f32[512]{0:T(512)}) custom-call(s32[4]{0:T(128)S(1)} %pad_add_fusion.place, f32[2]{0:T(128)S(1)} %pad_maximum_fusion.factors, bf16[512,1152]{1,0:T(8,128)(2,1)S(1)} %copy-done.1, bf16[128,1152]{1,0:T(8,128)(2,1)S(1)} %shard_map.70.own.refs_0_, bf16[128,1152]{1,0:T(8,128)(2,1)S(1)} %collective-permute-done.7.refs_1_, ...), custom_call_target="tpu_custom_call" | custom-call | flops 2415919104 | bytes 5900312 | tf_op jit(solution)/shard_map/pallas_call | solution.py:37
  78.3 4.3 %all-to-all-done.2.terms = bf16[32,4,1152]{2,1,0:T(4,128)(2,1)S(1)} async-done(((bf16[32,4,1152]{2,1,0:T(4,128)(2,1)}), bf16[32,4,1152]{2,1,0:T(4,128)(2,1)S(1)}, u32[]{:S(2)}, u32[]{:S(2)}) %all-to-all-start.2) | async-done | bytes 294944 | tf_op jit(solution)/shard_map/all_to_all | solution.py:262
  82.6 1.2 %shard_map.74 = f32[2,2,1152]{2,1,0:T(2,128)} custom-call(f32[2]{0:T(128)S(1)} %pad_maximum_fusion.factors, bf16[32,4,1152]{2,1,0:T(4,128)(2,1)S(1)} %all-to-all-done.2.terms), custom_call_target="tpu_custom_call" | custom-call | bytes 313352 | tf_op jit(solution)/shard_map/pallas_call | solution.py:37
  (23 shorter events, 0.7 us)
Async XLA Ops:
  0.6 5.6 %collective-permute-start = (bf16[512,1152]{1,0:T(8,128)(2,1)}, bf16[512,1152]{1,0:T(8,128)(2,1)S(1)}, u32[]{:S(2)}, u32[]{:S(2)}) collective-permute-start(bf16[512,1152]{1,0:T(8,128)(2,1)} %text.1), channel_id=1, source_target_pairs={{0,1},{128,129}} | collective-permute-start | bytes 3538952 | tf_op jit(solution)/shard_map/ppermute | solution.py:222
  1.4 19.4 %collective-permute-start.2 = (bf16[512,1152]{1,0:T(8,128)(2,1)}, bf16[512,1152]{1,0:T(8,128)(2,1)}, u32[]{:S(2)}, u32[]{:S(2)}) collective-permute-start(bf16[512,1152]{1,0:T(8,128)(2,1)} %image.1), channel_id=1, source_target_pairs={{0,6},{1,3},{2,0},{3,5},{4,2},{5,7},{6,4},{7,1},{8,14},{9,11},{10,... | collective-permute-start | bytes 3538952 | tf_op jit(solution)/shard_map/ppermute | solution.py:27
  4.5 1.3 %copy-start = (bf16[512,1152]{1,0:T(8,128)(2,1)S(1)}, bf16[512,1152]{1,0:T(8,128)(2,1)}, u32[]{:S(2)}) copy-start(bf16[512,1152]{1,0:T(8,128)(2,1)} %text.1) | copy-start | bytes 3538948
  6.8 16.8 %copy-start.1 = (bf16[512,1152]{1,0:T(8,128)(2,1)S(1)}, bf16[512,1152]{1,0:T(8,128)(2,1)}, u32[]{:S(2)}) copy-start(bf16[512,1152]{1,0:T(8,128)(2,1)} %image.1) | copy-start | bytes 3538948
  6.8 0.8 collective-permute-start.1
  8.9 23.0 %all-to-all-start = ((bf16[32,4,1152]{2,1,0:T(4,128)(2,1)}), bf16[32,4,1152]{2,1,0:T(4,128)(2,1)S(1)}, u32[]{:S(2)}, u32[]{:S(2)}) async-start(bf16[32,4,1152]{2,1,0:T(4,128)(2,1)} %shard_map.69), calls=%async_computation | async-start | bytes 589824 | tf_op jit(solution)/shard_map/all_to_all | solution.py:237
  20.8 34.9 %collective-permute-start.5 = (bf16[512,1152]{1,0:T(8,128)(2,1)}, bf16[512,1152]{1,0:T(8,128)(2,1)}, u32[]{:S(2)}, u32[]{:S(2)}) collective-permute-start(bf16[512,1152]{1,0:T(8,128)(2,1)} %collective-permute-done.2.refs_1_), channel_id=1, source_target_pairs={{0,6},{1,3},{2,0},{3,5},{4,2},{5,7},{6,4},{7,1},{8,14},{9,11},{10,... | collective-permute-start | bytes 3538952 | tf_op jit(solution)/shard_map/ppermute | solution.py:27
  23.6 32.1 %collective-permute-start.4 = (bf16[512,1152]{1,0:T(8,128)(2,1)S(1)}, bf16[512,1152]{1,0:T(8,128)(2,1)}, u32[]{:S(2)}, u32[]{:S(2)}) collective-permute-start(bf16[512,1152]{1,0:T(8,128)(2,1)S(1)} %copy-done.1), channel_id=1, source_target_pairs={{0,2},{1,7},{2,4},{3,1},{4,6},{5,3},{6,0},{7,5},{8,10},{9,15},{10,... | collective-permute-start | bytes 3538952 | tf_op jit(solution)/shard_map/ppermute | solution.py:27
  50.8 4.8 %collective-permute-start.3 = (bf16[128,1152]{1,0:T(8,128)(2,1)S(1)}, bf16[128,1152]{1,0:T(8,128)(2,1)S(1)}, u32[]{:S(2)}, u32[]{:S(2)}) collective-permute-start(bf16[128,1152]{1,0:T(8,128)(2,1)S(1)} %shard_map.70.own.refs_0_), channel_id=1, source_target_pairs={{0,1},{1,0},{2,3},{3,2},{4,5},{5,4},{6,7},{7,6},{8,9},{9,8},{10,11... | collective-permute-start | bytes 884744 | tf_op jit(solution)/shard_map/ppermute | solution.py:31
  52.2 10.8 %collective-permute-start.7 = (bf16[128,1152]{1,0:T(8,128)(2,1)S(1)}, bf16[128,1152]{1,0:T(8,128)(2,1)S(1)}, u32[]{:S(2)}, u32[]{:S(2)}) collective-permute-start(bf16[128,1152]{1,0:T(8,128)(2,1)S(1)} %shard_map.70.own.refs_0_), channel_id=1, source_target_pairs={{0,2},{1,7},{2,4},{3,1},{4,6},{5,3},{6,0},{7,5},{8,10},{9,15},{10,... | collective-permute-start | bytes 884744 | tf_op jit(solution)/shard_map/ppermute | solution.py:27
  52.9 10.2 %collective-permute-start.8 = (bf16[128,1152]{1,0:T(8,128)(2,1)S(1)}, bf16[128,1152]{1,0:T(8,128)(2,1)S(1)}, u32[]{:S(2)}, u32[]{:S(2)}) collective-permute-start(bf16[128,1152]{1,0:T(8,128)(2,1)S(1)} %shard_map.70.own.refs_0_), channel_id=1, source_target_pairs={{0,6},{1,3},{2,0},{3,5},{4,2},{5,7},{6,4},{7,1},{8,14},{9,11},{10,... | collective-permute-start | bytes 884744 | tf_op jit(solution)/shard_map/ppermute | solution.py:27
  60.9 2.2 %collective-permute-start.6 = (bf16[128,1152]{1,0:T(8,128)(2,1)S(1)}, bf16[128,1152]{1,0:T(8,128)(2,1)S(1)}, u32[]{:S(2)}, u32[]{:S(2)}) collective-permute-start(bf16[128,1152]{1,0:T(8,128)(2,1)S(1)} %get-tuple-element.26), channel_id=1, source_target_pairs={{0,1},{1,0},{2,3},{3,2},{4,5},{5,4},{6,7},{7,6},{8,9},{9,8},{10,11... | collective-permute-start | bytes 884744 | tf_op jit(solution)/shard_map/ppermute | solution.py:31
  63.1 7.9 %collective-permute-start.9 = (bf16[128,1152]{1,0:T(8,128)(2,1)S(1)}, bf16[128,1152]{1,0:T(8,128)(2,1)S(1)}, u32[]{:S(2)}, u32[]{:S(2)}) collective-permute-start(bf16[128,1152]{1,0:T(8,128)(2,1)S(1)} %collective-permute-done.7.refs_1_), channel_id=1, source_target_pairs={{0,2},{1,7},{2,4},{3,1},{4,6},{5,3},{6,0},{7,5},{8,10},{9,15},{10,... | collective-permute-start | bytes 884744 | tf_op jit(solution)/shard_map/ppermute | solution.py:27
  63.9 18.8 %all-to-all-start.2 = ((bf16[32,4,1152]{2,1,0:T(4,128)(2,1)}), bf16[32,4,1152]{2,1,0:T(4,128)(2,1)S(1)}, u32[]{:S(2)}, u32[]{:S(2)}) async-start(bf16[32,4,1152]{2,1,0:T(4,128)(2,1)} %shard_map.73), calls=%async_computation.2 | async-start | bytes 589824 | tf_op jit(solution)/shard_map/all_to_all | solution.py:262
  68.7 2.3 %collective-permute-start.10 = (bf16[128,1152]{1,0:T(8,128)(2,1)S(1)}, bf16[128,1152]{1,0:T(8,128)(2,1)S(1)}, u32[]{:S(2)}, u32[]{:S(2)}) collective-permute-start(bf16[128,1152]{1,0:T(8,128)(2,1)S(1)} %collective-permute-done.7.refs_1_), channel_id=1, source_target_pairs={{0,1},{1,0},{2,3},{3,2},{4,5},{5,4},{6,7},{7,6},{8,9},{9,8},{10,11... | collective-permute-start | bytes 884744 | tf_op jit(solution)/shard_map/ppermute | solution.py:31
  69.1 1.9 %collective-permute-start.11 = (bf16[128,1152]{1,0:T(8,128)(2,1)S(1)}, bf16[128,1152]{1,0:T(8,128)(2,1)S(1)}, u32[]{:S(2)}, u32[]{:S(2)}) collective-permute-start(bf16[128,1152]{1,0:T(8,128)(2,1)S(1)} %collective-permute-done.8.refs_2_), channel_id=1, source_target_pairs={{0,1},{1,0},{2,3},{3,2},{4,5},{5,4},{6,7},{7,6},{8,9},{9,8},{10,11... | collective-permute-start | bytes 884744 | tf_op jit(solution)/shard_map/ppermute | solution.py:31
  71.0 1.6 %collective-permute-start.12 = (bf16[128,1152]{1,0:T(8,128)(2,1)S(1)}, bf16[128,1152]{1,0:T(8,128)(2,1)S(1)}, u32[]{:S(2)}, u32[]{:S(2)}) collective-permute-start(bf16[128,1152]{1,0:T(8,128)(2,1)S(1)} %collective-permute-done.9.refs_3_), channel_id=1, source_target_pairs={{0,1},{1,0},{2,3},{3,2},{4,5},{5,4},{6,7},{7,6},{8,9},{9,8},{10,11... | collective-permute-start | bytes 884744 | tf_op jit(solution)/shard_map/ppermute | solution.py:31
